TPU v7x, 32 devices: a whole 2x2x4 slice. The times are simulated.
32 devices in a mesh: fsdp: 2 (over y), ctx: 4 (over x, core), tp: 4 (over z).
Axes of the slice: x: 2, y: 2, z: 4, core: 2. Of those that a mesh axis runs over, the one named last changes fastest.
Arguments:
- residual: bfloat16 [6144, 2560], P(('fsdp', 'ctx')), may hold values from -6 to 6
- cotangent: bfloat16 [6144, 2560], P(('fsdp', 'ctx')), may hold values from -6 to 6
- seq_lengths: int32 [6], replicated, may hold values from 129 to 2048, as said below
- dealing: int32 [6], replicated, may hold values from 0 to 5, as said below
- pregain: float32 [2560], replicated, may hold values from 0.5 to 1.5
- gatelinear: float32 [2560, 2560], P(('fsdp', 'ctx'), 'tp'), may hold values from -0.125 to 0.125
- recurlinear: float32 [2560, 2560], P(('fsdp', 'ctx'), 'tp'), may hold values from -0.125 to 0.125
- convkernel: float32 [4, 2560], P(None, 'tp'), may hold values from -2.5 to 2.5
- convbias: float32 [2560], P('tp'), may hold values from -2.5 to 2.5
- inputgate: float32 [256, 2560], P(('fsdp', 'ctx'), 'tp'), may hold values from -0.375 to 0.375
- inputbias: float32 [2560], P('tp'), may hold values from -3 to 3
- decaygate: float32 [256, 2560], P(('fsdp', 'ctx'), 'tp'), may hold values from -0.375 to 0.375
- decaybias: float32 [2560], P('tp'), may hold values from -3 to 3
- decayparam: float32 [2560], P('tp'), may hold values from -13 to -4
- outlinear: float32 [2560, 2560], P('tp', ('fsdp', 'ctx')), may hold values from -0.3125 to 0.3125
- postgain: float32 [2560], replicated, may hold values from 0.5 to 1.5
- mlpgate: float32 [2560, 7680], P(('fsdp', 'ctx'), 'tp'), may hold values from -0.125 to 0.125
- mlpvalue: float32 [2560, 7680], P(('fsdp', 'ctx'), 'tp'), may hold values from -0.125 to 0.125
- mlpdown: float32 [7680, 2560], P('tp', ('fsdp', 'ctx')), may hold values from -0.09375 to 0.09375
Outputs:
- output: bfloat16 [6144, 2560], P(('fsdp', 'ctx'))
- residual_grad: bfloat16 [6144, 2560], P(('fsdp', 'ctx'))
- pregain_grad: float32 [2560], replicated
- gatelinear_grad: float32 [2560, 2560], P(('fsdp', 'ctx'), 'tp')
- recurlinear_grad: float32 [2560, 2560], P(('fsdp', 'ctx'), 'tp')
- convkernel_grad: float32 [4, 2560], P(None, 'tp')
- convbias_grad: float32 [2560], P('tp')
- inputgate_grad: float32 [256, 2560], P(('fsdp', 'ctx'), 'tp')
- inputbias_grad: float32 [2560], P('tp')
- decaygate_grad: float32 [256, 2560], P(('fsdp', 'ctx'), 'tp')
- decaybias_grad: float32 [2560], P('tp')
- decayparam_grad: float32 [2560], P('tp')
- outlinear_grad: float32 [2560, 2560], P('tp', ('fsdp', 'ctx'))
- postgain_grad: float32 [2560], replicated
- mlpgate_grad: float32 [2560, 7680], P(('fsdp', 'ctx'), 'tp')
- mlpvalue_grad: float32 [2560, 7680], P(('fsdp', 'ctx'), 'tp')
- mlpdown_grad: float32 [7680, 2560], P('tp', ('fsdp', 'ctx'))
Inputs may be any that keep to these rules, and one draw needn't show every extreme that they name: `seq_lengths`: the three sequences dealt to one group have lengths summing to at most 3072. `dealing`: a permutation of the sequence numbers.
All inputs are finite; a program needn't handle non-finite values.
Results may differ from a plain program's by a relative error of at most 0.014.
Values may be sent and summed in bfloat16 or wider, within the bound.
No kernel may reach another device: no remote copies, remote signals or barrier semaphores. Data moves between devices by JAX's collectives and lax.ppermute only.
A program may use at most 256 MiB of HBM per device.

v0:
```python
from functools import partial

import jax
import jax.numpy as jnp
from jax import lax
from jax.sharding import PartitionSpec as P

BLOCK = 256


def passed_along(value, axis, steps):
    count = lax.axis_size(axis)
    initial, last = (max(0, -steps), min(count, count - steps))
    return lax.ppermute(value, axis, [(source, source + steps) for source in range(initial, last)])


def partner(shard, axis, stride):
    return lax.ppermute(shard, axis, [(i, i ^ 1 << stride) for i in range(lax.axis_size(axis))])


def prefix(value, axis, join, neutral, backward):
    count, mine = (lax.axis_size(axis), lax.axis_index(axis))
    pieces = jax.tree.map(lambda part: lax.all_gather(part, axis), value)
    if backward:
        pieces = jax.tree.map(lambda part: part[::-1], pieces)
        mine = count - 1 - mine
    total = jax.tree.map(
        lambda part, zero: jnp.full_like(part, 0) + jnp.asarray(zero, part.dtype), value, neutral
    )

    def turn(position, total):
        longer = join(total, jax.tree.map(lambda part: part[position], pieces))
        return jax.tree.map(lambda new, old: jnp.where(position < mine, new, old), longer, total)

    return lax.fori_loop(0, count - 1, turn, total)


def forward_dot(operand, weights):
    return jnp.dot(operand, weights, preferred_element_type=jnp.float32)


def input_dot(cotan, weights):
    return lax.dot_general(
        cotan, weights, (((1,), (1,)), ((), ())), preferred_element_type=jnp.float32
    )


def weight_dot(operand, cotan):
    return lax.dot_general(
        operand, cotan, (((0,), (0,)), ((), ())), preferred_element_type=jnp.float32
    )


def rms_norm(values, scales):
    return values * lax.rsqrt(jnp.mean(values * values, axis=-1, keepdims=True) + 1e-06) * scales


def gelu_tanh(values):
    return jax.nn.gelu(values, approximate=True)


def combine(earlier, latter):
    return (earlier[0] * latter[0], earlier[1] * latter[0] + latter[1])


def layout(positions, lengths):
    bounds = jnp.cumsum(lengths)
    segment = jnp.sum((positions[:, None] >= bounds[None, :]).astype(jnp.int32), axis=1)
    resets = (positions == 0) | jnp.any(positions[:, None] == bounds[None, :], axis=1)
    return (segment, resets)


def temporal_conv(extended, kernel, offset_bias, segment):
    length = extended.shape[0] - 3
    summed = jnp.zeros((length, extended.shape[1]), jnp.float32) + offset_bias
    for offset in range(4):
        matches = (segment[3:] == segment[3 - offset : 3 - offset + length]).astype(jnp.float32)
        summed = (
            summed + kernel[offset] * extended[3 - offset : 3 - offset + length] * matches[:, None]
        )
    return summed


def gate_inputs(conv_out, pre_input, pre_decay, decayparam, resets):
    gate_in = jax.nn.sigmoid(pre_input)
    gate_decay = jax.nn.sigmoid(pre_decay)
    log_decay = -8.0 * gate_decay * jax.nn.softplus(decayparam)
    scaling = jnp.where(resets[:, None], 1.0, jnp.sqrt(-jnp.expm1(2.0 * log_decay)))
    decays = jnp.where(resets[:, None], 0.0, jnp.exp(log_decay))
    return (conv_out * gate_in * scaling, decays)


def widen(values, is_odd, margin):
    filler = jnp.zeros((values.shape[0], margin), values.dtype)
    return jnp.where(
        is_odd, jnp.concatenate([filler, values], axis=1), jnp.concatenate([values, filler], axis=1)
    )


def narrow(values, is_odd, margin):
    keep_width = values.shape[1] - margin
    return jnp.where(is_odd, values[:, margin:], values[:, :keep_width])


def block_apply(context_blocks, padded):
    result = jnp.einsum("tbi,ibo->tbo", context_blocks, padded, preferred_element_type=jnp.float32)
    return result.reshape(context_blocks.shape[0], -1)


def block_grad(context_blocks, cotan_blocks):
    result = jnp.einsum(
        "tbi,tbo->ibo", context_blocks, cotan_blocks, preferred_element_type=jnp.float32
    )
    return result.reshape(context_blocks.shape[2], -1)


def block_back(cotan_blocks, padded):
    result = jnp.einsum("tbo,ibo->tbi", cotan_blocks, padded, preferred_element_type=jnp.float32)
    return result.reshape(cotan_blocks.shape[0], -1)


def per_device(
    residual,
    cotangent,
    seq_lengths,
    dealing,
    pregain,
    gatelinear,
    recurlinear,
    convkernel,
    convbias,
    inputgate,
    inputbias,
    decaygate,
    decaybias,
    decayparam,
    outlinear,
    postgain,
    mlpgate,
    mlpvalue,
    mlpdown,
):
    tok_rows = residual.shape[0]
    channels = convbias.shape[0]
    margin = BLOCK // 2
    tp_count = lax.axis_size("tp")
    is_odd = lax.axis_index("tp") % 2 == 1
    chosen = lax.dynamic_slice_in_dim(dealing, lax.axis_index("fsdp") * 3, 3)
    catalog = jnp.arange(seq_lengths.shape[0], dtype=jnp.int32)
    lengths = jnp.sum(
        jnp.where(chosen[:, None] == catalog[None, :], seq_lengths[None, :], 0), axis=1
    )
    positions = lax.axis_index("ctx") * tok_rows - 3 + jnp.arange(tok_rows + 3, dtype=jnp.int32)
    segment, resets_all = layout(positions, lengths)
    resets = resets_all[3:]
    keep_rows = (segment[3:] < 3).astype(jnp.float32)[:, None]
    (
        gate_full,
        recur_full,
        ingate_full,
        decay_full,
        hgate_full,
        value_full,
        output_full,
        down_full,
    ) = (
        lax.all_gather(gatelinear.astype(jnp.bfloat16), ("fsdp", "ctx"), axis=0, tiled=True),
        lax.all_gather(recurlinear.astype(jnp.bfloat16), ("fsdp", "ctx"), axis=0, tiled=True),
        lax.all_gather(inputgate.astype(jnp.bfloat16), ("fsdp", "ctx"), axis=0, tiled=True),
        lax.all_gather(decaygate.astype(jnp.bfloat16), ("fsdp", "ctx"), axis=0, tiled=True),
        lax.all_gather(mlpgate.astype(jnp.bfloat16), ("fsdp", "ctx"), axis=0, tiled=True),
        lax.all_gather(mlpvalue.astype(jnp.bfloat16), ("fsdp", "ctx"), axis=0, tiled=True),
        lax.all_gather(outlinear.astype(jnp.bfloat16), ("fsdp", "ctx"), axis=1, tiled=True),
        lax.all_gather(mlpdown.astype(jnp.bfloat16), ("fsdp", "ctx"), axis=1, tiled=True),
    )
    residual_wide = residual.astype(jnp.float32)
    normed, norm_back = jax.vjp(rms_norm, residual_wide, pregain)
    normed_low = normed.astype(jnp.bfloat16)
    gate_pre = forward_dot(normed_low, gate_full)
    branch = forward_dot(normed_low, recur_full)
    leading = passed_along(branch[tok_rows - 3 :], "ctx", 1)
    extended = jnp.concatenate([leading, branch], axis=0)
    conv_out, conv_back = jax.vjp(
        partial(temporal_conv, segment=segment), extended, convkernel, convbias
    )
    conv_low = conv_out.astype(jnp.bfloat16)
    outgoing = jnp.where(is_odd, conv_low[:, :margin], conv_low[:, channels - margin :])
    incoming = partner(outgoing, "tp", 0)
    context = jnp.where(
        is_odd,
        jnp.concatenate([incoming, conv_low], axis=1),
        jnp.concatenate([conv_low, incoming], axis=1),
    )
    context_blocks = context.reshape(tok_rows, 3, BLOCK)
    ingate_pad = widen(ingate_full, is_odd, margin).reshape(BLOCK, 3, BLOCK)
    decay_pad = widen(decay_full, is_odd, margin).reshape(BLOCK, 3, BLOCK)
    pre_input = narrow(block_apply(context_blocks, ingate_pad), is_odd, margin) + inputbias
    pre_decay = narrow(block_apply(context_blocks, decay_pad), is_odd, margin) + decaybias
    (driven, decays), lru_back = jax.vjp(
        partial(gate_inputs, resets=resets), conv_out, pre_input, pre_decay, decayparam
    )
    prod_local, state_local = lax.associative_scan(combine, (decays, driven))
    identity = (jnp.ones((channels,), jnp.float32), jnp.zeros((channels,), jnp.float32))
    arriving = prefix((prod_local[-1], state_local[-1]), "ctx", combine, identity, False)
    states = state_local + prod_local * arriving[1][None, :]
    gelu_gate, gelu_gate_back = jax.vjp(gelu_tanh, gate_pre)
    mixed = (states * gelu_gate).astype(jnp.bfloat16)
    branch_part = forward_dot(mixed, output_full)
    middle = residual_wide + lax.psum(branch_part, "tp")
    normed_two, norm_two_back = jax.vjp(rms_norm, middle, postgain)
    normed_two_low = normed_two.astype(jnp.bfloat16)
    hidden_gate = forward_dot(normed_two_low, hgate_full)
    hidden_value = forward_dot(normed_two_low, value_full)
    gelu_hidden, gelu_hidden_back = jax.vjp(gelu_tanh, hidden_gate)
    hidden = (gelu_hidden * hidden_value).astype(jnp.bfloat16)
    mlp_part = forward_dot(hidden, down_full)
    summed_mlp = lax.psum(mlp_part.astype(jnp.bfloat16), "tp").astype(jnp.float32)
    block_out = (keep_rows * (middle + summed_mlp)).astype(jnp.bfloat16)
    (
        gate_full,
        recur_full,
        ingate_full,
        decay_full,
        hgate_full,
        value_full,
        output_full,
        down_full,
    ) = (
        lax.all_gather(gatelinear.astype(jnp.bfloat16), ("fsdp", "ctx"), axis=0, tiled=True),
        lax.all_gather(recurlinear.astype(jnp.bfloat16), ("fsdp", "ctx"), axis=0, tiled=True),
        lax.all_gather(inputgate.astype(jnp.bfloat16), ("fsdp", "ctx"), axis=0, tiled=True),
        lax.all_gather(decaygate.astype(jnp.bfloat16), ("fsdp", "ctx"), axis=0, tiled=True),
        lax.all_gather(mlpgate.astype(jnp.bfloat16), ("fsdp", "ctx"), axis=0, tiled=True),
        lax.all_gather(mlpvalue.astype(jnp.bfloat16), ("fsdp", "ctx"), axis=0, tiled=True),
        lax.all_gather(outlinear.astype(jnp.bfloat16), ("fsdp", "ctx"), axis=1, tiled=True),
        lax.all_gather(mlpdown.astype(jnp.bfloat16), ("fsdp", "ctx"), axis=1, tiled=True),
    )
    ingate_pad = widen(ingate_full, is_odd, margin).reshape(BLOCK, 3, BLOCK)
    decay_pad = widen(decay_full, is_odd, margin).reshape(BLOCK, 3, BLOCK)
    upstream = cotangent.astype(jnp.float32) * keep_rows
    upstream_low = upstream.astype(jnp.bfloat16)
    hidden_cot = input_dot(upstream_low, down_full)
    down_grad = weight_dot(hidden, upstream_low)
    value_cot = (hidden_cot * gelu_hidden).astype(jnp.bfloat16)
    hgate_cot = gelu_hidden_back(hidden_cot * hidden_value)[0].astype(jnp.bfloat16)
    hgate_grad = weight_dot(normed_two_low, hgate_cot)
    value_grad = weight_dot(normed_two_low, value_cot)
    normed_two_part = input_dot(hgate_cot, hgate_full) + input_dot(value_cot, value_full)
    middle_norm_cot, postgain_whole = norm_two_back(lax.psum(normed_two_part, "tp"))
    postgain_grad = postgain_whole / tp_count
    middle_cot = upstream + middle_norm_cot
    middle_low = middle_cot.astype(jnp.bfloat16)
    mixed_cot = input_dot(middle_low, output_full)
    output_grad = weight_dot(mixed, middle_low)
    states_cot = mixed_cot * gelu_gate
    gate_pre_cot = gelu_gate_back(mixed_cot * states)[0].astype(jnp.bfloat16)
    next_decays = jnp.concatenate([decays[1:], jnp.ones((1, channels), jnp.float32)], axis=0)
    rev_prod, rev_state = lax.associative_scan(combine, (next_decays, states_cot), reverse=True)
    returning = prefix(
        (decays[0] * rev_prod[0], decays[0] * rev_state[0]), "ctx", combine, identity, True
    )
    adjoint = rev_state + rev_prod * returning[1][None, :]
    previous = jnp.concatenate([arriving[1][None, :], states[:-1]], axis=0)
    conv_direct, input_cot, decay_cot, decayparam_grad = lru_back((adjoint, adjoint * previous))
    inputbias_grad = jnp.sum(input_cot, axis=0)
    decaybias_grad = jnp.sum(decay_cot, axis=0)
    input_low = widen(input_cot.astype(jnp.bfloat16), is_odd, margin).reshape(tok_rows, 3, BLOCK)
    decay_low = widen(decay_cot.astype(jnp.bfloat16), is_odd, margin).reshape(tok_rows, 3, BLOCK)
    ingate_grad = narrow(block_grad(context_blocks, input_low), is_odd, margin)
    decay_grad = narrow(block_grad(context_blocks, decay_low), is_odd, margin)
    context_cot = block_back(input_low, ingate_pad) + block_back(decay_low, decay_pad)
    own_cot = narrow(context_cot, is_odd, margin)
    going = jnp.where(is_odd, context_cot[:, :margin], context_cot[:, channels:])
    coming = partner(going.astype(jnp.bfloat16), "tp", 0).astype(going.dtype)
    spacer = jnp.zeros((tok_rows, channels - margin), jnp.float32)
    conv_cot = (
        conv_direct
        + own_cot
        + jnp.where(
            is_odd,
            jnp.concatenate([coming, spacer], axis=1),
            jnp.concatenate([spacer, coming], axis=1),
        )
    )
    extended_cot, kernel_grad, convbias_grad = conv_back(conv_cot)
    trailing = passed_along(extended_cot[:3], "ctx", -1)
    branch_cot = extended_cot[3:] + jnp.concatenate(
        [jnp.zeros((tok_rows - 3, channels), jnp.float32), trailing], axis=0
    )
    branch_low = branch_cot.astype(jnp.bfloat16)
    recur_grad = weight_dot(normed_low, branch_low)
    gatelin_grad = weight_dot(normed_low, gate_pre_cot)
    normed_part = input_dot(gate_pre_cot, gate_full) + input_dot(branch_low, recur_full)
    residual_norm_cot, pregain_whole = norm_back(
        lax.psum(normed_part.astype(jnp.bfloat16), "tp").astype(jnp.float32)
    )
    pregain_grad = pregain_whole / tp_count
    residual_grad = (middle_cot + residual_norm_cot).astype(jnp.bfloat16)
    scattered = (
        lax.psum_scatter(
            gatelin_grad.astype(jnp.bfloat16), ("fsdp", "ctx"), scatter_dimension=0, tiled=True
        ).astype(jnp.float32),
        lax.psum_scatter(
            recur_grad.astype(jnp.bfloat16), ("fsdp", "ctx"), scatter_dimension=0, tiled=True
        ).astype(jnp.float32),
        lax.psum_scatter(
            ingate_grad.astype(jnp.bfloat16), ("fsdp", "ctx"), scatter_dimension=0, tiled=True
        ).astype(jnp.float32),
        lax.psum_scatter(
            decay_grad.astype(jnp.bfloat16), ("fsdp", "ctx"), scatter_dimension=0, tiled=True
        ).astype(jnp.float32),
        lax.psum_scatter(
            hgate_grad.astype(jnp.bfloat16), ("fsdp", "ctx"), scatter_dimension=0, tiled=True
        ).astype(jnp.float32),
        lax.psum_scatter(
            value_grad.astype(jnp.bfloat16), ("fsdp", "ctx"), scatter_dimension=0, tiled=True
        ).astype(jnp.float32),
        lax.psum_scatter(
            output_grad.astype(jnp.bfloat16), ("fsdp", "ctx"), scatter_dimension=1, tiled=True
        ).astype(jnp.float32),
        lax.psum_scatter(
            down_grad.astype(jnp.bfloat16), ("fsdp", "ctx"), scatter_dimension=1, tiled=True
        ).astype(jnp.float32),
    )
    smalls = lax.psum(
        (kernel_grad, convbias_grad, inputbias_grad, decaybias_grad, decayparam_grad),
        ("fsdp", "ctx"),
    )
    gains = lax.psum((pregain_grad, postgain_grad), ("fsdp", "ctx", "tp"))
    return (
        block_out,
        residual_grad,
        gains[0],
        scattered[0],
        scattered[1],
        smalls[0],
        smalls[1],
        scattered[2],
        smalls[2],
        scattered[3],
        smalls[3],
        smalls[4],
        scattered[6],
        gains[1],
        scattered[4],
        scattered[5],
        scattered[7],
    )


def solution(mesh):
    return jax.shard_map(
        per_device,
        mesh=mesh,
        in_specs=(
            P(("fsdp", "ctx"), None),
            P(("fsdp", "ctx"), None),
            P(),
            P(),
            P(),
            P(("fsdp", "ctx"), "tp"),
            P(("fsdp", "ctx"), "tp"),
            P(None, "tp"),
            P("tp"),
            P(("fsdp", "ctx"), "tp"),
            P("tp"),
            P(("fsdp", "ctx"), "tp"),
            P("tp"),
            P("tp"),
            P("tp", ("fsdp", "ctx")),
            P(),
            P(("fsdp", "ctx"), "tp"),
            P(("fsdp", "ctx"), "tp"),
            P("tp", ("fsdp", "ctx")),
        ),
        out_specs=(
            P(("fsdp", "ctx"), None),
            P(("fsdp", "ctx"), None),
            P(),
            P(("fsdp", "ctx"), "tp"),
            P(("fsdp", "ctx"), "tp"),
            P(None, "tp"),
            P("tp"),
            P(("fsdp", "ctx"), "tp"),
            P("tp"),
            P(("fsdp", "ctx"), "tp"),
            P("tp"),
            P("tp"),
            P("tp", ("fsdp", "ctx")),
            P(),
            P(("fsdp", "ctx"), "tp"),
            P(("fsdp", "ctx"), "tp"),
            P("tp", ("fsdp", "ctx")),
        ),
        check_vma=False,
    )
```

profile of v0, /device:TPU:0, one launch (start us, length us, event | category | flops | bytes accessed | tf_op | source)
XLA Modules:
  0.0 2149.8 jit_solution(4645160094513202012)
XLA Ops:
  15.5 11.7 all_gather.47
  27.4 9.5 all_gather.48
  38.2 8.8 all-gather.11.cloned.1.call-done
  47.0 6.4 fusion.88
  57.7 5.9 fusion.92
  232.0 5.5 slice.751
  280.2 10.4 multiply_convert_fusion.4
  290.6 7.7 fusion.109
  305.6 266.8 %all-reduce.100.cloned.1.call-done = f32[768,2560]{1,0:T(8,128)} async-done(((f32[768,2560]{1,0:T(8,128)}), f32[768,2560]{1,0:T(8,128)}) %all-reduce.100.cloned.1.call-update) | async-done | bytes 7864336 | tf_op jit(solution)/shard_map/psum | solution.py:209
  583.7 50.4 %all-gather.17.cloned.1.call-done = bf16[2560,1920]{1,0:T(8,128)(2,1)} async-done(((bf16[320,1920]{1,0:T(8,128)(2,1)}), bf16[2560,1920]{1,0:T(8,128)(2,1)}) %all-gather.17.cloned.1.call-update) | async-done | bytes 9830416 | tf_op jit(solution)/shard_map/all_gather | solution.py:171
  634.1 13.9 fusion.110
  648.0 48.3 %all-gather.19.cloned.1.call-done = bf16[2560,1920]{1,0:T(8,128)(2,1)} async-done(((bf16[320,1920]{1,0:T(8,128)(2,1)}), bf16[2560,1920]{1,0:T(8,128)(2,1)}) %all-gather.19.cloned.1.call-update) | async-done | bytes 9830416 | tf_op jit(solution)/shard_map/all_gather | solution.py:172
  696.3 13.9 fusion.111
  710.2 48.5 %all-gather.21.cloned.1.call-done = bf16[1920,2560]{0,1:T(8,128)(2,1)} async-done(((bf16[1920,320]{0,1:T(8,128)(2,1)}), bf16[1920,2560]{0,1:T(8,128)(2,1)}) %all-gather.21.cloned.1.call-update) | async-done | bytes 9830416 | tf_op jit(solution)/shard_map/all_gather | solution.py:174
  758.7 21.3 multiply_convert_fusion.2
  780.1 12.0 fusion.112
  792.1 15.2 convolution_add_fusion
  810.4 6.0 slice.775
  826.5 8.4 slice.776
  834.9 8.3 slice.782
  848.6 232.7 %all-reduce.102.cloned.1.call-done = f32[768,2560]{1,0:T(8,128)} async-done(((f32[768,2560]{1,0:T(8,128)}), f32[768,2560]{1,0:T(8,128)}) %all-reduce.102.cloned.1.call-update) | async-done | bytes 7864336 | tf_op jit(solution)/shard_map/psum | solution.py:249
  1081.3 7.4 multiply_reduce_fusion
  1090.2 5.7 fusion.4
  1095.9 7.4 fusion.43
  1112.8 8.3 slice.773
  1243.4 5.6 pad.328
  1258.6 5.7 pad.310
  1264.2 8.6 slice.846
  1301.6 9.9 rev.15
  1311.5 16.0 rev.14
  1327.5 8.3 multiply_reduce_fusion.3
  1354.3 8.6 convolution_convert_fusion.4
  1364.1 7.3 convolution_convert_fusion.6
  1386.4 6.4 multiply_reduce_fusion.7
  1402.4 13.2 convolution_convert_fusion.2
  1415.7 13.3 convolution_convert_fusion.1
  1429.7 13.6 convolution_convert_fusion
  1443.4 13.3 convolution_convert_fusion.3
  1465.8 25.5 %all-reduce.94 = (f32[4,640]{1,0:T(4,128)}, f32[640]{0:T(1024)}, f32[640]{0:T(1024)}, f32[640]{0:T(1024)}, f32[640]{0:T(1024)}) all-reduce(f32[4,640]{1,0:T(4,128)S(1)} %pad_add_fusion.6, f32[640]{0:T(1024)S(1)} %get-tuple-element.253, f32[640]{0:T(1024)S(1)} %copy-done.104, ...), channel_id=1, replica_groups=mesh['fsdp'=2,'ctx'=4,'tp'=4] {'fsdp','ctx'}, use_global_device_ids=true, to_apply=%region_24.25 | all-reduce | flops 5120 | bytes 40960 | tf_op jit(solution)/shard_map/psum | solution.py:325
  1496.0 19.6 reduce-scatter.9.cloned.1.call-done
  1517.5 48.4 %reduce-scatter.11.cloned.1.call-done = bf16[320,640]{1,0:T(8,128)(2,1)} async-done(((bf16[2560,640]{1,0:T(8,128)(2,1)}), bf16[320,640]{1,0:T(8,128)(2,1)}) %reduce-scatter.11.cloned.1.call-update) | async-done | bytes 409616 | tf_op jit(solution)/shard_map/reduce_scatter | solution.py:303
  1567.8 79.8 %reduce-scatter.19.cloned.1.call-done = bf16[320,1920]{1,0:T(8,128)(2,1)} async-done(((bf16[2560,1920]{1,0:T(8,128)(2,1)}), bf16[320,1920]{1,0:T(8,128)(2,1)}) %reduce-scatter.19.cloned.1.call-update) | async-done | bytes 1228816 | tf_op jit(solution)/shard_map/reduce_scatter | solution.py:312
  1650.5 78.9 %reduce-scatter.21.cloned.1.call-done = bf16[320,1920]{1,0:T(8,128)(2,1)} async-done(((bf16[2560,1920]{1,0:T(8,128)(2,1)}), bf16[320,1920]{1,0:T(8,128)(2,1)}) %reduce-scatter.21.cloned.1.call-update) | async-done | bytes 1228816 | tf_op jit(solution)/shard_map/reduce_scatter | solution.py:315
  1732.3 78.8 %reduce-scatter.23.cloned.1.call-done = bf16[1920,320]{0,1:T(8,128)(2,1)} async-done(((bf16[1920,2560]{0,1:T(8,128)(2,1)}), bf16[1920,320]{0,1:T(8,128)(2,1)}) %reduce-scatter.23.cloned.1.call-update) | async-done | bytes 1228816 | tf_op jit(solution)/shard_map/reduce_scatter | solution.py:321
  1814.0 274.1 %all-reduce.104.cloned.1.call-done = (bf16[768,2560]{1,0:T(8,128)(2,1)}, bf16[768,2560]{1,0:T(8,128)(2,1)}) async-done(((bf16[768,2560]{1,0:T(8,128)(2,1)}, bf16[768,2560]{1,0:T(8,128)(2,1)}), (bf16[768,2560]{1,0:T(8,128)(2,1)}, bf16[768,2560]{1,0:T(8,128)(2,1)})) %all-reduce.104.cloned.1.call-update) | async-done | bytes 7864336 | tf_op jit(solution)/shard_map/psum | solution.py:217
  2088.1 5.8 fusion.3
  2093.9 6.6 fusion.6
  2103.4 39.7 %all-reduce.93 = (f32[2560]{0:T(1024)}, f32[2560]{0:T(1024)}) all-reduce(f32[2560]{0:T(1024)S(1)} %broadcast_multiply_fusion.2, f32[2560]{0:T(1024)S(1)} %broadcast_multiply_fusion.1), channel_id=1, replica_groups=mesh['fsdp'=2,'ctx'=4,'tp'=4] {'fsdp','ctx','tp'}, use_global_device_ids=true, to_apply=%region_17.18 | all-reduce | flops 5120 | bytes 40960 | tf_op jit(solution)/shard_map/psum | solution.py:329
  (777 shorter events, 506.3 us)
Async XLA Ops:
  7.2 39.8 %all-gather.11.cloned.1.call-start = ((), (), s32[]{:S(2)}) async-start(), calls=%async_computation.8 | async-start | bytes 3686400 | tf_op jit(solution)/shard_map/all_gather | solution.py:168
  9.3 270.8 %all-gather.13.cloned.1.call-start = ((), (), s32[]{:S(2)}) async-start(), calls=%async_computation.9 | async-start | bytes 3686400 | tf_op jit(solution)/shard_map/all_gather | solution.py:167
  10.2 280.3 %all-gather.15.cloned.1.call-start = ((), (), s32[]{:S(2)}) async-start(), calls=%async_computation.10 | async-start | bytes 3686400 | tf_op jit(solution)/shard_map/all_gather | solution.py:173
  11.1 561.3 %all-reduce.100.cloned.1.call-start = ((), (), s32[]{:S(2)}) async-start(), calls=%async_computation.11 | async-start | bytes 15728640 | tf_op jit(solution)/shard_map/psum | solution.py:209
  12.5 45.2 %copy-start.66 = (f32[768]{0:T(1024)}, f32[768]{0:T(1024)S(1)}, u32[]{:S(2)}) copy-start(f32[768]{0:T(1024)S(1)} %get-tuple-element.415) | copy-start | bytes 9220
  12.5 45.2 %copy-start.68 = (f32[768]{0:T(1024)}, f32[768]{0:T(1024)S(1)}, u32[]{:S(2)}) copy-start(f32[768]{0:T(1024)S(1)} %get-tuple-element.416) | copy-start | bytes 9220
  12.5 45.2 %copy-start.70 = (f32[768]{0:T(1024)}, f32[768]{0:T(1024)S(1)}, u32[]{:S(2)}) copy-start(f32[768]{0:T(1024)S(1)} %get-tuple-element.417) | copy-start | bytes 9220
  12.5 14.9 copy-start.63
  15.5 37.9 %copy-start.94 = (f32[768]{0:T(1024)}, f32[768]{0:T(1024)S(1)}, u32[]{:S(2)}) copy-start(f32[768]{0:T(1024)S(1)} %fusion.7) | copy-start | bytes 9220
  15.5 31.5 %copy-start.74 = (f32[2560]{0:T(1024)S(1)}, f32[2560]{0:T(1024)}, u32[]{:S(2)}) copy-start(f32[2560]{0:T(1024)} %param.27) | copy-start | bytes 30724
  15.5 264.6 %copy-start.84 = (f32[768]{0:T(1024)}, f32[768]{0:T(1024)S(1)}, u32[]{:S(2)}) copy-start(f32[768]{0:T(1024)S(1)} %fusion.76) | copy-start | bytes 9220
  38.2 35.9 %copy-start.29 = (bf16[256,768]{0,1:T(8,128)(2,1)}, bf16[256,768]{0,1:T(8,128)(2,1)S(1)}, u32[]{:S(2)}) copy-start(bf16[256,768]{0,1:T(8,128)(2,1)S(1)} %get-tuple-element.419) | copy-start | bytes 1179652
  38.2 18.6 copy-start.123
  38.2 19.5 copy-start.136
  54.7 3.0 collective-permute-start
  63.6 27.4 %copy-start.8 = (f32[768,640]{1,0:T(8,128)}, f32[768,640]{1,0:T(8,128)S(1)}, u32[]{:S(2)}) copy-start(f32[768,640]{1,0:T(8,128)S(1)} %get-tuple-element.308) | copy-start | bytes 5898244
  63.6 7.5 collective-permute-start.1
  65.8 30.6 %copy-start.72 = (f32[640]{0:T(1024)}, f32[640]{0:T(1024)S(1)}, u32[]{:S(2)}) copy-start(f32[640]{0:T(1024)S(1)} %get-tuple-element.413) | copy-start | bytes 7684
  98.0 140.2 %copy-start.9 = (f32[768,640]{1,0:T(8,128)}, f32[768,640]{1,0:T(8,128)S(1)}, u32[]{:S(2)}) copy-start(f32[768,640]{1,0:T(8,128)S(1)} %exponential_select_fusion) | copy-start | bytes 5898244
  298.3 335.8 %all-gather.17.cloned.1.call-start = ((), (), s32[]{:S(2)}) async-start(), calls=%async_computation.12 | async-start | bytes 11059200 | tf_op jit(solution)/shard_map/all_gather | solution.py:171
  301.2 395.2 %all-gather.19.cloned.1.call-start = ((), (), s32[]{:S(2)}) async-start(), calls=%async_computation.13 | async-start | bytes 11059200 | tf_op jit(solution)/shard_map/all_gather | solution.py:172
  304.2 454.5 %all-gather.21.cloned.1.call-start = ((), (), s32[]{:S(2)}) async-start(), calls=%async_computation.14 | async-start | bytes 11059200 | tf_op jit(solution)/shard_map/all_gather | solution.py:174
  305.5 275.5 %copy-start.57 = (f32[2560]{0:T(1024)S(1)}, f32[2560]{0:T(1024)}, u32[]{:S(2)}) copy-start(f32[2560]{0:T(1024)} %param.38) | copy-start | bytes 30724
  305.5 775.8 %all-reduce.102.cloned.1.call-start = ((), (), s32[]{:S(2)}) async-start(), calls=%async_computation.15 | async-start | bytes 15728640 | tf_op jit(solution)/shard_map/psum | solution.py:249
  648.0 110.8 %copy-start.97 = (f32[768]{0:T(1024)S(1)}, f32[768]{0:T(1024)}, u32[]{:S(2)}) copy-start(f32[768]{0:T(1024)} %get-tuple-element.414) | copy-start | bytes 9220
  696.3 83.7 %slice-start.3 = ((s8[9830400]{0:T(1024)(128)(4,1)}), s8[1441792]{0:T(1024)(128)(4,1)S(1)}, s32[]{:S(2)}) async-start(s8[9830400]{0:T(1024)(128)(4,1)} %bitcast.108), calls=%async_computation.28 | async-start | bytes 2883584
  758.7 21.3 slice-start.4
  758.7 21.3 slice-start.5
  807.4 683.9 %reduce-scatter.15.cloned.1.call-start = ((), (), s32[]{:S(2)}) async-start(), calls=%async_computation.19 | async-start | bytes 368640 | tf_op jit(solution)/shard_map/reduce_scatter | solution.py:309
  1208.0 13.7 copy-start.99
  1208.0 13.8 copy-start.122
  1208.0 13.8 copy-start.121
  1311.5 16.0 copy-start.6
  1311.5 16.0 copy-start.73
  1311.5 16.0 copy-start.96
  1311.5 16.0 copy-start.101
  1311.5 16.0 copy-start.112
  1345.0 147.6 %reduce-scatter.13.cloned.1.call-start = ((), (), s32[]{:S(2)}) async-start(), calls=%async_computation.18 | async-start | bytes 368640 | tf_op jit(solution)/shard_map/reduce_scatter | solution.py:306
  1354.2 139.8 %reduce-scatter.17.cloned.1.call-start = ((), (), s32[]{:S(2)}) async-start(), calls=%async_computation.20 | async-start | bytes 3686400 | tf_op jit(solution)/shard_map/reduce_scatter | solution.py:318
  1362.9 152.7 %reduce-scatter.9.cloned.1.call-start = ((), (), s32[]{:S(2)}) async-start(), calls=%async_computation.16 | async-start | bytes 3686400 | tf_op jit(solution)/shard_map/reduce_scatter | solution.py:300
  1371.4 194.5 %reduce-scatter.11.cloned.1.call-start = ((), (), s32[]{:S(2)}) async-start(), calls=%async_computation.17 | async-start | bytes 3686400 | tf_op jit(solution)/shard_map/reduce_scatter | solution.py:303
  1375.8 10.4 collective-permute-start.2
  1393.5 3.3 collective-permute-start.3
  1401.9 245.7 %reduce-scatter.19.cloned.1.call-start = ((), (), s32[]{:S(2)}) async-start(), calls=%async_computation.21 | async-start | bytes 11059200 | tf_op jit(solution)/shard_map/reduce_scatter | solution.py:312
  1415.6 313.7 %reduce-scatter.21.cloned.1.call-start = ((), (), s32[]{:S(2)}) async-start(), calls=%async_computation.22 | async-start | bytes 11059200 | tf_op jit(solution)/shard_map/reduce_scatter | solution.py:315
  1429.0 382.1 %reduce-scatter.23.cloned.1.call-start = ((), (), s32[]{:S(2)}) async-start(), calls=%async_computation.23 | async-start | bytes 11059200 | tf_op jit(solution)/shard_map/reduce_scatter | solution.py:321
  1443.4 644.7 %all-reduce.104.cloned.1.call-start = ((), (), s32[]{:S(2)}) async-start(), calls=%async_computation.24 | async-start | bytes 15728640 | tf_op jit(solution)/shard_map/psum | solution.py:217
  1729.4 364.5 %copy-start.95 = (f32[768]{0:T(1024)S(1)}, f32[768]{0:T(1024)}, u32[]{:S(2)}) copy-start(f32[768]{0:T(1024)} %copy-done.94) | copy-start | bytes 9220
  (127 other events, 633.4 us)
Sparse Core Ops, SparseCore 0:
  10.5 36.4 all-gather.10
  48.8 32.8 all-gather.12
  83.6 32.8 all-gather.14
  298.4 273.8 all-reduce.99
  574.7 59.3 all-gather.16
  635.8 60.4 all-gather.18
  698.2 60.4 all-gather.20
  807.5 273.7 all-reduce.101
  1345.1 32.6 reduce-scatter.14
  1381.3 33.7 reduce-scatter.12
  1418.5 46.8 reduce-scatter.16
  1468.7 46.8 reduce-scatter.8
  1519.0 46.8 reduce-scatter.10
  1569.3 78.3 reduce-scatter.18
  1651.1 78.2 reduce-scatter.20
  1732.8 78.2 reduce-scatter.22
  1813.9 274.0 all-reduce.103
where the time goes:
time: 2170 us; the launch traced here: 2150 us
  waiting for transfers between devices  1240 us (57%)
  local copies, waits for them, and re-layouts  400 us (18%)
  matrix products  198 us (9%)
  other arithmetic  180 us (8%)
  blocking collectives  107 us (5%)
    psum x1, waiting for transfers between devices, per_device(): lax.psum(mlp_part.astype(jnp.bfloat16), 'tp').astype(jnp.float32)  274 us
    psum x1, waiting for transfers between devices, per_device(): middle = residual_wide + lax.psum(branch_part, 'tp')  267 us
    psum x1, waiting for transfers between devices, per_device(): lax.psum(normed_two_part, 'tp')  233 us
    slice x69, local copies, waits for them, and re-layouts, per_device(): lax.associative_scan(combine, (next_decays, states_cot), reverse=True)  150 us
    slice x65, local copies, waits for them, and re-layouts, per_device(): prod_local, state_local = lax.associative_scan(combine, (decays, driven))  101 us
    reduce_scatter x1, waiting for transfers between devices, per_device(): lax.psum_scatter(hgate_grad.astype(jnp.bfloat16), ('fsdp', 'ctx'), scatte...  79.8 us
    reduce_scatter x1, waiting for transfers between devices, per_device(): lax.psum_scatter(value_grad.astype(jnp.bfloat16), ('fsdp', 'ctx'), scatte...  78.9 us
    reduce_scatter x1, waiting for transfers between devices, per_device(): lax.psum_scatter(down_grad.astype(jnp.bfloat16), ('fsdp', 'ctx'), scatter...  78.8 us
  transfers between devices with their start and end apart: 21, of which 15 were waited for; matrix products, arithmetic and copies ran while one was open for 20% of the time, Pallas kernels for 0%

commit v1 on v0

v1 whole, which is shorter than its diff:
```python
from functools import partial

import jax
import jax.numpy as jnp
from jax import lax
from jax.experimental import pallas as pl
from jax.experimental.pallas import tpu as pltpu
from jax.sharding import PartitionSpec as P

BLOCK = 256
HALF = BLOCK // 2
ROWS = 128
MIB = 1024 * 1024
F32 = jnp.float32
BF16 = jnp.bfloat16


def flip(value, position):
    ctx_bits = lax.axis_size("ctx").bit_length() - 1
    axis, bit = ("ctx", position) if position < ctx_bits else ("fsdp", position - ctx_bits)
    return lax.ppermute(value, axis, [(i, i ^ (1 << bit)) for i in range(lax.axis_size(axis))])


def partner(value, bit=0):
    return lax.ppermute(value, "tp", [(i, i ^ (1 << bit)) for i in range(lax.axis_size("tp"))])


def cube_bits():
    return (lax.axis_size("fsdp") * lax.axis_size("ctx")).bit_length() - 1


def cube_index():
    return lax.axis_index("fsdp") * lax.axis_size("ctx") + lax.axis_index("ctx")


def slow_order(backward):
    order = list(range(1, cube_bits()))
    return order[::-1] if backward else order


def gather_pieces(shard, backward):
    pieces = {0: shard}
    for position in slow_order(backward) + [0]:
        pieces.update({mask | 1 << position: flip(piece, position) for mask, piece in pieces.items()})
    return [pieces[mask] for mask in sorted(pieces)]


def assemble(pieces):
    count, (rows, columns) = len(pieces), pieces[0].shape

    def kernel(me_ref, *refs):
        sources, target, sems = refs[:count], refs[count], refs[count + 1]
        copies = []
        for mask in range(count):
            start = pl.multiple_of((me_ref[0] ^ mask) * rows, 16)
            copies.append(
                pltpu.make_async_copy(sources[mask], target.at[pl.ds(start, rows)], sems.at[mask])
            )
        for copy in copies:
            copy.start()
        for copy in copies:
            copy.wait()

    return pl.pallas_call(
        kernel,
        in_specs=[pl.BlockSpec(memory_space=pltpu.SMEM)]
        + [pl.BlockSpec(memory_space=pl.ANY)] * count,
        out_specs=pl.BlockSpec(memory_space=pltpu.VMEM),
        out_shape=jax.ShapeDtypeStruct((count * rows, columns), pieces[0].dtype),
        scratch_shapes=[pltpu.SemaphoreType.DMA((count,))],
        compiler_params=pltpu.CompilerParams(vmem_limit_bytes=32 * MIB),
        cost_estimate=pl.CostEstimate(
            flops=0, bytes_accessed=4 * count * rows * columns, transcendentals=0
        ),
        name="assemble",
    )(cube_index().astype(jnp.int32).reshape(1), *pieces)


def scatter_sum(grad, backward):
    count = 1 << cube_bits()
    rows = grad.shape[0] // count
    me = cube_index()
    order = [0] + slow_order(backward)[::-1]
    held = {
        mask: lax.dynamic_slice_in_dim(grad, (me ^ mask) * rows, rows) for mask in range(count)
    }
    for position in order:
        bit = 1 << position
        keep = [mask for mask in held if not mask & bit]
        outgoing = jnp.concatenate([held[mask | bit].astype(BF16) for mask in keep], axis=0)
        incoming = flip(outgoing, position)
        held = {
            mask: held[mask].astype(F32) + incoming[i * rows : (i + 1) * rows].astype(F32)
            for i, mask in enumerate(keep)
        }
    return held[0]


def line_sum(partial_sums):
    count, mine = lax.axis_size("tp"), lax.axis_index("tp")
    rows = partial_sums.shape[0] // count

    def chunk(number):
        start = jnp.clip(number, 0, count - 1) * rows
        return lax.dynamic_slice_in_dim(partial_sums, start, rows).astype(F32)

    from_left = from_right = None
    for step in range(1, count):
        rightward = chunk(mine + count - step)
        leftward = chunk(mine - count + step)
        if step > 1:
            rightward = rightward + from_left.astype(F32)
            leftward = leftward + from_right.astype(F32)
        from_left = lax.ppermute(
            rightward.astype(BF16), "tp", [(s, s + 1) for s in range(min(step, count - 1))]
        )
        from_right = lax.ppermute(
            leftward.astype(BF16), "tp", [(s, s - 1) for s in range(max(count - step, 1), count)]
        )
    return chunk(mine) + from_left.astype(F32) + from_right.astype(F32)


def line_gather(share):
    count, mine = lax.axis_size("tp"), lax.axis_index("tp")
    left, right = {0: share}, {0: share}
    for step in range(1, count):
        left[step] = lax.ppermute(
            left[step - 1], "tp", [(s, s + 1) for s in range(step - 1, count - 1)]
        )
        right[step] = lax.ppermute(
            right[step - 1], "tp", [(s, s - 1) for s in range(1, count - step + 1)]
        )
    parts = []
    for number in range(count):
        choice = left[count - 1 - number] if number < count - 1 else share
        for place in range(count - 2, -1, -1):
            here = left[place - number] if place >= number else right[number - place]
            choice = jnp.where(mine == place, here, choice)
        parts.append(choice)
    return jnp.concatenate(parts, axis=0)


def shifted(value, steps):
    count = lax.axis_size("ctx")
    pairs = [(s, s + steps) for s in range(count) if 0 <= s + steps < count]
    return lax.ppermute(value, "ctx", pairs)


def carried(ends, backward):
    sign = -1 if backward else 1
    state = None
    for distance in range(lax.axis_size("ctx") - 1, 0, -1):
        pair = shifted(ends, sign * distance)
        state = pair[1] if state is None else pair[1] + pair[0] * state
    return jnp.broadcast_to(state[None], ends.shape)


def since_start(info_ref, row):
    place = info_ref[3] + row + lax.broadcasted_iota(jnp.int32, (8, 128), 0)
    begin = jnp.zeros((8, 128), jnp.int32)
    for j in range(3):
        begin = jnp.where(place >= info_ref[j], info_ref[j], begin)
    return place - begin


def wide(tile, columns):
    return jnp.concatenate([tile] * (columns // 128), axis=1)


def rows_of(columns):
    return lax.broadcasted_iota(jnp.int32, (8, columns), 0)


def moved(tile, other, steps, row):
    both = pltpu.roll(tile, steps % 8, 0), pltpu.roll(other, steps % 8, 0)
    inside = (row >= steps) if steps > 0 else (row < 8 + steps)
    return jnp.where(inside, *both)


def one_less_exp(value, half_exp):
    series = jnp.ones_like(value)
    for n in range(8, 1, -1):
        series = 1.0 + value * (1.0 / n) * series
    return jnp.where(value > -0.5, -value * series, 1.0 - half_exp * half_exp)


def sigmoid(value):
    return 1.0 / (1.0 + jnp.exp(-value))


def gelu_both(value):
    c = 0.7978845608028654
    square = value * value
    bent = jnp.tanh(c * value * (1.0 + 0.044715 * square))
    half = 0.5 * (1.0 + bent)
    slope = half + 0.5 * value * (1.0 - bent * bent) * c * (1.0 + 3 * 0.044715 * square)
    return value * half, slope


def dot(a, b):
    return jnp.dot(a, b, preferred_element_type=F32)


def dot_nt(a, b):
    return lax.dot_general(a, b, (((1,), (1,)), ((), ())), preferred_element_type=F32)


def dot_tn(a, b):
    return lax.dot_general(a, b, (((0,), (0,)), ((), ())), preferred_element_type=F32)


def const_spec(shape):
    return pl.BlockSpec(shape, lambda i: (0,) * len(shape), pipeline_mode=pl.Buffered(1))


def row_spec(columns):
    return pl.BlockSpec((ROWS, columns), lambda i: (i, 0))


SMEM_SPEC = pl.BlockSpec(memory_space=pltpu.SMEM)


def params(mib):
    return pltpu.CompilerParams(
        dimension_semantics=("arbitrary",), vmem_limit_bytes=mib * MIB
    )


def recur_forward(info, normed, lead, gate_w, recur_w, taps, gates_in, gates_decay, vectors):
    tokens, width = normed.shape
    channels = gate_w.shape[1]
    reach = taps.shape[1]
    tiles = ROWS // 8

    def kernel(
        info_ref, x_ref, lead_ref, gate_ref, recur_ref, taps_ref, gin_ref, gdec_ref, vec_ref,
        gate_pre_ref, branch_ref, lead_branch_ref, conv_ref, low_ref, pre_in_ref, pre_dec_ref,
        decay_ref, prod_ref, state_ref, ends_ref,
        ext, conv, carry_p, carry_s,
    ):
        i = pl.program_id(0)

        @pl.when(i == 0)
        def _():
            first = dot(lead_ref[...], recur_ref[:, :reach])[8:]
            ext[0:8, :] = first
            lead_branch_ref[...] = first[:, :channels]
            carry_p[...] = jnp.ones_like(carry_p)
            carry_s[...] = jnp.zeros_like(carry_s)

        @pl.when(i > 0)
        def _():
            ext[0:8, :] = ext[ROWS : ROWS + 8, :]

        x = x_ref[...]
        ext[8:, :] = dot(x, recur_ref[:, :reach])
        gate_pre_ref[...] = dot(x, gate_ref[...])
        branch_ref[...] = ext[8:, :channels]
        row_wide = rows_of(reach)
        row = rows_of(channels)

        def conv_tile(t, _):
            base = pl.multiple_of(t * 8, 8)
            since = since_start(info_ref, i * ROWS + base)
            current, before = ext[pl.ds(base + 8, 8), :], ext[pl.ds(base, 8), :]
            total = taps_ref[4:5, :] + taps_ref[0:1, :] * current
            for k in range(1, 4):
                earlier = moved(current, before, k, row_wide)
                total = total + taps_ref[k : k + 1, :] * jnp.where(
                    wide(since >= k, reach), earlier, 0.0
                )
            conv[pl.ds(base, 8), :] = total
            return 0

        lax.fori_loop(0, tiles, conv_tile, 0)
        conv_ref[...] = conv[:, :channels]
        low = conv[...].astype(BF16)
        low_ref[...] = low
        for begin in range(0, channels, BLOCK):
            end = min(begin + BLOCK, channels)
            block = low[:, begin : begin + BLOCK]
            pre_in_ref[:, begin:end] = dot(block, gin_ref[:, begin:end]) + vec_ref[0:1, begin:end]
            pre_dec_ref[:, begin:end] = dot(block, gdec_ref[:, begin:end]) + vec_ref[1:2, begin:end]

        def scan_tile(t, carry):
            base = pl.multiple_of(t * 8, 8)
            at = pl.ds(base, 8)
            start = wide(since_start(info_ref, i * ROWS + base) == 0, channels)
            log_decay = sigmoid(pre_dec_ref[at, :]) * vec_ref[2:3, :]
            decay = jnp.exp(log_decay)
            scale = jnp.sqrt(one_less_exp(2.0 * log_decay, decay))
            a = jnp.where(start, 0.0, decay)
            b = conv_ref[at, :] * sigmoid(pre_in_ref[at, :]) * jnp.where(start, 1.0, scale)
            decay_ref[at, :] = a
            for s in (1, 2, 4):
                inside = row >= s
                b = b + a * jnp.where(inside, pltpu.roll(b, s, 0), 0.0)
                a = a * jnp.where(inside, pltpu.roll(a, s, 0), 1.0)
            b = b + a * carry[1]
            a = a * carry[0]
            prod_ref[at, :] = a
            state_ref[at, :] = b
            return (
                jnp.broadcast_to(a[7:8, :], a.shape),
                jnp.broadcast_to(b[7:8, :], b.shape),
            )

        last = lax.fori_loop(0, tiles, scan_tile, (carry_p[...], carry_s[...]))
        carry_p[...] = last[0]
        carry_s[...] = last[1]
        ends_ref[...] = jnp.where(row == 0, last[0], last[1])

    narrow = jax.ShapeDtypeStruct((tokens, channels), F32)
    small = jax.ShapeDtypeStruct((8, channels), F32)
    return pl.pallas_call(
        kernel,
        grid=(tokens // ROWS,),
        in_specs=[
            SMEM_SPEC,
            row_spec(width),
            const_spec((16, width)),
            const_spec((width, channels)),
            const_spec((width, recur_w.shape[1])),
            const_spec((8, reach)),
            const_spec((BLOCK, channels)),
            const_spec((BLOCK, channels)),
            const_spec((8, channels)),
        ],
        out_specs=[
            row_spec(channels),
            row_spec(channels),
            pl.BlockSpec((8, channels), lambda i: (0, 0)),
            row_spec(channels),
            row_spec(reach),
            row_spec(channels),
            row_spec(channels),
            row_spec(channels),
            row_spec(channels),
            row_spec(channels),
            pl.BlockSpec((8, channels), lambda i: (0, 0)),
        ],
        out_shape=[
            narrow, narrow, small, narrow, jax.ShapeDtypeStruct((tokens, reach), BF16),
            narrow, narrow, narrow, narrow, narrow, small,
        ],
        scratch_shapes=[
            pltpu.VMEM((ROWS + 8, reach), F32),
            pltpu.VMEM((ROWS, reach), F32),
            pltpu.VMEM((8, channels), F32),
            pltpu.VMEM((8, channels), F32),
        ],
        compiler_params=params(40),
        cost_estimate=pl.CostEstimate(
            flops=2 * tokens * width * (channels + reach),
            bytes_accessed=30 * MIB,
            transcendentals=6 * tokens * channels,
        ),
        name="recur_forward",
    )(info, normed, lead, gate_w, recur_w, taps, gates_in, gates_decay, vectors)


def mix_forward(prod, state, gate_pre, arriving, out_t):
    tokens, channels = prod.shape
    width = out_t.shape[0]

    def kernel(prod_ref, state_ref, gate_ref, arr_ref, out_ref, states_ref, mixed_ref, part_ref):
        states = state_ref[...] + prod_ref[...] * arr_ref[0:1, :]
        states_ref[...] = states
        mixed = (states * gelu_both(gate_ref[...])[0]).astype(BF16)
        mixed_ref[...] = mixed
        part_ref[...] = dot_nt(mixed, out_ref[...]).astype(BF16)

    return pl.pallas_call(
        kernel,
        grid=(tokens // ROWS,),
        in_specs=[
            row_spec(channels),
            row_spec(channels),
            row_spec(channels),
            const_spec((8, channels)),
            const_spec((width, channels)),
        ],
        out_specs=[row_spec(channels), row_spec(channels), row_spec(width)],
        out_shape=[
            jax.ShapeDtypeStruct((tokens, channels), F32),
            jax.ShapeDtypeStruct((tokens, channels), BF16),
            jax.ShapeDtypeStruct((tokens, width), BF16),
        ],
        compiler_params=params(40),
        cost_estimate=pl.CostEstimate(
            flops=2 * tokens * width * channels,
            bytes_accessed=16 * MIB,
            transcendentals=tokens * channels,
        ),
        name="mix_forward",
    )(prod, state, gate_pre, arriving, out_t)


def mix_backward(middle_low, out_t, gate_pre, states, decays):
    tokens, channels = states.shape
    width = out_t.shape[0]
    tiles = ROWS // 8
    steps = tokens // ROWS

    def kernel(
        mid_ref, out_ref, gate_ref, states_ref, decay_ref,
        cot_ref, prod_ref, state_ref, ends_ref,
        mixed_cot, carry_p, carry_s, next_decay,
    ):
        i = pl.program_id(0)

        @pl.when(i == 0)
        def _():
            carry_p[...] = jnp.ones_like(carry_p)
            carry_s[...] = jnp.zeros_like(carry_s)
            next_decay[...] = jnp.ones_like(next_decay)

        mixed_cot[...] = dot(mid_ref[...], out_ref[...])
        row = rows_of(channels)

        def tile(t, carry):
            base = pl.multiple_of((tiles - 1 - t) * 8, 8)
            at = pl.ds(base, 8)
            value, slope = gelu_both(gate_ref[at, :])
            cot = mixed_cot[at, :]
            mixed_cot[at, :] = cot * states_ref[at, :] * slope
            decay = decay_ref[at, :]
            a = moved(decay, carry[2], -1, row)
            b = cot * value
            for s in (1, 2, 4):
                inside = row < 8 - s
                b = b + a * jnp.where(inside, pltpu.roll(b, 8 - s, 0), 0.0)
                a = a * jnp.where(inside, pltpu.roll(a, 8 - s, 0), 1.0)
            b = b + a * carry[1]
            a = a * carry[0]
            prod_ref[at, :] = a
            state_ref[at, :] = b
            return (
                jnp.broadcast_to(a[0:1, :], a.shape),
                jnp.broadcast_to(b[0:1, :], b.shape),
                decay,
            )

        last = lax.fori_loop(0, tiles, tile, (carry_p[...], carry_s[...], next_decay[...]))
        cot_ref[...] = mixed_cot[...].astype(BF16)
        carry_p[...], carry_s[...], next_decay[...] = last
        ends_ref[...] = jnp.where(row == 0, last[0], last[1]) * jnp.broadcast_to(
            last[2][0:1, :], (8, channels)
        )

    def back(columns):
        return pl.BlockSpec((ROWS, columns), lambda i: (steps - 1 - i, 0))

    return pl.pallas_call(
        kernel,
        grid=(steps,),
        in_specs=[
            back(width), const_spec((width, channels)), back(channels), back(channels),
            back(channels),
        ],
        out_specs=[
            back(channels), back(channels), back(channels),
            pl.BlockSpec((8, channels), lambda i: (0, 0)),
        ],
        out_shape=[
            jax.ShapeDtypeStruct((tokens, channels), BF16),
            jax.ShapeDtypeStruct((tokens, channels), F32),
            jax.ShapeDtypeStruct((tokens, channels), F32),
            jax.ShapeDtypeStruct((8, channels), F32),
        ],
        scratch_shapes=[pltpu.VMEM((ROWS, channels), F32)] + [pltpu.VMEM((8, channels), F32)] * 3,
        compiler_params=params(40),
        cost_estimate=pl.CostEstimate(
            flops=2 * tokens * width * channels,
            bytes_accessed=20 * MIB,
            transcendentals=tokens * channels,
        ),
        name="mix_backward",
    )(middle_low, out_t, gate_pre, states, decays)


def gates_backward(
    info, prod, state, returning, states, arriving, pre_in, pre_dec, conv, gates_in, gates_decay,
    vectors,
):
    tokens, channels = states.shape
    reach = channels + HALF
    tiles = ROWS // 8

    def kernel(
        info_ref, prod_ref, state_ref, ret_ref, states_ref, arr_ref, pre_in_ref, pre_dec_ref,
        conv_ref, gin_ref, gdec_ref, vec_ref,
        own_ref, going_ref, in_low_ref, dec_low_ref, sums_ref,
        in_cot, dec_cot, direct, previous,
    ):
        i = pl.program_id(0)

        @pl.when(i == 0)
        def _():
            previous[...] = arr_ref[...]
            sums_ref[...] = jnp.zeros_like(sums_ref)

        row = rows_of(channels)

        def tile(t, carry):
            base = pl.multiple_of(t * 8, 8)
            at = pl.ds(base, 8)
            before, sum_in, sum_dec, sum_par = carry
            start = wide(since_start(info_ref, i * ROWS + base) == 0, channels)
            adjoint = state_ref[at, :] + prod_ref[at, :] * ret_ref[0:1, :]
            here = states_ref[at, :]
            last = moved(here, before, 1, row)
            conv_out = conv_ref[at, :]
            gate = sigmoid(pre_in_ref[at, :])
            gate_dec = sigmoid(pre_dec_ref[at, :])
            log_decay = gate_dec * vec_ref[2:3, :]
            decay = jnp.exp(log_decay)
            rest = one_less_exp(2.0 * log_decay, decay)
            inverse = lax.rsqrt(rest)
            scale = jnp.where(start, 1.0, rest * inverse)
            with_conv = adjoint * conv_out
            dscale = with_conv * gate
            dlog = jnp.where(
                start, 0.0, decay * (adjoint * last - dscale * decay * inverse)
            )
            input_cot = dscale * scale * (1.0 - gate)
            shared = dlog * gate_dec
            decay_cot = shared * (1.0 - gate_dec) * vec_ref[2:3, :]
            direct[at, :] = adjoint * gate * scale
            in_cot[at, :] = input_cot
            dec_cot[at, :] = decay_cot
            return here, sum_in + input_cot, sum_dec + decay_cot, sum_par + shared

        zero = jnp.zeros((8, channels), F32)
        last = lax.fori_loop(0, tiles, tile, (previous[...], zero, zero, zero))
        previous[...] = last[0]
        for n in range(3):
            sums_ref[n * 8 : n * 8 + 8, :] += last[n + 1]
        in_low = in_cot[...].astype(BF16)
        dec_low = dec_cot[...].astype(BF16)
        in_low_ref[...] = in_low
        dec_low_ref[...] = dec_low
        for begin in range(0, channels, BLOCK):
            end = min(begin + BLOCK, channels)
            back = dot_nt(in_low[:, begin:end], gin_ref[:, begin:end]) + dot_nt(
                dec_low[:, begin:end], gdec_ref[:, begin:end]
            )
            own_ref[:, begin:end] = direct[:, begin:end] + back[:, : end - begin]
            if end - begin < BLOCK:
                going_ref[...] = back[:, end - begin :].astype(BF16)

    narrow = jax.ShapeDtypeStruct((tokens, channels), F32)
    low = jax.ShapeDtypeStruct((tokens, channels), BF16)
    return pl.pallas_call(
        kernel,
        grid=(tokens // ROWS,),
        in_specs=[
            SMEM_SPEC,
            row_spec(channels),
            row_spec(channels),
            const_spec((8, channels)),
            row_spec(channels),
            const_spec((8, channels)),
            row_spec(channels),
            row_spec(channels),
            row_spec(channels),
            const_spec((BLOCK, channels)),
            const_spec((BLOCK, channels)),
            const_spec((8, channels)),
        ],
        out_specs=[
            row_spec(channels),
            row_spec(reach - channels),
            row_spec(channels),
            row_spec(channels),
            pl.BlockSpec((24, channels), lambda i: (0, 0)),
        ],
        out_shape=[
            narrow, jax.ShapeDtypeStruct((tokens, reach - channels), BF16), low, low,
            jax.ShapeDtypeStruct((24, channels), F32),
        ],
        scratch_shapes=[pltpu.VMEM((ROWS, channels), F32)] * 3 + [pltpu.VMEM((8, channels), F32)],
        compiler_params=params(40),
        cost_estimate=pl.CostEstimate(
            flops=4 * tokens * BLOCK * channels,
            bytes_accessed=20 * MIB,
            transcendentals=5 * tokens * channels,
        ),
        name="gates_backward",
    )(
        info, prod, state, returning, states, arriving, pre_in, pre_dec, conv, gates_in,
        gates_decay, vectors,
    )


def conv_backward(
    info, own, coming, trail, branch, lead_branch, gate_cot, residual, gate_w, recur_w, taps
):
    tokens, channels = own.shape
    width = gate_w.shape[0]
    tiles = ROWS // 8
    borrowed = coming.shape[1]

    def kernel(
        info_ref, own_ref, coming_ref, trail_ref, branch_ref, lead_ref, gate_cot_ref, res_ref,
        gate_ref, recur_ref, taps_ref,
        low_ref, part_ref, sums_ref, gain_ref,
        cot, branch_cot,
    ):
        i = pl.program_id(0)

        @pl.when(i == 0)
        def _():
            cot[0:tokens, :] = own_ref[...]
            cot[0:tokens, channels - borrowed :] += coming_ref[...].astype(F32)
            cot[tokens:, :] = trail_ref[...]
            sums_ref[...] = jnp.zeros_like(sums_ref)
            gain_ref[...] = jnp.zeros_like(gain_ref)

        row = rows_of(channels)

        def tile(t, carry):
            begin = pl.multiple_of(i * ROWS + t * 8, 8)
            since = since_start(info_ref, begin)
            since_next = since_start(info_ref, begin + 8)
            here, after = cot[pl.ds(begin, 8), :], cot[pl.ds(begin + 8, 8), :]
            values = branch_ref[pl.ds(begin, 8), :]
            earlier = branch_ref[pl.ds(pl.multiple_of(jnp.maximum(begin - 8, 0), 8), 8), :]
            before = jnp.where(begin == 0, lead_ref[...], earlier)
            total = taps_ref[0:1, :channels] * here
            sums = [carry[0] + here * values]
            for k in range(1, 4):
                near = jnp.where(wide(since >= k, channels), here, 0.0)
                far = jnp.where(wide(since_next >= k, channels), after, 0.0)
                total = total + taps_ref[k : k + 1, :channels] * moved(near, far, -k, row)
                sums.append(carry[k] + near * moved(values, before, k, row))
            sums.append(carry[4] + here)
            branch_cot[pl.ds(pl.multiple_of(t * 8, 8), 8), :] = total
            return tuple(sums)

        zero = jnp.zeros((8, channels), F32)
        last = lax.fori_loop(0, tiles, tile, (zero,) * 5)
        for n in range(5):
            sums_ref[n * 8 : n * 8 + 8, :] += last[n]
        low = branch_cot[...].astype(BF16)
        low_ref[...] = low
        back = dot_nt(gate_cot_ref[...], gate_ref[...]) + dot_nt(low, recur_ref[:, :channels])
        part_ref[...] = back.astype(BF16)
        values = res_ref[...].astype(F32)
        scaled = values * lax.rsqrt(jnp.mean(values * values, axis=-1, keepdims=True) + 1e-06)
        gain_ref[...] += jnp.sum((back * scaled).reshape(ROWS // 8, 8, width), axis=0)

    return pl.pallas_call(
        kernel,
        grid=(tokens // ROWS,),
        in_specs=[
            SMEM_SPEC,
            const_spec((tokens, channels)),
            const_spec((tokens, borrowed)),
            const_spec((8, channels)),
            const_spec((tokens, channels)),
            const_spec((8, channels)),
            row_spec(channels),
            row_spec(width),
            const_spec((width, channels)),
            const_spec((width, recur_w.shape[1])),
            const_spec((8, taps.shape[1])),
        ],
        out_specs=[
            row_spec(channels),
            row_spec(width),
            pl.BlockSpec((40, channels), lambda i: (0, 0)),
            pl.BlockSpec((8, width), lambda i: (0, 0)),
        ],
        out_shape=[
            jax.ShapeDtypeStruct((tokens, channels), BF16),
            jax.ShapeDtypeStruct((tokens, width), BF16),
            jax.ShapeDtypeStruct((40, channels), F32),
            jax.ShapeDtypeStruct((8, width), F32),
        ],
        scratch_shapes=[
            pltpu.VMEM((tokens + 8, channels), F32),
            pltpu.VMEM((ROWS, channels), F32),
        ],
        compiler_params=params(48),
        cost_estimate=pl.CostEstimate(
            flops=4 * tokens * width * channels,
            bytes_accessed=24 * MIB,
            transcendentals=0,
        ),
        name="conv_backward",
    )(
        info, own, coming, trail, branch, lead_branch, gate_cot, residual, gate_w, recur_w, taps
    )


def norm_scale(values):
    return lax.rsqrt(jnp.mean(values * values, axis=-1, keepdims=True) + 1e-06)


def norm_cot(values, gain, cotan):
    r = norm_scale(values)
    through = cotan * gain
    return r * through - values * (r * r * r) * jnp.mean(through * values, axis=-1, keepdims=True)


def per_device(
    residual,
    cotangent,
    seq_lengths,
    dealing,
    pregain,
    gatelinear,
    recurlinear,
    convkernel,
    convbias,
    inputgate,
    inputbias,
    decaygate,
    decaybias,
    decayparam,
    outlinear,
    postgain,
    mlpgate,
    mlpvalue,
    mlpdown,
):
    tokens, width = residual.shape
    channels = convbias.shape[0]
    shard_rows = gatelinear.shape[0]
    tp_count, tp_mine = lax.axis_size("tp"), lax.axis_index("tp")
    is_odd = tp_mine % 2 == 1
    share = tokens // tp_count

    def canon(values):
        rolled = jnp.concatenate([values[..., HALF:], values[..., :HALF]], axis=-1)
        return jnp.where(is_odd, rolled, values)

    def uncanon(values):
        rolled = jnp.concatenate([values[..., -HALF:], values[..., :-HALF]], axis=-1)
        return jnp.where(is_odd, rolled, values)

    def swap_rows(values):
        rolled = jnp.concatenate([values[HALF:], values[:HALF]], axis=0)
        return jnp.where(is_odd, rolled, values)

    def my_share(values):
        return lax.dynamic_slice_in_dim(values, tp_mine * share, share)

    chosen = lax.dynamic_slice_in_dim(dealing, lax.axis_index("fsdp") * 3, 3)
    catalog = jnp.arange(seq_lengths.shape[0], dtype=jnp.int32)
    lengths = jnp.sum(
        jnp.where(chosen[:, None] == catalog[None, :], seq_lengths[None, :], 0), axis=1
    )
    bounds = jnp.cumsum(lengths)
    base = (lax.axis_index("ctx") * tokens).astype(jnp.int32)
    info = jnp.concatenate([bounds.astype(jnp.int32), base[None], jnp.zeros((4,), jnp.int32)])
    live = (base + jnp.arange(tokens, dtype=jnp.int32) < bounds[2]).astype(F32)[:, None]

    recur_low = canon(recurlinear.astype(BF16))
    recur_wide = jnp.concatenate([recur_low, partner(recur_low[:, channels - HALF :])], axis=1)
    small_gates = jnp.concatenate(
        [canon(inputgate.astype(BF16)), canon(decaygate.astype(BF16))], axis=0
    ).reshape(shard_rows, -1)
    recur_wide = jnp.concatenate([recur_wide, small_gates], axis=1)
    gate_full = assemble(gather_pieces(canon(gatelinear.astype(BF16)), False))
    recur_full = assemble(gather_pieces(recur_wide, True))
    out_full = assemble(gather_pieces(canon(outlinear.astype(BF16).T), False))
    down_low = mlpdown.astype(BF16).T
    cut = down_low.shape[1] // 3 // 128 * 128
    down_first = assemble(gather_pieces(down_low[:, :cut], False))
    down_rest = assemble(gather_pieces(down_low[:, cut:], True))
    down_full = jnp.concatenate([down_first, down_rest], axis=1)
    hgate_full = assemble(gather_pieces(mlpgate.astype(BF16), False))
    value_full = assemble(gather_pieces(mlpvalue.astype(BF16), True))

    gates = recur_full[:, channels + HALF :].reshape(1 << cube_bits(), 2, -1, channels)

    def gate_weights(number):
        whole = gates[:, number].reshape(BLOCK, channels)
        return jnp.concatenate(
            [whole[:, : channels - HALF], swap_rows(whole[:, channels - HALF :])], axis=1
        )

    gates_in, gates_decay = gate_weights(0), gate_weights(1)
    taps = canon(jnp.concatenate([convkernel, convbias[None], jnp.zeros((3, channels), F32)]))
    taps = jnp.concatenate([taps, partner(taps[:, channels - HALF :])], axis=1)
    vectors = canon(
        jnp.stack([inputbias, decaybias, -8.0 * jax.nn.softplus(decayparam)] + [inputbias] * 5)
    )

    residual_wide = residual.astype(F32)

    def pre_norm(values):
        values = values.astype(F32)
        return (values * norm_scale(values) * pregain).astype(BF16)

    normed = pre_norm(residual)
    lead = pre_norm(shifted(residual[tokens - 16 :], 1))
    (
        gate_pre, branch, lead_branch, conv, conv_low, pre_in, pre_dec, decays, prod, state, ends
    ) = recur_forward(
        info, normed, lead, gate_full, recur_full, taps, gates_in, gates_decay, vectors
    )
    arriving = carried(ends, False)
    states, mixed, mix_part = mix_forward(prod, state, gate_pre, arriving, out_full)
    middle = my_share(residual).astype(F32) + line_sum(mix_part)
    scaled_two = middle * norm_scale(middle)
    normed_two = line_gather((scaled_two * postgain).astype(BF16))
    hidden_gate = dot(normed_two, hgate_full)
    hidden_value = dot(normed_two, value_full)
    gelu_hidden, gelu_slope = gelu_both(hidden_gate)
    hidden = (gelu_hidden * hidden_value).astype(BF16)

    upstream = cotangent.astype(F32) * live
    upstream_low = upstream.astype(BF16)
    hidden_cot = dot(upstream_low, down_full)
    value_cot = (hidden_cot * gelu_hidden).astype(BF16)
    hgate_cot = (hidden_cot * hidden_value * gelu_slope).astype(BF16)
    normed_two_part = (dot_nt(hgate_cot, hgate_full) + dot_nt(value_cot, value_full)).astype(BF16)
    normed_two_cot = line_sum(normed_two_part)
    postgain_grad = jnp.sum(normed_two_cot * scaled_two, axis=0)
    middle_cot = my_share(upstream) + norm_cot(middle, postgain, normed_two_cot)
    middle_low = line_gather(middle_cot.astype(BF16))

    mlp_sum = line_sum(dot_nt(hidden, down_full).astype(BF16))
    block_out = line_gather((my_share(live) * (middle + mlp_sum)).astype(BF16))

    down_grad = dot_tn(upstream_low, hidden).astype(BF16)
    hgate_grad = dot_tn(normed_two, hgate_cot).astype(BF16)
    value_grad = dot_tn(normed_two, value_cot).astype(BF16)

    gate_pre_cot, rev_prod, rev_state, rev_ends = mix_backward(
        middle_low, out_full, gate_pre, states, decays
    )
    returning = carried(rev_ends, True)
    own, going, input_low, decay_low, gate_sums = gates_backward(
        info, rev_prod, rev_state, returning, states, arriving, pre_in, pre_dec, conv, gates_in,
        gates_decay, vectors,
    )
    coming = partner(going)
    trail = shifted(own[:8], -1)
    trail_coming = shifted(partner(going[:16]), -1)[:8].astype(F32)
    trail = jnp.concatenate(
        [trail[:, : channels - HALF], trail[:, channels - HALF :] + trail_coming], axis=1
    )
    branch_low, normed_part, conv_sums, gain_sums = conv_backward(
        info, own, coming, trail, branch, lead_branch, gate_pre_cot, residual, gate_full,
        recur_full, taps,
    )
    normed_cot = line_sum(normed_part)
    residual_own = my_share(residual).astype(F32)
    residual_grad = line_gather(
        (middle_cot + norm_cot(residual_own, pregain, normed_cot)).astype(BF16)
    )

    out_grad = dot_tn(middle_low, mixed).astype(BF16)
    gatelin_grad = dot_tn(normed, gate_pre_cot).astype(BF16)
    recur_grad = dot_tn(normed, branch_low).astype(BF16)

    def gate_grads(cotan):
        whole = jnp.concatenate(
            [
                dot_tn(conv_low[:, begin : begin + BLOCK], cotan[:, begin : begin + BLOCK])
                for begin in range(0, channels, BLOCK)
            ],
            axis=1,
        )
        return jnp.concatenate(
            [whole[:, : channels - HALF], swap_rows(whole[:, channels - HALF :])], axis=1
        ).reshape(1 << cube_bits(), -1, channels)

    small_grads = jnp.concatenate(
        [gate_grads(input_low), gate_grads(decay_low)], axis=1
    ).reshape(-1, channels)
    small_own = uncanon(scatter_sum(small_grads, False))
    gate_rows = inputgate.shape[0]

    parts = jnp.sum(
        jnp.concatenate([conv_sums, gate_sums], axis=0).reshape(8, 8, channels), axis=1
    )
    gains = jnp.concatenate(
        [jnp.sum(gain_sums, axis=0).reshape(-1, channels), postgain_grad.reshape(-1, channels)]
    )
    sums = jnp.concatenate([parts, gains])
    for position in range(cube_bits()):
        sums = sums + flip(sums, position)
    gains = sums[8:]
    for bit in range(tp_count.bit_length() - 1):
        gains = gains + partner(gains, bit)
    gains = gains.reshape(2, width)
    parts = uncanon(sums[:8])

    return (
        block_out,
        residual_grad,
        gains[0],
        uncanon(scatter_sum(gatelin_grad, False)),
        uncanon(scatter_sum(recur_grad, True)),
        parts[0:4],
        parts[4],
        small_own[:gate_rows],
        parts[5],
        small_own[gate_rows:],
        parts[6],
        parts[7] * (-8.0 * jax.nn.sigmoid(decayparam)),
        uncanon(scatter_sum(out_grad, False)).T,
        gains[1],
        scatter_sum(hgate_grad, False),
        scatter_sum(value_grad, True),
        jnp.concatenate(
            [scatter_sum(down_grad[:, :cut], False), scatter_sum(down_grad[:, cut:], True)], axis=1
        ).T,
    )


def solution(mesh):
    rows, by_tp = P(("fsdp", "ctx"), None), P("tp")
    matrix, turned = P(("fsdp", "ctx"), "tp"), P("tp", ("fsdp", "ctx"))
    return jax.shard_map(
        per_device,
        mesh=mesh,
        in_specs=(
            rows, rows, P(), P(), P(), matrix, matrix, P(None, "tp"), by_tp, matrix, by_tp, matrix,
            by_tp, by_tp, turned, P(), matrix, matrix, turned,
        ),
        out_specs=(
            rows, rows, P(), matrix, matrix, P(None, "tp"), by_tp, matrix, by_tp, matrix, by_tp,
            by_tp, turned, P(), matrix, matrix, turned,
        ),
        check_vma=False,
    )
```

time: 2170 us -> 1090 us (0.50)
  waiting for transfers between devices: 1240 us -> 411 us
  local copies, waits for them, and re-layouts: 400 us -> 77.9 us
  starting transfers between devices: 6.81 us -> 212 us
  blocking collectives: 107 us -> 0 us
  Pallas kernels: 0 us -> 95.7 us
  matrix products: 198 us -> 131 us
  other arithmetic: 180 us -> 144 us
    psum x3 -> x0, waiting for transfers between devices: 774 us -> none  [the longest x1 274 us: per_device(): lax.psum(mlp_part.astype(jnp.bfloat16), 'tp').astype(jnp.float32)]
    ppermute x4 -> x139, waiting for transfers between devices: 6.61 us -> 411 us  [the longest x76 157 us: flip(): lax.ppermute(value, axis, [(i, i ^ 1 << bit) for i in range(lax.axis_size...]
    reduce_scatter x8 -> x0, waiting for transfers between devices: 305 us -> none  [the longest x1 79.8 us: per_device(): lax.psum_scatter(hgate_grad.astype(jnp.bfloat16), ('fsdp', 'ctx'), scatte...]
    slice x144 -> x49, local copies, waits for them, and re-layouts: 262 us -> 11.1 us  [the longest x1 3.28 us: per_device(): down_grad[:, cut:]]
    ppermute x4 -> x139, starting transfers between devices: 5.31 us -> 212 us  [the longest x76 65.3 us: flip(): lax.ppermute(value, axis, [(i, i ^ 1 << bit) for i in range(lax.axis_size...]
    all_gather x6 -> x0, waiting for transfers between devices: 156 us -> none  [the longest x1 50.4 us: per_device(): lax.all_gather(mlpgate.astype(jnp.bfloat16), ('fsdp', 'ctx'), axis=0, til...]
    pallas_call x0 -> x12, Pallas kernels: none -> 95.7 us  [the longest x1 24.3 us: recur_forward(): pl.pallas_call(kernel, grid=(tokens // ROWS,), in_specs=[SMEM_SPEC, row_s...]
    dot_general x24 -> x18, matrix products: 198 us -> 131 us  [the longest x12 51.9 us: dot_tn(): lax.dot_general(a, b, (((0,), (0,)), ((), ())), preferred_element_type=F32)]
  transfers between devices with their start and end apart: 21 -> 139, of which waited for: 15 -> 50; matrix products, arithmetic and copies ran while one was open for 20% -> 20% of each run, Pallas kernels for 0% -> 8%
where the time goes in v1:
time: 1090 us; the launch traced here: 1080 us
  waiting for transfers between devices  411 us (38%)
  starting transfers between devices  212 us (19%)
  other arithmetic  144 us (13%)
  matrix products  131 us (12%)
  Pallas kernels  95.7 us (9%)
  local copies, waits for them, and re-layouts  77.9 us (7%)
    ppermute x76, waiting for transfers between devices, flip(): lax.ppermute(value, axis, [(i, i ^ 1 << bit) for i in range(lax.axis_size...  157 us
    ppermute x12, waiting for transfers between devices, line_sum(): lax.ppermute(rightward.astype(BF16), 'tp', [(s, s + 1) for s in range(min...  123 us
    ppermute x12, waiting for transfers between devices, line_gather(): lax.ppermute(right[step - 1], 'tp', [(s, s - 1) for s in range(1, count -...  92.5 us
    ppermute x76, starting transfers between devices, flip(): lax.ppermute(value, axis, [(i, i ^ 1 << bit) for i in range(lax.axis_size...  65.3 us
    ppermute x12, starting transfers between devices, line_sum(): lax.ppermute(rightward.astype(BF16), 'tp', [(s, s + 1) for s in range(min...  61.4 us
    dot_general x12, matrix products, dot_tn(): lax.dot_general(a, b, (((0,), (0,)), ((), ())), preferred_element_type=F32)  51.9 us
    dot_general x3, matrix products, dot(): return jnp.dot(a, b, preferred_element_type=F32)  44.6 us
    unnamed x264, local copies, waits for them, and re-layouts  43.6 us
  transfers between devices with their start and end apart: 139, of which 50 were waited for; matrix products, arithmetic and copies ran while one was open for 20% of the time, Pallas kernels for 8%

profile of v1, /device:TPU:0, one launch (start us, length us, event | category | flops | bytes accessed | tf_op | source)
XLA Modules:
  0.0 1075.3 jit_solution(3344917698504647505)
XLA Ops:
  43.7 8.2 collective-permute-done.6.refs_6_
  56.5 7.1 collective-permute-done.14.refs_6_
  75.5 24.3 %recur_forward.1 = (f32[768,640]{1,0:T(8,128)S(1)}, f32[768,640]{1,0:T(8,128)S(1)}, f32[8,640]{1,0:T(8,128)S(1)}, f32[768,640]{1,0:T(8,128)S(1)}, bf16[768,768]{...) custom-call(s32[8]{0:T(128)S(1)} %pad_add_fusion.info_ref, ...), custom_call_target="tpu_custom_call" | custom-call | flops 5536481280 | bytes 31457280 | tf_op jit(solution)/shard_map/recur_forward/pallas_call | solution.py:315
  117.6 7.9 mix_forward.1
  134.7 17.6 %collective-permute-done.27 = bf16[192,2560]{1,0:T(8,128)(2,1)} collective-permute-done((bf16[192,2560]{1,0:T(8,128)(2,1)}, bf16[192,2560]{1,0:T(8,128)(2,1)}, u32[]{:S(2)}, u32[]{:S(2)}) %collective-permute-start.27) | collective-permute-done | bytes 983072 | tf_op jit(solution)/shard_map/ppermute | solution.py:114
  165.6 13.1 %collective-permute-done.28 = bf16[192,2560]{1,0:T(8,128)(2,1)} collective-permute-done((bf16[192,2560]{1,0:T(8,128)(2,1)}, bf16[192,2560]{1,0:T(8,128)(2,1)}, u32[]{:S(2)}, u32[]{:S(2)}) %collective-permute-start.28) | collective-permute-done | bytes 983072 | tf_op jit(solution)/shard_map/ppermute | solution.py:114
  198.0 7.8 collective-permute-done.58.refs_6_
  215.7 15.6 %collective-permute-done.49.refs_4_ = bf16[320,1920]{1,0:T(8,128)(2,1)} collective-permute-done((bf16[320,1920]{1,0:T(8,128)(2,1)S(1)}, bf16[320,1920]{1,0:T(8,128)(2,1)}, u32[]{:S(2)}, u32[]{:S(2)}) %collective-permute-start.49) | collective-permute-done | bytes 1228832 | tf_op jit(solution)/shard_map/ppermute | solution.py:21
  240.3 21.3 %collective-permute-done.40.refs_2_ = bf16[320,1920]{1,0:T(8,128)(2,1)} collective-permute-done((bf16[320,1920]{1,0:T(8,128)(2,1)}, bf16[320,1920]{1,0:T(8,128)(2,1)}, u32[]{:S(2)}, u32[]{:S(2)}) %collective-permute-start.40) | collective-permute-done | bytes 1228832 | tf_op jit(solution)/shard_map/ppermute | solution.py:21
  264.1 15.0 %collective-permute-done.65.refs_6_ = bf16[320,1280]{1,0:T(8,128)(2,1)} collective-permute-done((bf16[320,1280]{1,0:T(8,128)(2,1)}, bf16[320,1280]{1,0:T(8,128)(2,1)}, u32[]{:S(2)}, u32[]{:S(2)}) %collective-permute-start.65) | collective-permute-done | bytes 819232 | tf_op jit(solution)/shard_map/ppermute | solution.py:21
  284.7 19.1 %collective-permute-done.51.refs_6_ = bf16[320,1920]{1,0:T(8,128)(2,1)} collective-permute-done((bf16[320,1920]{1,0:T(8,128)(2,1)}, bf16[320,1920]{1,0:T(8,128)(2,1)}, u32[]{:S(2)}, u32[]{:S(2)}) %collective-permute-start.51) | collective-permute-done | bytes 1228832 | tf_op jit(solution)/shard_map/ppermute | solution.py:21
  318.7 6.0 assemble.13
  324.8 9.8 collective-permute-done.44.refs_6_
  338.0 12.0 %fusion.3 = f32[768,1920]{1,0:T(8,128)} fusion(bf16[2560,1280]{1,0:T(8,128)(2,1)} %assemble.13, bf16[2560,640]{1,0:T(8,128)(2,1)S(1)} %assemble.12, bf16[768,2560]{1,0:T(8,128)(2,1)S(1)} %copy-done.82, f32[768]{0:T(1024)S(1)} %fusion.39), kind=kOutput, calls=%fused_computation.11 | convolution fusion | flops 7575306240 | bytes 19663872 | tf_op jit(solution)/shard_map/dot_general | solution.py:201
  364.9 8.8 select_select_fusion.15
  374.6 11.5 %fusion.49 = f32[768,1920]{1,0:T(8,128)} fusion(bf16[2560,1920]{1,0:T(8,128)(2,1)S(1)} %assemble.11, bf16[192,2560]{1,0:T(8,128)(2,1)} %get-tuple-element.159, bf16[192,2560]{1,0:T(8,128)(2,1)} %get-tuple-element.158, bf16[192,2560]{1,0:T(8,128)(2,1)S(1)} %get-tuple-element.157, bf16[192,2560]{1,0:T(8,128)(2,1)S(1)} %get-tuple-element.156), kind=kOutput, calls=%fused_computation.258 | convolution fusion | flops 7565475840 | bytes 19660800 | tf_op jit(solution)/shard_map/dot_general | solution.py:201
  386.1 21.1 %multiply_convert_fusion.1 = (bf16[768,1920]{1,0:T(8,128)(2,1)}, bf16[768,1920]{1,0:T(8,128)(2,1)}, bf16[768,1920]{1,0:T(8,128)(2,1)}) fusion(f32[768,1920]{1,0:T(8,128)} %fusion.3, f32[768,1920]{1,0:T(8,128)} %fusion.49, bf16[2560,1920]{1,0:T(8,128)(2,1)} %copy-done.3, bf16[192,2560]{1,0:T(8,128)(2,1)} %get-tuple-element.159, ...), kind=kOutput, calls=%fused_computation.14 | convolution fusion | flops 7600865280 | bytes 34406400 | tf_op jit(solution)/shard_map/dot_general | solution.py:201
  407.3 12.8 %fusion.6 = bf16[768,2560]{1,0:T(8,128)(2,1)} fusion(bf16[768,1920]{1,0:T(8,128)(2,1)} %get-tuple-element.89, bf16[2560,1280]{1,0:T(8,128)(2,1)} %assemble.13, bf16[2560,640]{1,0:T(8,128)(2,1)S(1)} %copy-done.7), kind=kOutput, calls=%fused_computation.19 | convolution fusion | flops 7571374080 | bytes 16711680 | tf_op jit(solution)/shard_map/dot_general | solution.py:205
  420.1 11.0 %convolution_convert_fusion = bf16[2560,1920]{1,0:T(8,128)(2,1)} fusion(bf16[768,1920]{1,0:T(8,128)(2,1)S(1)} %copy-done.125, bf16[768,2560]{1,0:T(8,128)(2,1)S(1)} %copy-done.83, f32[768]{0:T(1024)S(1)} %fusion.39), kind=kOutput, calls=%fused_computation | convolution fusion | flops 7560560640 | bytes 16714752 | tf_op jit(solution)/shard_map/dot_general | solution.py:209
  431.2 10.7 fusion.59
  441.9 13.3 %convolution_convert_fusion.1 = bf16[2560,1920]{1,0:T(8,128)(2,1)} fusion(bf16[768,1920]{1,0:T(8,128)(2,1)} %get-tuple-element.88, bf16[192,2560]{1,0:T(8,128)(2,1)} %get-tuple-element.159, bf16[192,2560]{1,0:T(8,128)(2,1)} %get-tuple-element.158, bf16[192,2560]{1,0:T(8,128)(2,1)} %copy-done.103, bf16[192,2560]{1,0:T(8,128)(2,1)S(1)} %get-tuple-element.156), kind=kOutput, calls=%fused_computation.1 | convolution fusion | flops 7570391040 | bytes 16711680 | tf_op jit(solution)/shard_map/dot_general | solution.py:209
  456.6 6.2 collective-permute-start.67
  464.4 11.2 %add_convert_fusion = bf16[768,2560]{1,0:T(8,128)(2,1)S(1)} fusion(f32[768,2560]{1,0:T(8,128)} %fusion.59, bf16[768,1920]{1,0:T(8,128)(2,1)} %get-tuple-element.87, bf16[2560,1920]{1,0:T(8,128)(2,1)S(1)} %bitcast.46), kind=kOutput, calls=%fused_computation.9 | convolution fusion | flops 7553679360 | bytes 24576000 | tf_op jit(solution)/shard_map/dot_general | solution.py:205
  493.2 11.1 %convolution_convert_fusion.2 = bf16[2560,1920]{1,0:T(8,128)(2,1)S(1)} fusion(bf16[768,1920]{1,0:T(8,128)(2,1)} %get-tuple-element.87, bf16[192,2560]{1,0:T(8,128)(2,1)} %get-tuple-element.159, bf16[192,2560]{1,0:T(8,128)(2,1)} %get-tuple-element.158, bf16[192,2560]{1,0:T(8,128)(2,1)} %copy-done.103, bf16[192,2560]{1,0:T(8,128)(2,1)} %copy-done.102), kind=kOutput, calls=%fused_computation.2 | convolution fusion | flops 7570391040 | bytes 16711680 | tf_op jit(solution)/shard_map/dot_general | solution.py:209
  517.3 14.9 %collective-permute-done.80 = bf16[192,2560]{1,0:T(8,128)(2,1)S(1)} collective-permute-done((bf16[192,2560]{1,0:T(8,128)(2,1)S(1)}, bf16[192,2560]{1,0:T(8,128)(2,1)S(1)}, u32[]{:S(2)}, u32[]{:S(2)}) %collective-permute-start.80) | collective-permute-done | bytes 983072 | tf_op jit(solution)/shard_map/ppermute | solution.py:114
  535.0 16.6 %collective-permute-done.68 = bf16[192,2560]{1,0:T(8,128)(2,1)S(1)} collective-permute-done((bf16[192,2560]{1,0:T(8,128)(2,1)S(1)}, bf16[192,2560]{1,0:T(8,128)(2,1)S(1)}, u32[]{:S(2)}, u32[]{:S(2)}) %collective-permute-start.68) | collective-permute-done | bytes 983072 | tf_op jit(solution)/shard_map/ppermute | solution.py:114
  554.9 5.9 collective-permute-start.81
  566.5 13.0 %collective-permute-done.81 = bf16[192,2560]{1,0:T(8,128)(2,1)} collective-permute-done((bf16[192,2560]{1,0:T(8,128)(2,1)S(1)}, bf16[192,2560]{1,0:T(8,128)(2,1)}, u32[]{:S(2)}, u32[]{:S(2)}) %collective-permute-start.81) | collective-permute-done | bytes 983072 | tf_op jit(solution)/shard_map/ppermute | solution.py:114
  579.5 7.9 collective-permute-start.69
  595.9 12.6 %collective-permute-done.69 = bf16[192,2560]{1,0:T(8,128)(2,1)} collective-permute-done((bf16[192,2560]{1,0:T(8,128)(2,1)}, bf16[192,2560]{1,0:T(8,128)(2,1)}, u32[]{:S(2)}, u32[]{:S(2)}) %collective-permute-start.69) | collective-permute-done | bytes 983072 | tf_op jit(solution)/shard_map/ppermute | solution.py:114
  608.5 15.1 %collective-permute-done.72 = bf16[192,2560]{1,0:T(8,128)(2,1)} collective-permute-done((bf16[192,2560]{1,0:T(8,128)(2,1)}, bf16[192,2560]{1,0:T(8,128)(2,1)}, u32[]{:S(2)}, u32[]{:S(2)}) %collective-permute-start.72) | collective-permute-done | bytes 983072 | tf_op jit(solution)/shard_map/ppermute | solution.py:117
  644.0 7.3 collective-permute-done.85
  663.0 6.4 collective-permute-done.88
  674.2 16.2 %collective-permute-done.76 = bf16[192,2560]{1,0:T(8,128)(2,1)} collective-permute-done((bf16[192,2560]{1,0:T(8,128)(2,1)}, bf16[192,2560]{1,0:T(8,128)(2,1)}, u32[]{:S(2)}, u32[]{:S(2)}) %collective-permute-start.76) | collective-permute-done | bytes 983072 | tf_op jit(solution)/shard_map/ppermute | solution.py:130
  700.5 10.8 %collective-permute-done.89 = bf16[192,2560]{1,0:T(8,128)(2,1)S(1)} collective-permute-done((bf16[192,2560]{1,0:T(8,128)(2,1)}, bf16[192,2560]{1,0:T(8,128)(2,1)S(1)}, u32[]{:S(2)}, u32[]{:S(2)}) %collective-permute-start.89) | collective-permute-done | bytes 983072 | tf_op jit(solution)/shard_map/ppermute | solution.py:130
  720.6 12.0 %collective-permute-done.77 = bf16[192,2560]{1,0:T(8,128)(2,1)} collective-permute-done((bf16[192,2560]{1,0:T(8,128)(2,1)}, bf16[192,2560]{1,0:T(8,128)(2,1)}, u32[]{:S(2)}, u32[]{:S(2)}) %collective-permute-start.77) | collective-permute-done | bytes 983072 | tf_op jit(solution)/shard_map/ppermute | solution.py:130
  735.4 18.1 %collective-permute-done.90 = bf16[192,2560]{1,0:T(8,128)(2,1)S(1)} collective-permute-done((bf16[192,2560]{1,0:T(8,128)(2,1)S(1)}, bf16[192,2560]{1,0:T(8,128)(2,1)S(1)}, u32[]{:S(2)}, u32[]{:S(2)}) %collective-permute-start.90) | collective-permute-done | bytes 983072 | tf_op jit(solution)/shard_map/ppermute | solution.py:130
  760.3 9.6 mix_backward.1
  793.6 10.2 gates_backward.1
  836.0 23.3 %conv_backward.1 = (bf16[768,640]{1,0:T(8,128)(2,1)S(1)}, bf16[768,2560]{1,0:T(8,128)(2,1)}, f32[40,640]{1,0:T(8,128)S(1)}, f32[8,2560]{1,0:T(8,128)S(1)}) custom-call(s32[8]{0:T(128)S(1)} %pad_add_fusion.info_ref, f32[768,640]{1,0:T(8,128)S(1)} %copy-done.53, bf16[768,128]{1,0:T(8,128)(2,1)S(1)} %collective-permute-done.94.coming_ref, ...), custom_call_target="tpu_custom_call" | custom-call | flops 5033164800 | bytes 25165824 | tf_op jit(solution)/shard_map/conv_backward/pallas_call | solution.py:653
  905.7 11.2 %collective-permute-done.98 = bf16[192,2560]{1,0:T(8,128)(2,1)S(1)} collective-permute-done((bf16[192,2560]{1,0:T(8,128)(2,1)}, bf16[192,2560]{1,0:T(8,128)(2,1)S(1)}, u32[]{:S(2)}, u32[]{:S(2)}) %collective-permute-start.98) | collective-permute-done | bytes 983072 | tf_op jit(solution)/shard_map/ppermute | solution.py:114
  932.7 12.7 %collective-permute-done.99 = bf16[192,2560]{1,0:T(8,128)(2,1)S(1)} collective-permute-done((bf16[192,2560]{1,0:T(8,128)(2,1)S(1)}, bf16[192,2560]{1,0:T(8,128)(2,1)S(1)}, u32[]{:S(2)}, u32[]{:S(2)}) %collective-permute-start.99) | collective-permute-done | bytes 983072 | tf_op jit(solution)/shard_map/ppermute | solution.py:114
  949.6 7.9 collective-permute-done.132
  963.1 11.7 %collective-permute-start.100 = (bf16[192,2560]{1,0:T(8,128)(2,1)S(1)}, bf16[192,2560]{1,0:T(8,128)(2,1)S(1)}, u32[]{:S(2)}, u32[]{:S(2)}) collective-permute-start(bf16[192,2560]{1,0:T(8,128)(2,1)S(1)} %get-tuple-element.112), channel_id=1, source_target_pairs={{0,1},{1,2},{2,3},{4,5},{5,6},{6,7},{8,9},{9,10},{10,11},{12,13},{... | collective-permute-start | bytes 2949128 | tf_op jit(solution)/shard_map/ppermute | solution.py:114
  981.5 10.8 %collective-permute-done.100 = bf16[192,2560]{1,0:T(8,128)(2,1)S(1)} collective-permute-done((bf16[192,2560]{1,0:T(8,128)(2,1)S(1)}, bf16[192,2560]{1,0:T(8,128)(2,1)S(1)}, u32[]{:S(2)}, u32[]{:S(2)}) %collective-permute-start.100) | collective-permute-done | bytes 983072 | tf_op jit(solution)/shard_map/ppermute | solution.py:114
  1014.3 15.7 %collective-permute-done.126 = bf16[320,640]{1,0:T(8,128)(2,1)S(1)} collective-permute-done((bf16[320,640]{1,0:T(8,128)(2,1)S(1)}, bf16[320,640]{1,0:T(8,128)(2,1)S(1)}, u32[]{:S(2)}, u32[]{:S(2)}) %collective-permute-start.126) | collective-permute-done | bytes 409632 | tf_op jit(solution)/shard_map/ppermute | solution.py:21
  1038.6 17.8 %collective-permute-done.108 = bf16[192,2560]{1,0:T(8,128)(2,1)S(1)} collective-permute-done((bf16[192,2560]{1,0:T(8,128)(2,1)S(1)}, bf16[192,2560]{1,0:T(8,128)(2,1)S(1)}, u32[]{:S(2)}, u32[]{:S(2)}) %collective-permute-start.108) | collective-permute-done | bytes 983072 | tf_op jit(solution)/shard_map/ppermute | solution.py:130
  1061.6 10.8 %collective-permute-done.109 = bf16[192,2560]{1,0:T(8,128)(2,1)S(1)} collective-permute-done((bf16[192,2560]{1,0:T(8,128)(2,1)S(1)}, bf16[192,2560]{1,0:T(8,128)(2,1)S(1)}, u32[]{:S(2)}, u32[]{:S(2)}) %collective-permute-start.109) | collective-permute-done | bytes 983072 | tf_op jit(solution)/shard_map/ppermute | solution.py:130
  (733 shorter events, 470.8 us)
Async XLA Ops:
  70.5 40.2 %collective-permute-start.20 = (bf16[320,640]{1,0:T(8,128)(2,1)S(1)}, bf16[320,640]{1,0:T(8,128)(2,1)S(1)}, u32[]{:S(2)}, u32[]{:S(2)}) collective-permute-start(bf16[320,640]{1,0:T(8,128)(2,1)S(1)} %maximum_select_fusion.5.refs_0_), channel_id=1, source_target_pairs={{0,4},{4,0},{8,12},{12,8},{1,5},{5,1},{9,13},{13,9},{2,6},{6,2},{1... | collective-permute-start | bytes 1228808 | tf_op jit(solution)/shard_map/ppermute | solution.py:21
  70.5 42.4 %collective-permute-start.22 = (bf16[320,640]{1,0:T(8,128)(2,1)S(1)}, bf16[320,640]{1,0:T(8,128)(2,1)}, u32[]{:S(2)}, u32[]{:S(2)}) collective-permute-start(bf16[320,640]{1,0:T(8,128)(2,1)S(1)} %collective-permute-done.21.refs_2_), channel_id=1, source_target_pairs={{0,4},{4,0},{8,12},{12,8},{1,5},{5,1},{9,13},{13,9},{2,6},{6,2},{1... | collective-permute-start | bytes 1228808 | tf_op jit(solution)/shard_map/ppermute | solution.py:21
  71.0 43.2 %collective-permute-start.24 = (bf16[320,640]{1,0:T(8,128)(2,1)}, bf16[320,640]{1,0:T(8,128)(2,1)}, u32[]{:S(2)}, u32[]{:S(2)}) collective-permute-start(bf16[320,640]{1,0:T(8,128)(2,1)} %collective-permute-done.23.refs_4_), channel_id=1, source_target_pairs={{0,4},{4,0},{8,12},{12,8},{1,5},{5,1},{9,13},{13,9},{2,6},{6,2},{1... | collective-permute-start | bytes 1228808 | tf_op jit(solution)/shard_map/ppermute | solution.py:21
  71.1 43.2 %collective-permute-start.26 = (bf16[320,640]{1,0:T(8,128)(2,1)}, bf16[320,640]{1,0:T(8,128)(2,1)}, u32[]{:S(2)}, u32[]{:S(2)}) collective-permute-start(bf16[320,640]{1,0:T(8,128)(2,1)} %collective-permute-done.25.refs_6_), channel_id=1, source_target_pairs={{0,4},{4,0},{8,12},{12,8},{1,5},{5,1},{9,13},{13,9},{2,6},{6,2},{1... | collective-permute-start | bytes 1228808 | tf_op jit(solution)/shard_map/ppermute | solution.py:21
  133.0 31.1 %collective-permute-start.30 = (bf16[192,2560]{1,0:T(8,128)(2,1)}, bf16[192,2560]{1,0:T(8,128)(2,1)}, u32[]{:S(2)}, u32[]{:S(2)}) collective-permute-start(bf16[192,2560]{1,0:T(8,128)(2,1)} %get-tuple-element.127), channel_id=1, source_target_pairs={{3,2},{7,6},{11,10},{15,14},{19,18},{23,22},{27,26},{31,30}} | collective-permute-start | bytes 2949128 | tf_op jit(solution)/shard_map/ppermute | solution.py:117
  161.4 33.2 %collective-permute-start.63 = (bf16[320,1280]{1,0:T(8,128)(2,1)}, bf16[320,1280]{1,0:T(8,128)(2,1)}, u32[]{:S(2)}, u32[]{:S(2)}) collective-permute-start(bf16[320,1280]{1,0:T(8,128)(2,1)} %slice.565.refs_0_), channel_id=1, source_target_pairs={{0,16},{16,0},{1,17},{17,1},{2,18},{18,2},{3,19},{19,3},{4,20},{20... | collective-permute-start | bytes 2457608 | tf_op jit(solution)/shard_map/ppermute | solution.py:21
  162.0 32.8 %collective-permute-start.61 = (bf16[320,1280]{1,0:T(8,128)(2,1)}, bf16[320,1280]{1,0:T(8,128)(2,1)}, u32[]{:S(2)}, u32[]{:S(2)}) collective-permute-start(bf16[320,1280]{1,0:T(8,128)(2,1)} %slice.565.refs_0_), channel_id=1, source_target_pairs={{0,8},{4,12},{8,0},{12,4},{1,9},{5,13},{9,1},{13,5},{2,10},{6,14},... | collective-permute-start | bytes 2457608 | tf_op jit(solution)/shard_map/ppermute | solution.py:21
  194.8 36.5 %collective-permute-start.49 = (bf16[320,1920]{1,0:T(8,128)(2,1)S(1)}, bf16[320,1920]{1,0:T(8,128)(2,1)}, u32[]{:S(2)}, u32[]{:S(2)}) collective-permute-start(bf16[320,1920]{1,0:T(8,128)(2,1)S(1)} %convert_element_type.661.refs_0_), channel_id=1, source_target_pairs={{0,16},{16,0},{1,17},{17,1},{2,18},{18,2},{3,19},{19,3},{4,20},{20... | collective-permute-start | bytes 3686408 | tf_op jit(solution)/shard_map/ppermute | solution.py:21
  196.3 36.7 %collective-permute-start.47 = (bf16[320,1920]{1,0:T(8,128)(2,1)S(1)}, bf16[320,1920]{1,0:T(8,128)(2,1)}, u32[]{:S(2)}, u32[]{:S(2)}) collective-permute-start(bf16[320,1920]{1,0:T(8,128)(2,1)S(1)} %convert_element_type.661.refs_0_), channel_id=1, source_target_pairs={{0,8},{4,12},{8,0},{12,4},{1,9},{5,13},{9,1},{13,5},{2,10},{6,14},... | collective-permute-start | bytes 3686408 | tf_op jit(solution)/shard_map/ppermute | solution.py:21
  231.3 30.3 %collective-permute-start.40 = (bf16[320,1920]{1,0:T(8,128)(2,1)}, bf16[320,1920]{1,0:T(8,128)(2,1)}, u32[]{:S(2)}, u32[]{:S(2)}) collective-permute-start(bf16[320,1920]{1,0:T(8,128)(2,1)} %convert_element_type.660.refs_0_), channel_id=1, source_target_pairs={{0,8},{4,12},{8,0},{12,4},{1,9},{5,13},{9,1},{13,5},{2,10},{6,14},... | collective-permute-start | bytes 3686408 | tf_op jit(solution)/shard_map/ppermute | solution.py:21
  234.5 29.4 %collective-permute-start.39 = (bf16[320,1920]{1,0:T(8,128)(2,1)}, bf16[320,1920]{1,0:T(8,128)(2,1)}, u32[]{:S(2)}, u32[]{:S(2)}) collective-permute-start(bf16[320,1920]{1,0:T(8,128)(2,1)} %convert_element_type.660.refs_0_), channel_id=1, source_target_pairs={{0,4},{4,0},{8,12},{12,8},{1,5},{5,1},{9,13},{13,9},{2,6},{6,2},{1... | collective-permute-start | bytes 3686408 | tf_op jit(solution)/shard_map/ppermute | solution.py:21
  234.5 44.6 %collective-permute-start.65 = (bf16[320,1280]{1,0:T(8,128)(2,1)}, bf16[320,1280]{1,0:T(8,128)(2,1)}, u32[]{:S(2)}, u32[]{:S(2)}) collective-permute-start(bf16[320,1280]{1,0:T(8,128)(2,1)} %collective-permute-done.63.refs_4_), channel_id=1, source_target_pairs={{0,8},{4,12},{8,0},{12,4},{1,9},{5,13},{9,1},{13,5},{2,10},{6,14},... | collective-permute-start | bytes 2457608 | tf_op jit(solution)/shard_map/ppermute | solution.py:21
  239.7 39.7 %collective-permute-start.64 = (bf16[320,1280]{1,0:T(8,128)(2,1)}, bf16[320,1280]{1,0:T(8,128)(2,1)S(1)}, u32[]{:S(2)}, u32[]{:S(2)}) collective-permute-start(bf16[320,1280]{1,0:T(8,128)(2,1)} %collective-permute-done.63.refs_4_), channel_id=1, source_target_pairs={{0,4},{4,0},{8,12},{12,8},{1,5},{5,1},{9,13},{13,9},{2,6},{6,2},{1... | collective-permute-start | bytes 2457608 | tf_op jit(solution)/shard_map/ppermute | solution.py:21
  262.2 41.6 %collective-permute-start.51 = (bf16[320,1920]{1,0:T(8,128)(2,1)}, bf16[320,1920]{1,0:T(8,128)(2,1)}, u32[]{:S(2)}, u32[]{:S(2)}) collective-permute-start(bf16[320,1920]{1,0:T(8,128)(2,1)} %collective-permute-done.49.refs_4_), channel_id=1, source_target_pairs={{0,8},{4,12},{8,0},{12,4},{1,9},{5,13},{9,1},{13,5},{2,10},{6,14},... | collective-permute-start | bytes 3686408 | tf_op jit(solution)/shard_map/ppermute | solution.py:21
  263.9 39.9 %collective-permute-start.50 = (bf16[320,1920]{1,0:T(8,128)(2,1)}, bf16[320,1920]{1,0:T(8,128)(2,1)S(1)}, u32[]{:S(2)}, u32[]{:S(2)}) collective-permute-start(bf16[320,1920]{1,0:T(8,128)(2,1)} %collective-permute-done.49.refs_4_), channel_id=1, source_target_pairs={{0,4},{4,0},{8,12},{12,8},{1,5},{5,1},{9,13},{13,9},{2,6},{6,2},{1... | collective-permute-start | bytes 3686408 | tf_op jit(solution)/shard_map/ppermute | solution.py:21
  304.8 29.7 %collective-permute-start.44 = (bf16[320,1920]{1,0:T(8,128)(2,1)}, bf16[320,1920]{1,0:T(8,128)(2,1)}, u32[]{:S(2)}, u32[]{:S(2)}) collective-permute-start(bf16[320,1920]{1,0:T(8,128)(2,1)} %collective-permute-done.40.refs_2_), channel_id=1, source_target_pairs={{0,16},{16,0},{1,17},{17,1},{2,18},{18,2},{3,19},{19,3},{4,20},{20... | collective-permute-start | bytes 3686408 | tf_op jit(solution)/shard_map/ppermute | solution.py:21
  335.1 29.8 %collective-permute-start.35 = (bf16[192,2560]{1,0:T(8,128)(2,1)}, bf16[192,2560]{1,0:T(8,128)(2,1)}, u32[]{:S(2)}, u32[]{:S(2)}) collective-permute-start(bf16[192,2560]{1,0:T(8,128)(2,1)} %collective-permute-done.34), channel_id=1, source_target_pairs={{2,3},{6,7},{10,11},{14,15},{18,19},{22,23},{26,27},{30,31}} | collective-permute-start | bytes 2949128 | tf_op jit(solution)/shard_map/ppermute | solution.py:127
  456.6 56.2 %collective-permute-start.67 = (bf16[192,2560]{1,0:T(8,128)(2,1)}, bf16[192,2560]{1,0:T(8,128)(2,1)}, u32[]{:S(2)}, u32[]{:S(2)}) collective-permute-start(bf16[192,2560]{1,0:T(8,128)(2,1)} %get-tuple-element.122), channel_id=1, source_target_pairs={{0,1},{4,5},{8,9},{12,13},{16,17},{20,21},{24,25},{28,29}} | collective-permute-start | bytes 2949128 | tf_op jit(solution)/shard_map/ppermute | solution.py:114
  462.8 72.2 %collective-permute-start.70 = (bf16[192,2560]{1,0:T(8,128)(2,1)}, bf16[192,2560]{1,0:T(8,128)(2,1)}, u32[]{:S(2)}, u32[]{:S(2)}) collective-permute-start(bf16[192,2560]{1,0:T(8,128)(2,1)} %get-tuple-element.123), channel_id=1, source_target_pairs={{3,2},{7,6},{11,10},{15,14},{19,18},{23,22},{27,26},{31,30}} | collective-permute-start | bytes 2949128 | tf_op jit(solution)/shard_map/ppermute | solution.py:117
  479.4 35.9 %collective-permute-start.82 = (bf16[192,2560]{1,0:T(8,128)(2,1)}, bf16[192,2560]{1,0:T(8,128)(2,1)}, u32[]{:S(2)}, u32[]{:S(2)}) collective-permute-start(bf16[192,2560]{1,0:T(8,128)(2,1)} %get-tuple-element.119), channel_id=1, source_target_pairs={{3,2},{7,6},{11,10},{15,14},{19,18},{23,22},{27,26},{31,30}} | collective-permute-start | bytes 2949128 | tf_op jit(solution)/shard_map/ppermute | solution.py:117
  489.4 144.7 %collective-permute-start.136 = (bf16[1280,1280]{1,0:T(8,128)(2,1)}, bf16[1280,1280]{1,0:T(8,128)(2,1)}, u32[]{:S(2)}, u32[]{:S(2)}) collective-permute-start(bf16[1280,1280]{1,0:T(8,128)(2,1)} %pad_maximum_fusion.11), channel_id=1, source_target_pairs={{0,4},{4,0},{8,12},{12,8},{1,5},{5,1},{9,13},{13,9},{2,6},{6,2},{1... | collective-permute-start | bytes 9830408 | tf_op jit(solution)/shard_map/ppermute | solution.py:21
  512.8 143.8 %collective-permute-start.130 = (bf16[1280,1920]{1,0:T(8,128)(2,1)}, bf16[1280,1920]{1,0:T(8,128)(2,1)}, u32[]{:S(2)}, u32[]{:S(2)}) collective-permute-start(bf16[1280,1920]{1,0:T(8,128)(2,1)} %pad_maximum_fusion.6), channel_id=1, source_target_pairs={{0,4},{4,0},{8,12},{12,8},{1,5},{5,1},{9,13},{13,9},{2,6},{6,2},{1... | collective-permute-start | bytes 14745608 | tf_op jit(solution)/shard_map/ppermute | solution.py:21
  515.3 36.2 %collective-permute-start.68 = (bf16[192,2560]{1,0:T(8,128)(2,1)S(1)}, bf16[192,2560]{1,0:T(8,128)(2,1)S(1)}, u32[]{:S(2)}, u32[]{:S(2)}) collective-permute-start(bf16[192,2560]{1,0:T(8,128)(2,1)S(1)} %add_convert_fusion.18), channel_id=1, source_target_pairs={{0,1},{1,2},{4,5},{5,6},{8,9},{9,10},{12,13},{13,14},{16,17},{17,1... | collective-permute-start | bytes 2949128 | tf_op jit(solution)/shard_map/ppermute | solution.py:114
  565.3 130.0 %collective-permute-start.127 = (bf16[1280,1920]{1,0:T(8,128)(2,1)}, bf16[1280,1920]{1,0:T(8,128)(2,1)}, u32[]{:S(2)}, u32[]{:S(2)}) collective-permute-start(bf16[1280,1920]{1,0:T(8,128)(2,1)} %pad_maximum_fusion.5), channel_id=1, source_target_pairs={{0,4},{4,0},{8,12},{12,8},{1,5},{5,1},{9,13},{13,9},{2,6},{6,2},{1... | collective-permute-start | bytes 14745608 | tf_op jit(solution)/shard_map/ppermute | solution.py:21
  587.4 36.1 %collective-permute-start.72 = (bf16[192,2560]{1,0:T(8,128)(2,1)}, bf16[192,2560]{1,0:T(8,128)(2,1)}, u32[]{:S(2)}, u32[]{:S(2)}) collective-permute-start(bf16[192,2560]{1,0:T(8,128)(2,1)} %add_convert_fusion.15), channel_id=1, source_target_pairs={{1,0},{2,1},{3,2},{5,4},{6,5},{7,6},{9,8},{10,9},{11,10},{13,12},{... | collective-permute-start | bytes 2949128 | tf_op jit(solution)/shard_map/ppermute | solution.py:117
  637.7 54.3 %collective-permute-start.137 = (bf16[640,1280]{1,0:T(8,128)(2,1)}, bf16[640,1280]{1,0:T(8,128)(2,1)}, u32[]{:S(2)}, u32[]{:S(2)}) collective-permute-start(bf16[640,1280]{1,0:T(8,128)(2,1)} %pad_maximum_fusion.18), channel_id=1, source_target_pairs={{0,8},{4,12},{8,0},{12,4},{1,9},{5,13},{9,1},{13,5},{2,10},{6,14},... | collective-permute-start | bytes 4915208 | tf_op jit(solution)/shard_map/ppermute | solution.py:21
  656.6 33.8 %collective-permute-start.76 = (bf16[192,2560]{1,0:T(8,128)(2,1)}, bf16[192,2560]{1,0:T(8,128)(2,1)}, u32[]{:S(2)}, u32[]{:S(2)}) collective-permute-start(bf16[192,2560]{1,0:T(8,128)(2,1)} %get-tuple-element.160), channel_id=1, source_target_pairs={{1,0},{2,1},{3,2},{5,4},{6,5},{7,6},{9,8},{10,9},{11,10},{13,12},{... | collective-permute-start | bytes 2949128 | tf_op jit(solution)/shard_map/ppermute | solution.py:130
  669.3 30.4 %collective-permute-start.86 = (bf16[192,2560]{1,0:T(8,128)(2,1)}, bf16[192,2560]{1,0:T(8,128)(2,1)S(1)}, u32[]{:S(2)}, u32[]{:S(2)}) collective-permute-start(bf16[192,2560]{1,0:T(8,128)(2,1)} %collective-permute-done.85), channel_id=1, source_target_pairs={{1,2},{2,3},{5,6},{6,7},{9,10},{10,11},{13,14},{14,15},{17,18},{18... | collective-permute-start | bytes 2949128 | tf_op jit(solution)/shard_map/ppermute | solution.py:127
  672.9 38.4 %collective-permute-start.89 = (bf16[192,2560]{1,0:T(8,128)(2,1)}, bf16[192,2560]{1,0:T(8,128)(2,1)S(1)}, u32[]{:S(2)}, u32[]{:S(2)}) collective-permute-start(bf16[192,2560]{1,0:T(8,128)(2,1)} %collective-permute-done.88), channel_id=1, source_target_pairs={{1,0},{2,1},{5,4},{6,5},{9,8},{10,9},{13,12},{14,13},{17,16},{18,1... | collective-permute-start | bytes 2949128 | tf_op jit(solution)/shard_map/ppermute | solution.py:130
  692.0 40.5 %collective-permute-start.77 = (bf16[192,2560]{1,0:T(8,128)(2,1)}, bf16[192,2560]{1,0:T(8,128)(2,1)}, u32[]{:S(2)}, u32[]{:S(2)}) collective-permute-start(bf16[192,2560]{1,0:T(8,128)(2,1)} %collective-permute-done.76), channel_id=1, source_target_pairs={{1,0},{2,1},{5,4},{6,5},{9,8},{10,9},{13,12},{14,13},{17,16},{18,1... | collective-permute-start | bytes 2949128 | tf_op jit(solution)/shard_map/ppermute | solution.py:130
  699.8 34.4 %collective-permute-start.87 = (bf16[192,2560]{1,0:T(8,128)(2,1)S(1)}, bf16[192,2560]{1,0:T(8,128)(2,1)S(1)}, u32[]{:S(2)}, u32[]{:S(2)}) collective-permute-start(bf16[192,2560]{1,0:T(8,128)(2,1)S(1)} %collective-permute-done.86), channel_id=1, source_target_pairs={{2,3},{6,7},{10,11},{14,15},{18,19},{22,23},{26,27},{30,31}} | collective-permute-start | bytes 2949128 | tf_op jit(solution)/shard_map/ppermute | solution.py:127
  711.4 42.1 %collective-permute-start.90 = (bf16[192,2560]{1,0:T(8,128)(2,1)S(1)}, bf16[192,2560]{1,0:T(8,128)(2,1)S(1)}, u32[]{:S(2)}, u32[]{:S(2)}) collective-permute-start(bf16[192,2560]{1,0:T(8,128)(2,1)S(1)} %collective-permute-done.89), channel_id=1, source_target_pairs={{1,0},{5,4},{9,8},{13,12},{17,16},{21,20},{25,24},{29,28}} | collective-permute-start | bytes 2949128 | tf_op jit(solution)/shard_map/ppermute | solution.py:130
  715.9 211.8 %collective-permute-start.133 = (bf16[1280,640]{1,0:T(8,128)(2,1)}, bf16[1280,640]{1,0:T(8,128)(2,1)}, u32[]{:S(2)}, u32[]{:S(2)}) collective-permute-start(bf16[1280,640]{1,0:T(8,128)(2,1)} %pad_maximum_fusion.17), channel_id=1, source_target_pairs={{0,4},{4,0},{8,12},{12,8},{1,5},{5,1},{9,13},{13,9},{2,6},{6,2},{1... | collective-permute-start | bytes 4915208 | tf_op jit(solution)/shard_map/ppermute | solution.py:21
  719.1 172.5 %collective-permute-start.131 = (bf16[640,1920]{1,0:T(8,128)(2,1)}, bf16[640,1920]{1,0:T(8,128)(2,1)}, u32[]{:S(2)}, u32[]{:S(2)}) collective-permute-start(bf16[640,1920]{1,0:T(8,128)(2,1)} %pad_maximum_fusion.13), channel_id=1, source_target_pairs={{0,8},{4,12},{8,0},{12,4},{1,9},{5,13},{9,1},{13,5},{2,10},{6,14},... | collective-permute-start | bytes 7372808 | tf_op jit(solution)/shard_map/ppermute | solution.py:21
  732.5 49.8 %collective-permute-start.75 = (bf16[192,2560]{1,0:T(8,128)(2,1)}, bf16[192,2560]{1,0:T(8,128)(2,1)}, u32[]{:S(2)}, u32[]{:S(2)}) collective-permute-start(bf16[192,2560]{1,0:T(8,128)(2,1)} %collective-permute-done.74), channel_id=1, source_target_pairs={{2,3},{6,7},{10,11},{14,15},{18,19},{22,23},{26,27},{30,31}} | collective-permute-start | bytes 2949128 | tf_op jit(solution)/shard_map/ppermute | solution.py:127
  734.1 49.5 %collective-permute-start.78 = (bf16[192,2560]{1,0:T(8,128)(2,1)}, bf16[192,2560]{1,0:T(8,128)(2,1)}, u32[]{:S(2)}, u32[]{:S(2)}) collective-permute-start(bf16[192,2560]{1,0:T(8,128)(2,1)} %collective-permute-done.77), channel_id=1, source_target_pairs={{1,0},{5,4},{9,8},{13,12},{17,16},{21,20},{25,24},{29,28}} | collective-permute-start | bytes 2949128 | tf_op jit(solution)/shard_map/ppermute | solution.py:130
  792.0 105.7 %collective-permute-start.128 = (bf16[640,1920]{1,0:T(8,128)(2,1)}, bf16[640,1920]{1,0:T(8,128)(2,1)}, u32[]{:S(2)}, u32[]{:S(2)}) collective-permute-start(bf16[640,1920]{1,0:T(8,128)(2,1)} %pad_maximum_fusion.12), channel_id=1, source_target_pairs={{0,16},{16,0},{1,17},{17,1},{2,18},{18,2},{3,19},{19,3},{4,20},{20... | collective-permute-start | bytes 7372808 | tf_op jit(solution)/shard_map/ppermute | solution.py:21
  831.6 45.6 %collective-permute-start.121 = (bf16[256,640]{1,0:T(8,128)(2,1)}, bf16[256,640]{1,0:T(8,128)(2,1)}, u32[]{:S(2)}, u32[]{:S(2)}) collective-permute-start(bf16[256,640]{1,0:T(8,128)(2,1)} %pad_maximum_fusion.29), channel_id=1, source_target_pairs={{0,4},{4,0},{8,12},{12,8},{1,5},{5,1},{9,13},{13,9},{2,6},{6,2},{1... | collective-permute-start | bytes 983048 | tf_op jit(solution)/shard_map/ppermute | solution.py:21
  877.2 50.5 %collective-permute-start.115 = (bf16[1280,640]{1,0:T(8,128)(2,1)}, bf16[1280,640]{1,0:T(8,128)(2,1)}, u32[]{:S(2)}, u32[]{:S(2)}) collective-permute-start(bf16[1280,640]{1,0:T(8,128)(2,1)} %pad_maximum_fusion.14), channel_id=1, source_target_pairs={{0,4},{4,0},{8,12},{12,8},{1,5},{5,1},{9,13},{13,9},{2,6},{6,2},{1... | collective-permute-start | bytes 4915208 | tf_op jit(solution)/shard_map/ppermute | solution.py:21
  890.3 57.1 %collective-permute-start.124 = (bf16[1280,640]{1,0:T(8,128)(2,1)S(1)}, bf16[1280,640]{1,0:T(8,128)(2,1)}, u32[]{:S(2)}, u32[]{:S(2)}) collective-permute-start(bf16[1280,640]{1,0:T(8,128)(2,1)S(1)} %copy-done.98), channel_id=1, source_target_pairs={{0,4},{4,0},{8,12},{12,8},{1,5},{5,1},{9,13},{13,9},{2,6},{6,2},{1... | collective-permute-start | bytes 4915208 | tf_op jit(solution)/shard_map/ppermute | solution.py:21
  927.7 53.0 %collective-permute-start.118 = (bf16[1280,640]{1,0:T(8,128)(2,1)S(1)}, bf16[1280,640]{1,0:T(8,128)(2,1)S(1)}, u32[]{:S(2)}, u32[]{:S(2)}) collective-permute-start(bf16[1280,640]{1,0:T(8,128)(2,1)S(1)} %copy-done.99), channel_id=1, source_target_pairs={{0,4},{4,0},{8,12},{12,8},{1,5},{5,1},{9,13},{13,9},{2,6},{6,2},{1... | collective-permute-start | bytes 4915208 | tf_op jit(solution)/shard_map/ppermute | solution.py:21
  927.7 29.9 %collective-permute-start.132 = (bf16[320,1920]{1,0:T(8,128)(2,1)S(1)}, bf16[320,1920]{1,0:T(8,128)(2,1)S(1)}, u32[]{:S(2)}, u32[]{:S(2)}) collective-permute-start(bf16[320,1920]{1,0:T(8,128)(2,1)S(1)} %add_convert_fusion.1), channel_id=1, source_target_pairs={{0,16},{16,0},{1,17},{17,1},{2,18},{18,2},{3,19},{19,3},{4,20},{20... | collective-permute-start | bytes 3686408 | tf_op jit(solution)/shard_map/ppermute | solution.py:21
  931.1 43.9 %collective-permute-start.129 = (bf16[320,1920]{1,0:T(8,128)(2,1)S(1)}, bf16[320,1920]{1,0:T(8,128)(2,1)S(1)}, u32[]{:S(2)}, u32[]{:S(2)}) collective-permute-start(bf16[320,1920]{1,0:T(8,128)(2,1)S(1)} %add_convert_fusion.4), channel_id=1, source_target_pairs={{0,8},{4,12},{8,0},{12,4},{1,9},{5,13},{9,1},{13,5},{2,10},{6,14},... | collective-permute-start | bytes 3686408 | tf_op jit(solution)/shard_map/ppermute | solution.py:21
  945.4 56.0 %collective-permute-start.134 = (bf16[640,640]{1,0:T(8,128)(2,1)S(1)}, bf16[640,640]{1,0:T(8,128)(2,1)S(1)}, u32[]{:S(2)}, u32[]{:S(2)}) collective-permute-start(bf16[640,640]{1,0:T(8,128)(2,1)S(1)} %pad_maximum_fusion.23), channel_id=1, source_target_pairs={{0,16},{16,0},{1,17},{17,1},{2,18},{18,2},{3,19},{19,3},{4,20},{20... | collective-permute-start | bytes 2457608 | tf_op jit(solution)/shard_map/ppermute | solution.py:21
  957.6 46.3 %collective-permute-start.125 = (bf16[640,640]{1,0:T(8,128)(2,1)S(1)}, bf16[640,640]{1,0:T(8,128)(2,1)S(1)}, u32[]{:S(2)}, u32[]{:S(2)}) collective-permute-start(bf16[640,640]{1,0:T(8,128)(2,1)S(1)} %pad_maximum_fusion.22), channel_id=1, source_target_pairs={{0,16},{16,0},{1,17},{17,1},{2,18},{18,2},{3,19},{19,3},{4,20},{20... | collective-permute-start | bytes 2457608 | tf_op jit(solution)/shard_map/ppermute | solution.py:21
  998.6 31.3 %collective-permute-start.104 = (bf16[192,2560]{1,0:T(8,128)(2,1)S(1)}, bf16[192,2560]{1,0:T(8,128)(2,1)S(1)}, u32[]{:S(2)}, u32[]{:S(2)}) collective-permute-start(bf16[192,2560]{1,0:T(8,128)(2,1)S(1)} %fusion.11), channel_id=1, source_target_pairs={{0,1},{1,2},{2,3},{4,5},{5,6},{6,7},{8,9},{9,10},{10,11},{12,13},{... | collective-permute-start | bytes 2949128 | tf_op jit(solution)/shard_map/ppermute | solution.py:127
  1003.9 32.7 %collective-permute-start.135 = (bf16[320,640]{1,0:T(8,128)(2,1)S(1)}, bf16[320,640]{1,0:T(8,128)(2,1)S(1)}, u32[]{:S(2)}, u32[]{:S(2)}) collective-permute-start(bf16[320,640]{1,0:T(8,128)(2,1)S(1)} %add_convert_fusion.26), channel_id=1, source_target_pairs={{0,8},{4,12},{8,0},{12,4},{1,9},{5,13},{9,1},{13,5},{2,10},{6,14},... | collective-permute-start | bytes 1228808 | tf_op jit(solution)/shard_map/ppermute | solution.py:21
  1029.9 30.4 %collective-permute-start.120 = (bf16[320,640]{1,0:T(8,128)(2,1)S(1)}, bf16[320,640]{1,0:T(8,128)(2,1)S(1)}, u32[]{:S(2)}, u32[]{:S(2)}) collective-permute-start(bf16[320,640]{1,0:T(8,128)(2,1)S(1)} %add_convert_fusion.32), channel_id=1, source_target_pairs={{0,16},{16,0},{1,17},{17,1},{2,18},{18,2},{3,19},{19,3},{4,20},{20... | collective-permute-start | bytes 1228808 | tf_op jit(solution)/shard_map/ppermute | solution.py:21
  (224 other events, 3334.3 us)

commit v2 on v1

v2 whole, which is shorter than its diff:
```python
from functools import partial

import jax
import jax.numpy as jnp
from jax import lax
from jax.experimental import pallas as pl
from jax.experimental.pallas import tpu as pltpu
from jax.sharding import PartitionSpec as P

BLOCK = 256
HALF = BLOCK // 2
ROWS = 192
MIB = 1024 * 1024
VMEM_MIB = 60
F32 = jnp.float32
BF16 = jnp.bfloat16


def flip(value, position):
    ctx_bits = lax.axis_size("ctx").bit_length() - 1
    axis, bit = ("ctx", position) if position < ctx_bits else ("fsdp", position - ctx_bits)
    return lax.ppermute(value, axis, [(i, i ^ (1 << bit)) for i in range(lax.axis_size(axis))])


def partner(value, bit=0):
    return lax.ppermute(value, "tp", [(i, i ^ (1 << bit)) for i in range(lax.axis_size("tp"))])


def cube_bits():
    return (lax.axis_size("fsdp") * lax.axis_size("ctx")).bit_length() - 1


def cube_index():
    return lax.axis_index("fsdp") * lax.axis_size("ctx") + lax.axis_index("ctx")


def slow_order(backward):
    order = list(range(1, cube_bits()))
    return order[::-1] if backward else order


def leap(value, mask):
    count = 1 << cube_bits()
    return lax.ppermute(value, ("fsdp", "ctx"), [(i, i ^ mask) for i in range(count)])


class Later:
    def __init__(self, value):
        self.value = value


class Windows:
    def __init__(self):
        self.live = []
        self.event = None

    def now(self, value):
        if self.event is None:
            return value
        return jax.tree.map(lambda one: lax.optimization_barrier((one, self.event))[0], value)

    def lead(self, values):
        values = lax.optimization_barrier(tuple(values))
        self.event = values[0]
        return values

    def step(self, *works):
        works = [work if isinstance(work, tuple) else (0, work) for work in works]
        self.live = sorted(self.live + [(*work, None) for work in works], key=lambda one: one[0])
        waiting = []
        for rank, work, value in self.live:
            if isinstance(value, Later):
                waiting.append((rank, work, value.value))
                continue
            try:
                if rank > 1 and value is not None:
                    value = self.now(value)
                waiting.append((rank, work, work.send(value)))
            except StopIteration:
                pass
        flown = [isinstance(value, Later) for _, _, value in waiting]
        leaves, tree = jax.tree.flatten([v for (_, _, v), late in zip(waiting, flown) if not late])
        if leaves:
            leaves = lax.optimization_barrier(tuple(leaves))
            self.event = min(leaves, key=lambda leaf: leaf.size)
        values = iter(jax.tree.unflatten(tree, leaves))
        self.live = [
            (rank, work, value if late else next(values))
            for (rank, work, value), late in zip(waiting, flown)
        ]


def together(*works):
    pairs = [(work, None) for work in works]
    while True:
        found = []
        for work, value in pairs:
            try:
                found.append((work, work.send(value)))
            except StopIteration:
                pass
        if not found:
            return
        late = any(isinstance(value, Later) for _, value in found)
        plain = [value.value if isinstance(value, Later) else value for _, value in found]
        values = yield Later(plain) if late else plain
        pairs = [(work, value) for (work, _), value in zip(found, values)]


def gather(kept, name, shard, backward, floating=False):
    pieces = fresh = {0: shard}
    done = {}
    for number, position in enumerate(slow_order(backward)):
        found = {mask | 1 << position: flip(piece, position) for mask, piece in pieces.items()}
        near = {mask | 1: flip(piece, 0) for mask, piece in fresh.items()}
        found, near = yield Later((found, near)) if floating and number else (found, near)
        if floating and number == 0:
            yield ()
        pieces, fresh = {**pieces, **found}, found
        done.update(near)
    near = yield {mask | 1: flip(piece, 0) for mask, piece in fresh.items()}
    pieces.update(done)
    pieces.update(near)
    kept[name] = assemble([pieces[mask] for mask in sorted(pieces)])


def gather_direct(kept, name, shard, floating=False):
    count = 1 << cube_bits()
    flying = {mask: leap(shard, mask) for mask in range(2, count, 2)}, flip(shard, 0)
    pieces, near = yield Later(flying) if floating else flying
    far = {mask | 1: flip(piece, 0) for mask, piece in pieces.items()}
    if not floating:
        far = yield far
    pieces = {**pieces, **far, 0: shard, 1: near}
    kept[name] = assemble([pieces[mask] for mask in sorted(pieces)])


def assemble(pieces):
    count, (rows, columns) = len(pieces), pieces[0].shape

    def kernel(me_ref, *refs):
        sources, target, sems = refs[:count], refs[count], refs[count + 1]
        copies = []
        for mask in range(count):
            start = pl.multiple_of((me_ref[0] ^ mask) * rows, 16)
            copies.append(
                pltpu.make_async_copy(sources[mask], target.at[pl.ds(start, rows)], sems.at[mask])
            )
        for copy in copies:
            copy.start()
        for copy in copies:
            copy.wait()

    return pl.pallas_call(
        kernel,
        in_specs=[pl.BlockSpec(memory_space=pltpu.SMEM)]
        + [pl.BlockSpec(memory_space=pl.ANY)] * count,
        out_specs=pl.BlockSpec(memory_space=pltpu.VMEM),
        out_shape=jax.ShapeDtypeStruct((count * rows, columns), pieces[0].dtype),
        scratch_shapes=[pltpu.SemaphoreType.DMA((count,))],
        compiler_params=pltpu.CompilerParams(vmem_limit_bytes=VMEM_MIB * MIB),
        cost_estimate=pl.CostEstimate(
            flops=0, bytes_accessed=4 * count * rows * columns, transcendentals=0
        ),
        name="assemble",
    )(cube_index().astype(jnp.int32).reshape(1), *pieces)


def scatter_masks(backward):
    order = slow_order(backward)[::-1]
    top = len(order) - 1
    return order, [
        sum(1 << position for n, position in enumerate(order) if number >> (top - n) & 1)
        for number in range(1 << len(order))
    ]


def scatter(kept, name, sent, held, backward, floating=0):
    order, _ = scatter_masks(backward)
    arrived = flip(sent, 0)
    if floating < 2:
        arrived = yield arrived
    for number, position in enumerate(order):
        half = held.shape[0] // 2
        outgoing = held[half:].astype(F32) + arrived[half:].astype(F32)
        held = held[:half].astype(F32) + arrived[:half].astype(F32)
        arrived = flip(outgoing.astype(BF16), position)
        arrived = yield Later(arrived) if floating and number == 0 else arrived
    kept[name] = held.astype(F32) + arrived.astype(F32)


def line_sum(win, partial_sums):
    count, mine = lax.axis_size("tp"), lax.axis_index("tp")
    rows = partial_sums.shape[0] // count

    def chunk(number):
        start = jnp.clip(number, 0, count - 1) * rows
        return lax.dynamic_slice_in_dim(partial_sums, start, rows).astype(F32)

    from_left = from_right = None
    for step in range(1, count):
        rightward = chunk(mine + count - step)
        leftward = chunk(mine - count + step)
        if step > 1:
            rightward = rightward + from_left.astype(F32)
            leftward = leftward + from_right.astype(F32)
        rightward, leftward = win.lead((rightward.astype(BF16), leftward.astype(BF16)))
        from_left = lax.ppermute(
            rightward, "tp", [(s, s + 1) for s in range(min(step, count - 1))]
        )
        from_right = lax.ppermute(
            leftward, "tp", [(s, s - 1) for s in range(max(count - step, 1), count)]
        )
        from_left, from_right = yield from_left, from_right
    return chunk(mine) + from_left.astype(F32) + from_right.astype(F32)


def line_gather(win, share):
    count, mine = lax.axis_size("tp"), lax.axis_index("tp")
    left, right = {0: share}, {0: share}
    for step in range(1, count):
        rightward, leftward = win.lead((left[step - 1], right[step - 1]))
        left[step], right[step] = yield (
            lax.ppermute(rightward, "tp", [(s, s + 1) for s in range(step - 1, count - 1)]),
            lax.ppermute(leftward, "tp", [(s, s - 1) for s in range(1, count - step + 1)]),
        )
    return in_line(left, right)


def in_line(left, right):
    count, mine = lax.axis_size("tp"), lax.axis_index("tp")
    parts = []
    for number in range(count):
        choice = left[count - 1 - number]
        for place in range(count - 2, -1, -1):
            here = left[place - number] if place >= number else right[number - place]
            choice = jnp.where(mine == place, here, choice)
        parts.append(choice)
    return parts


def shifted(value, steps):
    count = lax.axis_size("ctx")
    pairs = [(s, s + steps) for s in range(count) if 0 <= s + steps < count]
    return lax.ppermute(value, "ctx", pairs)


def carried(ends, backward):
    sign = -1 if backward else 1
    pairs = [
        shifted(ends, sign * distance) for distance in range(lax.axis_size("ctx") - 1, 0, -1)
    ]
    state = pairs[0][1]
    for pair in pairs[1:]:
        state = pair[1] + pair[0] * state
    return jnp.broadcast_to(state[None], ends.shape)


def since_start(info_ref, row):
    place = info_ref[3] + row + lax.broadcasted_iota(jnp.int32, (8, 128), 0)
    begin = jnp.zeros((8, 128), jnp.int32)
    for j in range(3):
        begin = jnp.where(place >= info_ref[j], info_ref[j], begin)
    return place - begin


def wide(tile, columns):
    return jnp.concatenate([tile] * (columns // 128), axis=1)


def rows_of(columns):
    return lax.broadcasted_iota(jnp.int32, (8, columns), 0)


def moved(tile, other, steps, row):
    both = pltpu.roll(tile, steps % 8, 0), pltpu.roll(other, steps % 8, 0)
    inside = (row >= steps) if steps > 0 else (row < 8 + steps)
    return jnp.where(inside, *both)


def one_less_exp(value, half_exp):
    series = jnp.ones_like(value)
    for n in range(8, 1, -1):
        series = 1.0 + value * (1.0 / n) * series
    return jnp.where(value > -0.5, -value * series, 1.0 - half_exp * half_exp)


def sigmoid(value):
    return 1.0 / (1.0 + jnp.exp(-value))


def gelu_both(value):
    c = 0.7978845608028654
    square = value * value
    bent = jnp.tanh(c * value * (1.0 + 0.044715 * square))
    half = 0.5 * (1.0 + bent)
    slope = half + 0.5 * value * (1.0 - bent * bent) * c * (1.0 + 3 * 0.044715 * square)
    return value * half, slope


def dot(a, b):
    return jnp.dot(a, b, preferred_element_type=F32)


def dot_nt(a, b):
    return lax.dot_general(a, b, (((1,), (1,)), ((), ())), preferred_element_type=F32)


def dot_tn(a, b):
    return lax.dot_general(a, b, (((0,), (0,)), ((), ())), preferred_element_type=F32)


def const_spec(shape):
    return pl.BlockSpec(shape, lambda i: (0,) * len(shape), pipeline_mode=pl.Buffered(1))


def row_spec(columns):
    return pl.BlockSpec((ROWS, columns), lambda i: (i, 0))


SMEM_SPEC = pl.BlockSpec(memory_space=pltpu.SMEM)


def params():
    return pltpu.CompilerParams(
        dimension_semantics=("arbitrary",), vmem_limit_bytes=VMEM_MIB * MIB
    )


def recur_forward(info, branch, extra, taps, gates_in, gates_decay, vectors):
    channels = branch.shape[1]
    reach = channels + HALF
    lead = branch.shape[0] % ROWS
    tokens = branch.shape[0] - lead
    tiles = ROWS // 8

    def kernel(
        info_ref, branch_ref, extra_ref, taps_ref, gin_ref, gdec_ref, vec_ref,
        conv_ref, low_ref, pre_in_ref, pre_dec_ref, decay_ref, prod_ref, state_ref, ends_ref,
        conv, carry_p, carry_s,
    ):
        i = pl.program_id(0)

        @pl.when(i == 0)
        def _():
            carry_p[...] = jnp.ones_like(carry_p)
            carry_s[...] = jnp.zeros_like(carry_s)

        row = rows_of(channels)

        def conv_part(source, begin, width):
            row_part = rows_of(width)
            columns = slice(begin, begin + width)

            def tile(t, _):
                base = pl.multiple_of(t * 8, 8)
                place = pl.multiple_of(lead + i * ROWS + base, 8)
                since = since_start(info_ref, i * ROWS + base)
                current = source[pl.ds(place, 8), :]
                before = source[pl.ds(pl.multiple_of(place - 8, 8), 8), :]
                total = taps_ref[4:5, columns] + taps_ref[0:1, columns] * current
                for k in range(1, 4):
                    earlier = moved(current, before, k, row_part)
                    total = total + taps_ref[k : k + 1, columns] * jnp.where(
                        wide(since >= k, width), earlier, 0.0
                    )
                conv[pl.ds(base, 8), columns] = total
                return 0

            lax.fori_loop(0, tiles, tile, 0, unroll=4)

        conv_part(branch_ref, 0, channels)
        conv_part(extra_ref, channels, HALF)
        conv_ref[...] = conv[:, :channels]
        low = conv[...].astype(BF16)
        low_ref[...] = low
        for begin in range(0, channels, BLOCK):
            end = min(begin + BLOCK, channels)
            part = low[:, begin : begin + BLOCK]
            pre_in_ref[:, begin:end] = dot(part, gin_ref[:, begin:end]) + vec_ref[0:1, begin:end]
            pre_dec_ref[:, begin:end] = dot(part, gdec_ref[:, begin:end]) + vec_ref[1:2, begin:end]

        def scan_tile(t, carry):
            base = pl.multiple_of(t * 8, 8)
            at = pl.ds(base, 8)
            start = wide(since_start(info_ref, i * ROWS + base) == 0, channels)
            log_decay = sigmoid(pre_dec_ref[at, :]) * vec_ref[2:3, :]
            decay = jnp.exp(log_decay)
            scale = jnp.sqrt(one_less_exp(2.0 * log_decay, decay))
            a = jnp.where(start, 0.0, decay)
            b = conv_ref[at, :] * sigmoid(pre_in_ref[at, :]) * jnp.where(start, 1.0, scale)
            decay_ref[at, :] = a
            for s in (1, 2, 4):
                inside = row >= s
                b = b + a * jnp.where(inside, pltpu.roll(b, s, 0), 0.0)
                a = a * jnp.where(inside, pltpu.roll(a, s, 0), 1.0)
            b = b + a * carry[1]
            a = a * carry[0]
            prod_ref[at, :] = a
            state_ref[at, :] = b
            return (
                jnp.broadcast_to(a[7:8, :], a.shape),
                jnp.broadcast_to(b[7:8, :], b.shape),
            )

        last = lax.fori_loop(0, tiles, scan_tile, (carry_p[...], carry_s[...]), unroll=4)
        carry_p[...] = last[0]
        carry_s[...] = last[1]
        ends_ref[...] = jnp.where(row == 0, last[0], last[1])

    narrow = jax.ShapeDtypeStruct((tokens, channels), F32)
    return pl.pallas_call(
        kernel,
        grid=(tokens // ROWS,),
        in_specs=[
            SMEM_SPEC,
            const_spec(branch.shape),
            const_spec(extra.shape),
            const_spec((8, reach)),
            const_spec((BLOCK, channels)),
            const_spec((BLOCK, channels)),
            const_spec((8, channels)),
        ],
        out_specs=[row_spec(channels), row_spec(reach)]
        + [row_spec(channels)] * 5
        + [pl.BlockSpec((8, channels), lambda i: (0, 0))],
        out_shape=[narrow, jax.ShapeDtypeStruct((tokens, reach), BF16)]
        + [narrow] * 5
        + [jax.ShapeDtypeStruct((8, channels), F32)],
        scratch_shapes=[
            pltpu.VMEM((ROWS, reach), F32),
            pltpu.VMEM((8, channels), F32),
            pltpu.VMEM((8, channels), F32),
        ],
        compiler_params=params(),
        cost_estimate=pl.CostEstimate(
            flops=4 * tokens * BLOCK * channels + 150 * tokens * channels,
            bytes_accessed=20 * MIB,
            transcendentals=6 * tokens * channels,
        ),
        name="recur_forward",
    )(info, branch, extra, taps, gates_in, gates_decay, vectors)


def mix_forward(prod, state, gate_pre, arriving):
    tokens, channels = prod.shape

    def kernel(prod_ref, state_ref, gate_ref, arr_ref, states_ref, mixed_ref):
        states = state_ref[...] + prod_ref[...] * arr_ref[0:1, :]
        states_ref[...] = states
        mixed_ref[...] = (states * gelu_both(gate_ref[...])[0]).astype(BF16)

    return pl.pallas_call(
        kernel,
        grid=(tokens // ROWS,),
        in_specs=[row_spec(channels)] * 3 + [const_spec((8, channels))],
        out_specs=[row_spec(channels)] * 2,
        out_shape=[
            jax.ShapeDtypeStruct((tokens, channels), F32),
            jax.ShapeDtypeStruct((tokens, channels), BF16),
        ],
        compiler_params=params(),
        cost_estimate=pl.CostEstimate(
            flops=20 * tokens * channels,
            bytes_accessed=9 * MIB,
            transcendentals=tokens * channels,
        ),
        name="mix_forward",
    )(prod, state, gate_pre, arriving)


def mix_product(mixed, out_ws, residual):
    many, wides = len(mixed), len(out_ws)
    each = many // wides
    tokens, channels = mixed[0].shape
    width = out_ws[0].shape[0]
    cut = 512

    def kernel(*refs):
        out_refs = refs[many : many + wides]
        res_ref, middle_ref = refs[many + wides :]
        total = res_ref[...].astype(F32)
        for n in range(many):
            begin = n % each * channels
            total = total + dot_nt(refs[n][...], out_refs[n // each][:, begin : begin + channels])
        middle_ref[...] = total

    columns = pl.BlockSpec((tokens, cut), lambda i: (0, i))
    return pl.pallas_call(
        kernel,
        grid=(width // cut,),
        in_specs=[const_spec((tokens, channels))] * many
        + [pl.BlockSpec((cut, each * channels), lambda i: (i, 0))] * wides
        + [columns],
        out_specs=columns,
        out_shape=jax.ShapeDtypeStruct((tokens, width), F32),
        compiler_params=params(),
        cost_estimate=pl.CostEstimate(
            flops=2 * many * tokens * width * channels,
            bytes_accessed=30 * MIB,
            transcendentals=0,
        ),
        name="mix_product",
    )(*mixed, *out_ws, residual)


def mix_backward(mixed_cot, gate_pre, states, decays):
    tokens, channels = states.shape
    tiles = ROWS // 8
    steps = tokens // ROWS

    def kernel(
        mixed_ref, gate_ref, states_ref, decay_ref,
        cot_ref, prod_ref, state_ref, ends_ref,
        gate_cot, carry_p, carry_s, next_decay,
    ):
        i = pl.program_id(0)

        @pl.when(i == 0)
        def _():
            carry_p[...] = jnp.ones_like(carry_p)
            carry_s[...] = jnp.zeros_like(carry_s)
            next_decay[...] = jnp.ones_like(next_decay)

        gate_cot[...] = mixed_ref[...].astype(F32)
        row = rows_of(channels)

        def tile(t, carry):
            base = pl.multiple_of((tiles - 1 - t) * 8, 8)
            at = pl.ds(base, 8)
            value, slope = gelu_both(gate_ref[at, :])
            cot = gate_cot[at, :]
            gate_cot[at, :] = cot * states_ref[at, :] * slope
            decay = decay_ref[at, :]
            a = moved(decay, carry[2], -1, row)
            b = cot * value
            for s in (1, 2, 4):
                inside = row < 8 - s
                b = b + a * jnp.where(inside, pltpu.roll(b, 8 - s, 0), 0.0)
                a = a * jnp.where(inside, pltpu.roll(a, 8 - s, 0), 1.0)
            b = b + a * carry[1]
            a = a * carry[0]
            prod_ref[at, :] = a
            state_ref[at, :] = b
            return (
                jnp.broadcast_to(a[0:1, :], a.shape),
                jnp.broadcast_to(b[0:1, :], b.shape),
                decay,
            )

        last = lax.fori_loop(
            0, tiles, tile, (carry_p[...], carry_s[...], next_decay[...]), unroll=4
        )
        cot_ref[...] = gate_cot[...].astype(BF16)
        carry_p[...], carry_s[...], next_decay[...] = last
        ends_ref[...] = jnp.where(row == 0, last[0], last[1]) * jnp.broadcast_to(
            last[2][0:1, :], (8, channels)
        )

    back = pl.BlockSpec((ROWS, channels), lambda i: (steps - 1 - i, 0))
    return pl.pallas_call(
        kernel,
        grid=(steps,),
        in_specs=[back] * 4,
        out_specs=[back] * 3 + [pl.BlockSpec((8, channels), lambda i: (0, 0))],
        out_shape=[
            jax.ShapeDtypeStruct((tokens, channels), BF16),
            jax.ShapeDtypeStruct((tokens, channels), F32),
            jax.ShapeDtypeStruct((tokens, channels), F32),
            jax.ShapeDtypeStruct((8, channels), F32),
        ],
        scratch_shapes=[pltpu.VMEM((ROWS, channels), F32)] + [pltpu.VMEM((8, channels), F32)] * 3,
        compiler_params=params(),
        cost_estimate=pl.CostEstimate(
            flops=60 * tokens * channels,
            bytes_accessed=14 * MIB,
            transcendentals=tokens * channels,
        ),
        name="mix_backward",
    )(mixed_cot, gate_pre, states, decays)


def gates_backward(
    info, prod, state, returning, states, arriving, pre_in, pre_dec, conv, gates_in, gates_decay,
    vectors,
):
    tokens, channels = pre_in.shape
    steps = tokens // ROWS
    reach = channels + HALF
    tiles = ROWS // 8

    def kernel(
        info_ref, prod_ref, state_ref, ret_ref, states_ref, arr_ref, pre_in_ref, pre_dec_ref,
        conv_ref, gin_ref, gdec_ref, vec_ref,
        own_ref, going_ref, in_low_ref, dec_low_ref, sums_ref,
        in_cot, dec_cot, direct, previous,
    ):
        i = pl.program_id(0)

        @pl.when(i == 0)
        def _():
            previous[...] = arr_ref[...]
            sums_ref[...] = jnp.zeros_like(sums_ref)

        row = rows_of(channels)

        def tile(t, carry):
            base = pl.multiple_of(t * 8, 8)
            at = pl.ds(base, 8)
            before, sum_in, sum_dec, sum_par = carry
            start = wide(since_start(info_ref, i * ROWS + base) == 0, channels)
            adjoint = state_ref[at, :] + prod_ref[at, :] * ret_ref[0:1, :]
            here = states_ref[at, :]
            last = moved(here, before, 1, row)
            conv_out = conv_ref[at, :]
            gate = sigmoid(pre_in_ref[at, :])
            gate_dec = sigmoid(pre_dec_ref[at, :])
            log_decay = gate_dec * vec_ref[2:3, :]
            decay = jnp.exp(log_decay)
            rest = one_less_exp(2.0 * log_decay, decay)
            inverse = lax.rsqrt(rest)
            scale = jnp.where(start, 1.0, rest * inverse)
            with_conv = adjoint * conv_out
            dscale = with_conv * gate
            dlog = jnp.where(
                start, 0.0, decay * (adjoint * last - dscale * decay * inverse)
            )
            input_cot = dscale * scale * (1.0 - gate)
            shared = dlog * gate_dec
            decay_cot = shared * (1.0 - gate_dec) * vec_ref[2:3, :]
            direct[at, :] = adjoint * gate * scale
            in_cot[at, :] = input_cot
            dec_cot[at, :] = decay_cot
            return here, sum_in + input_cot, sum_dec + decay_cot, sum_par + shared

        zero = jnp.zeros((8, channels), F32)
        last = lax.fori_loop(0, tiles, tile, (previous[...], zero, zero, zero), unroll=2)
        previous[...] = last[0]
        for n in range(3):
            sums_ref[n * 8 : n * 8 + 8, :] += last[n + 1]
        in_low = in_cot[...].astype(BF16)
        dec_low = dec_cot[...].astype(BF16)
        in_low_ref[...] = in_low
        dec_low_ref[...] = dec_low
        for begin in range(0, channels, BLOCK):
            end = min(begin + BLOCK, channels)
            back = dot_nt(in_low[:, begin:end], gin_ref[:, begin:end]) + dot_nt(
                dec_low[:, begin:end], gdec_ref[:, begin:end]
            )
            own_ref[:, begin:end] = direct[:, begin:end] + back[:, : end - begin]
            if end - begin < BLOCK:
                going_ref[...] = back[:, end - begin :].astype(BF16)

    narrow = jax.ShapeDtypeStruct((tokens, channels), F32)
    low = jax.ShapeDtypeStruct((tokens, channels), BF16)
    return pl.pallas_call(
        kernel,
        grid=(steps,),
        in_specs=[
            SMEM_SPEC,
            row_spec(channels),
            row_spec(channels),
            const_spec((8, channels)),
            row_spec(channels),
            const_spec((8, channels)),
            row_spec(channels),
            row_spec(channels),
            row_spec(channels),
            const_spec((BLOCK, channels)),
            const_spec((BLOCK, channels)),
            const_spec((8, channels)),
        ],
        out_specs=[
            row_spec(channels),
            row_spec(reach - channels),
            row_spec(channels),
            row_spec(channels),
            pl.BlockSpec((24, channels), lambda i: (0, 0)),
        ],
        out_shape=[
            narrow, jax.ShapeDtypeStruct((tokens, reach - channels), BF16), low, low,
            jax.ShapeDtypeStruct((24, channels), F32),
        ],
        scratch_shapes=[pltpu.VMEM((ROWS, channels), F32)] * 3 + [pltpu.VMEM((8, channels), F32)],
        compiler_params=params(),
        cost_estimate=pl.CostEstimate(
            flops=4 * tokens * BLOCK * channels,
            bytes_accessed=20 * MIB,
            transcendentals=5 * tokens * channels,
        ),
        name="gates_backward",
    )(
        info, prod, state, returning, states, arriving, pre_in, pre_dec, conv, gates_in,
        gates_decay, vectors,
    )


def conv_backward(info, own, coming, trail, branch, taps):
    tokens, channels = own.shape
    tiles = ROWS // 8
    lead = branch.shape[0] - tokens
    borrowed = coming.shape[1]

    def kernel(
        info_ref, own_ref, coming_ref, trail_ref, branch_ref, taps_ref,
        low_ref, sums_ref,
        cot, branch_cot, before,
    ):
        i = pl.program_id(0)
        steps = pl.num_programs(0)

        @pl.when(i == 0)
        def _():
            sums_ref[...] = jnp.zeros_like(sums_ref)
            before[...] = trail_ref[...]

        @pl.when(i > 0)
        def _():
            before[...] = cot[0:8, :]

        cot[0:ROWS, :] = own_ref[...]
        cot[0:ROWS, channels - borrowed :] += coming_ref[...].astype(F32)
        cot[ROWS:, :] = before[...]
        row = rows_of(channels)

        def tile(t, carry):
            local = pl.multiple_of(t * 8, 8)
            begin = pl.multiple_of((steps - 1 - i) * ROWS + local, 8)
            since = since_start(info_ref, begin)
            since_next = since_start(info_ref, begin + 8)
            here, next_rows = cot[pl.ds(local, 8), :], cot[pl.ds(local + 8, 8), :]
            place = pl.multiple_of(lead + begin, 8)
            values = branch_ref[pl.ds(place, 8), :]
            last = branch_ref[pl.ds(pl.multiple_of(place - 8, 8), 8), :]
            total = taps_ref[0:1, :channels] * here
            sums = [carry[0] + here * values]
            for k in range(1, 4):
                near = jnp.where(wide(since >= k, channels), here, 0.0)
                far = jnp.where(wide(since_next >= k, channels), next_rows, 0.0)
                total = total + taps_ref[k : k + 1, :channels] * moved(near, far, -k, row)
                sums.append(carry[k] + near * moved(values, last, k, row))
            sums.append(carry[4] + here)
            branch_cot[pl.ds(local, 8), :] = total
            return tuple(sums)

        zero = jnp.zeros((8, channels), F32)
        last = lax.fori_loop(0, tiles, tile, (zero,) * 5, unroll=2)
        for n in range(5):
            sums_ref[n * 8 : n * 8 + 8, :] += last[n]
        low_ref[...] = branch_cot[...].astype(BF16)

    steps = tokens // ROWS

    def back(columns):
        return pl.BlockSpec((ROWS, columns), lambda i: (steps - 1 - i, 0))

    return pl.pallas_call(
        kernel,
        grid=(steps,),
        in_specs=[
            SMEM_SPEC,
            back(channels),
            back(borrowed),
            const_spec((8, channels)),
            const_spec(branch.shape),
            const_spec((8, taps.shape[1])),
        ],
        out_specs=[back(channels), pl.BlockSpec((40, channels), lambda i: (0, 0))],
        out_shape=[
            jax.ShapeDtypeStruct((tokens, channels), BF16),
            jax.ShapeDtypeStruct((40, channels), F32),
        ],
        scratch_shapes=[
            pltpu.VMEM((ROWS + 8, channels), F32),
            pltpu.VMEM((ROWS, channels), F32),
            pltpu.VMEM((8, channels), F32),
        ],
        compiler_params=params(),
        cost_estimate=pl.CostEstimate(
            flops=40 * tokens * channels, bytes_accessed=8 * MIB, transcendentals=0
        ),
        name="conv_backward",
    )(info, own, coming, trail, branch, taps)


def hidden_forward(normed, gate_w, value_w, hidden_cot):
    rows, width = normed.shape
    units = gate_w.shape[1]
    cut = 384

    def kernel(x_ref, gate_ref, value_ref, cot_ref, hidden_ref, gate_cot_ref, value_cot_ref):
        both = dot(x_ref[...], jnp.concatenate([gate_ref[...], value_ref[...]], axis=1))
        value, slope = gelu_both(both[:, :cut])
        other, cot = both[:, cut:], cot_ref[...]
        hidden_ref[...] = (value * other).astype(BF16)
        gate_cot_ref[...] = (cot * other * slope).astype(BF16)
        value_cot_ref[...] = (cot * value).astype(BF16)

    columns = pl.BlockSpec((rows, cut), lambda i: (0, i))
    return pl.pallas_call(
        kernel,
        grid=(units // cut,),
        in_specs=[
            const_spec((rows, width)),
            pl.BlockSpec((width, cut), lambda i: (0, i)),
            pl.BlockSpec((width, cut), lambda i: (0, i)),
            columns,
        ],
        out_specs=[columns] * 3,
        out_shape=[jax.ShapeDtypeStruct((rows, units), BF16)] * 3,
        compiler_params=params(),
        cost_estimate=pl.CostEstimate(
            flops=4 * rows * width * units,
            bytes_accessed=4 * width * units,
            transcendentals=rows * units,
        ),
        name="hidden_forward",
    )(normed, gate_w, value_w, hidden_cot)


def back_product(cots, weights):
    count = len(cots)
    width, columns = weights[0].shape
    rows = cots[0].shape[0]
    cut = 512

    def kernel(*refs):
        total = dot_nt(refs[0][...], refs[count][...])
        for n in range(1, count):
            total = total + dot_nt(refs[n][...], refs[count + n][...])
        refs[2 * count][...] = total.astype(BF16)

    return pl.pallas_call(
        kernel,
        grid=(width // cut,),
        in_specs=[const_spec((rows, columns))] * count
        + [pl.BlockSpec((cut, columns), lambda i: (i, 0))] * count,
        out_specs=pl.BlockSpec((rows, cut), lambda i: (0, i)),
        out_shape=jax.ShapeDtypeStruct((rows, width), BF16),
        compiler_params=params(),
        cost_estimate=pl.CostEstimate(
            flops=2 * count * rows * width * columns,
            bytes_accessed=2 * count * width * columns,
            transcendentals=0,
        ),
        name="back_product",
    )(*cots, *weights)


def grad_product(left, right, backward):
    tokens, width = left.shape
    columns = right.shape[1]
    _, masks = scatter_masks(backward)
    many = len(masks)
    rows = width // many // 2
    me = cube_index().astype(jnp.int32)
    if 2 * rows % 128:
        whole = dot_tn(left, right).astype(BF16)

        def laid(other):
            return jnp.concatenate(
                [
                    lax.dynamic_slice_in_dim(whole, (me ^ mask ^ other) * rows, rows)
                    for mask in masks
                ]
            )

        return laid(1), laid(0)

    def kernel(table_ref, left_ref, right_ref, sent_ref, held_ref):
        both = dot_tn(left_ref[...], right_ref[...]).astype(BF16)
        first = table_ref[many] == 0
        sent_ref[...] = jnp.where(first, both[rows:], both[:rows])
        held_ref[...] = jnp.where(first, both[:rows], both[rows:])

    table = jnp.stack([(me ^ mask) >> 1 for mask in masks] + [me & 1])
    out_spec = pl.BlockSpec((rows, columns), lambda i, table: (i, 0))
    return pl.pallas_call(
        kernel,
        grid_spec=pltpu.PrefetchScalarGridSpec(
            num_scalar_prefetch=1,
            grid=(many,),
            in_specs=[
                pl.BlockSpec((tokens, 2 * rows), lambda i, table: (0, table[i])),
                pl.BlockSpec(
                    (tokens, columns), lambda i, table: (0, 0), pipeline_mode=pl.Buffered(1)
                ),
            ],
            out_specs=[out_spec, out_spec],
        ),
        out_shape=[jax.ShapeDtypeStruct((width // 2, columns), BF16)] * 2,
        compiler_params=params(),
        cost_estimate=pl.CostEstimate(
            flops=2 * tokens * width * columns,
            bytes_accessed=2 * width * columns + 2 * tokens * (width + columns),
            transcendentals=0,
        ),
        name="grad_product",
    )(table, left, right)


def norm_scale(values):
    return lax.rsqrt(jnp.mean(values * values, axis=-1, keepdims=True) + 1e-06)


def norm_cot(values, gain, cotan):
    r = norm_scale(values)
    through = cotan * gain
    return r * through - values * (r * r * r) * jnp.mean(through * values, axis=-1, keepdims=True)


def per_device(
    residual,
    cotangent,
    seq_lengths,
    dealing,
    pregain,
    gatelinear,
    recurlinear,
    convkernel,
    convbias,
    inputgate,
    inputbias,
    decaygate,
    decaybias,
    decayparam,
    outlinear,
    postgain,
    mlpgate,
    mlpvalue,
    mlpdown,
):
    tokens, width = residual.shape
    channels = convbias.shape[0]
    shard_rows = gatelinear.shape[0]
    tp_count, mine = lax.axis_size("tp"), lax.axis_index("tp")
    is_odd = mine % 2 == 1
    share = tokens // tp_count
    win, kept = Windows(), {}

    def canon(values):
        rolled = jnp.concatenate([values[..., HALF:], values[..., :HALF]], axis=-1)
        return jnp.where(is_odd, rolled, values)

    def uncanon(values):
        rolled = jnp.concatenate([values[..., -HALF:], values[..., :-HALF]], axis=-1)
        return jnp.where(is_odd, rolled, values)

    def swap_rows(values):
        rolled = jnp.concatenate([values[HALF:], values[:HALF]], axis=0)
        return jnp.where(is_odd, rolled, values)

    def my_rows(values):
        return lax.dynamic_slice_in_dim(values, mine * share, share)

    chosen = lax.dynamic_slice_in_dim(dealing, lax.axis_index("fsdp") * 3, 3)
    catalog = jnp.arange(seq_lengths.shape[0], dtype=jnp.int32)
    lengths = jnp.sum(
        jnp.where(chosen[:, None] == catalog[None, :], seq_lengths[None, :], 0), axis=1
    )
    bounds = jnp.cumsum(lengths)
    base = (lax.axis_index("ctx") * tokens).astype(jnp.int32)
    info = jnp.concatenate([bounds.astype(jnp.int32), base[None], jnp.zeros((4,), jnp.int32)])
    live = (base + jnp.arange(tokens, dtype=jnp.int32) < bounds[2]).astype(F32)[:, None]

    def pre_norm(values):
        values = values.astype(F32)
        return (values * norm_scale(values) * pregain).astype(BF16)

    recur_low = canon(recurlinear.astype(BF16))
    small_gates = jnp.concatenate(
        [canon(inputgate.astype(BF16)), canon(decaygate.astype(BF16))], axis=0
    ).reshape(shard_rows, -1)
    own_taps = canon(jnp.concatenate([convkernel, convbias[None], jnp.zeros((3, channels), F32)]))
    lead = 16

    def gather_pieces(shard, backward):
        pieces = {0: shard}
        for position in slow_order(backward) + [0]:
            found = {mask | 1 << position: flip(piece, position) for mask, piece in pieces.items()}
            pieces.update(found)
        return [pieces[mask] for mask in sorted(pieces)]

    gate_pieces = gather_pieces(canon(gatelinear.astype(BF16)), False)
    recur_pieces = gather_pieces(recur_low, True)
    borrowed, earlier, borrowed_taps = (
        partner(recur_low[:, channels - HALF :]),
        shifted(residual[tokens - lead :], 1),
        partner(own_taps[:, channels - HALF :]),
    )
    extra_pieces = gather_pieces(jnp.concatenate([borrowed, small_gates], axis=1), True)
    kept["gate"], kept["recur"], kept["extra"] = (
        assemble(gate_pieces), assemble(recur_pieces), assemble(extra_pieces)
    )
    kept["taps"] = jnp.concatenate([own_taps, borrowed_taps], axis=1)
    kept["normed"] = pre_norm(jnp.concatenate([earlier, residual]))
    win.event = recur_pieces[2]

    def gathered(shard):
        return lax.all_gather(win.now(shard), ("fsdp", "ctx"), axis=0, tiled=True)

    down_full = gathered(mlpdown.astype(BF16).T)
    hgate_full = gathered(mlpgate.astype(BF16))
    value_full = gathered(mlpvalue.astype(BF16))

    out_low = win.now(canon(outlinear.astype(BF16).T))
    left, right = {0: out_low}, {0: out_low}
    for step in range(1, tp_count):
        left[step] = lax.ppermute(
            left[step - 1], "tp", [(n, n + 1) for n in range(step - 1, tp_count - 1)]
        )
        right[step] = lax.ppermute(
            right[step - 1], "tp", [(n, n - 1) for n in range(1, tp_count - step + 1)]
        )
    out_parts = in_line(left, right)
    half = tp_count // 2

    vectors = canon(
        jnp.stack([inputbias, decaybias, -8.0 * jax.nn.softplus(decayparam)] + [inputbias] * 5)
    )

    def gate_weights(gates, number):
        whole = gates[:, number].reshape(BLOCK, channels)
        return jnp.concatenate(
            [whole[:, : channels - HALF], swap_rows(whole[:, channels - HALF :])], axis=1
        )

    def recur():
        gates = kept["extra"][:, HALF:].reshape(1 << cube_bits(), 2, -1, channels)
        kept["gates"] = gate_weights(gates, 0), gate_weights(gates, 1)
        normed = kept["normed"]
        branch = dot(normed, kept["recur"])
        gate_pre = dot(normed[lead:], kept["gate"])
        forward = recur_forward(
            info, branch, dot(normed, kept["extra"][:, :HALF]), kept["taps"], *kept["gates"],
            vectors,
        )
        kept["branch"], kept["gate_pre"], kept["forward"] = yield branch, gate_pre, forward
        *_, prod, state, ends = kept["forward"]
        arriving = carried(ends, False)
        kept["arriving"], (kept["states"], kept["mixed"]) = yield (
            arriving, mix_forward(prod, state, kept["gate_pre"], arriving)
        )
        kept["mixed_all"] = yield from line_gather(win, kept["mixed"])

    def gather_out():
        first, rest = out_parts[:half], out_parts[half:]
        yield from together(
            gather(kept, "out_first", jnp.concatenate(first, axis=1), False, True),
            gather(kept, "out_rest", jnp.concatenate(rest, axis=1), True, True),
        )

    win.step((-3, gather_out()), (-2, recur()))
    win.step()

    upstream = cotangent.astype(F32) * live
    upstream_low = upstream.astype(BF16)

    def start_hidden_cot():
        kept["down"] = win.now(down_full)
        kept["hidden_cot"] = yield dot(upstream_low, kept["down"])

    for step in range(1, tp_count):
        win.step(*[start_hidden_cot()] * (step == tp_count - 2))

    def feed_forward():
        out = kept["out_first"], kept["out_rest"]
        middle = mix_product(kept["mixed_all"], out, residual)
        normed_two = (middle * norm_scale(middle) * postgain).astype(BF16)
        kept["middle"], kept["two"], kept["out"] = yield middle, normed_two, out
        weights = win.now((hgate_full, value_full))
        hidden, gate_cot, value_cot = hidden_forward(kept["two"], *weights, kept["hidden_cot"])
        part = back_product([gate_cot, value_cot], weights)
        kept["hidden"], kept["gate_cot"], kept["value_cot"], kept["part"] = yield (
            hidden, gate_cot, value_cot, part
        )

    while "out_rest" not in kept:
        win.step()
    win.step(feed_forward())
    while "out" not in kept:
        win.step()

    def sum_two():
        kept["two_cot"] = yield from line_sum(win, kept["part"])

    def down_sum():
        kept["down_part"] = yield back_product([kept["hidden"]], [kept["down"]])

    def weight_grad(name, left, right, backward, floating=0):
        sent, held = yield grad_product(*win.now((left, right)), backward)
        yield from scatter(kept, name, sent, held, backward, floating)

    win.step((1, sum_two()), (2, down_sum()))
    win.step((2, weight_grad("hgate_grad", kept["two"], kept["gate_cot"], False, 1)))
    win.step((2, weight_grad("value_grad", kept["two"], kept["value_cot"], True, 2)))
    for _ in range(tp_count - 4):
        win.step()

    def recur_back():
        conv, _, pre_in, pre_dec, decays, *_ = kept["forward"]
        two_cot, middle = kept["two_cot"], my_rows(kept["middle"])
        cot = my_rows(upstream) + norm_cot(middle, postgain, two_cot)
        gain = jnp.sum(two_cot * middle * norm_scale(middle), axis=0)
        low = cot.astype(BF16)
        mixed_cot = jnp.concatenate([dot(low, out).astype(BF16) for out in kept["out"]], axis=1)
        mixed_cot = lax.all_to_all(mixed_cot, "tp", split_axis=1, concat_axis=0, tiled=True)
        gate_pre_cot, rev_prod, rev_state, rev_ends = mix_backward(
            mixed_cot, kept["gate_pre"], kept["states"], decays
        )
        part, low, _ = lax.optimization_barrier((kept["down_part"], low, rev_ends))
        kept["down_sum"] = lax.psum_scatter(part, "tp", scatter_dimension=0, tiled=True)
        kept["low_all"] = lax.all_gather(low, "tp", axis=0, tiled=True)
        returning = carried(rev_ends, True)
        own, going, input_low, decay_low, gate_sums = gates_backward(
            info, rev_prod, rev_state, returning, kept["states"], kept["arriving"], pre_in,
            pre_dec, conv, *kept["gates"], vectors,
        )
        coming = partner(going)
        trail = shifted(own[:8], -1)
        trail_coming = shifted(partner(going[:16]), -1)[:8].astype(F32)
        trail = jnp.concatenate(
            [trail[:, : channels - HALF], trail[:, channels - HALF :] + trail_coming], axis=1
        )
        branch_low, conv_sums = conv_backward(
            info, own, coming, trail, kept["branch"], kept["taps"]
        )
        part = back_product([gate_pre_cot, branch_low], [kept["gate"], kept["recur"]])
        (
            kept["cot"], kept["gain_two"], kept["gate_pre_cot"], kept["branch_low"], kept["lows"],
            kept["sums"], kept["part"],
        ) = yield (
            cot, gain, gate_pre_cot, branch_low, (input_low, decay_low), (conv_sums, gate_sums),
            part,
        )

    win.step((1, recur_back()))

    residual_mine = my_rows(residual).astype(F32)

    def finish():
        kept["normed_cot"] = yield from line_sum(win, kept["part"])
        cot = kept["cot"] + norm_cot(residual_mine, pregain, kept["normed_cot"])
        kept["residual_grad"] = yield from line_gather(win, cot.astype(BF16))

    def finish_output():
        total = my_rows(kept["middle"]) + win.now(kept["down_sum"]).astype(F32)
        low = yield (my_rows(live) * total).astype(BF16)
        kept["output"] = lax.all_gather(low, "tp", axis=0, tiled=True)

    def gate_grads(cotan):
        conv_low = kept["forward"][1]
        whole = jnp.concatenate(
            [
                dot_tn(conv_low[:, begin : begin + BLOCK], cotan[:, begin : begin + BLOCK])
                for begin in range(0, channels, BLOCK)
            ],
            axis=1,
        )
        return jnp.concatenate(
            [whole[:, : channels - HALF], swap_rows(whole[:, channels - HALF :])], axis=1
        ).reshape(1 << cube_bits(), -1, channels)

    def small_grads():
        small = jnp.concatenate([gate_grads(cotan) for cotan in win.now(kept["lows"])], axis=1)
        me, masks = cube_index(), scatter_masks(False)[1]
        sent, held = yield [
            jnp.concatenate(
                [
                    lax.dynamic_index_in_dim(small, me ^ mask ^ other, keepdims=False)
                    for mask in masks
                ]
            ).astype(BF16)
            for other in (1, 0)
        ]
        yield from scatter(kept, "small", sent, held, False)

    def cube_sum(name, values):
        for position in range(cube_bits()):
            values = values + (yield flip(values, position))
        kept[name] = values

    def sum_gains():
        cot = kept["normed_cot"]
        gain = jnp.sum(cot * residual_mine * norm_scale(residual_mine), axis=0)
        values = jnp.stack([gain, kept["gain_two"]])
        for number in range(cube_bits() + tp_count.bit_length() - 1):
            if number < cube_bits():
                values = values + flip(values, number)
            else:
                values = values + partner(values, number - cube_bits())
            if number % 2:
                values = yield values
        kept["gains"] = values

    win.step(
        (1, finish()),
        (2, finish_output()),
        (2, weight_grad("down_grad", upstream_low, kept["hidden"], False, 1)),
    )
    normed = kept["normed"][lead:]
    win.step(
        (2, weight_grad("gate_grad", normed, kept["gate_pre_cot"], False)),
        (2, weight_grad("recur_grad", normed, kept["branch_low"], True)),
        (2, cube_sum(
            "parts", jnp.sum(jnp.concatenate(kept["sums"]).reshape(8, 8, channels), axis=1)
        )),
    )
    win.step(
        (2, weight_grad("out_grad", kept["low_all"], kept["mixed"], True)), (2, small_grads())
    )
    win.step((2, sum_gains()))
    while win.live:
        win.step()

    gate_rows = inputgate.shape[0]
    small_own, parts = uncanon(kept["small"]), uncanon(kept["parts"])
    return (
        kept["output"],
        jnp.concatenate(kept["residual_grad"]),
        kept["gains"][0],
        uncanon(kept["gate_grad"]),
        uncanon(kept["recur_grad"]),
        parts[0:4],
        parts[4],
        small_own[:gate_rows],
        parts[5],
        small_own[gate_rows:],
        parts[6],
        parts[7] * (-8.0 * jax.nn.sigmoid(decayparam)),
        uncanon(kept["out_grad"]).T,
        kept["gains"][1],
        kept["hgate_grad"],
        kept["value_grad"],
        kept["down_grad"].T,
    )


def solution(mesh):
    rows, by_tp = P(("fsdp", "ctx"), None), P("tp")
    matrix, turned = P(("fsdp", "ctx"), "tp"), P("tp", ("fsdp", "ctx"))
    return jax.shard_map(
        per_device,
        mesh=mesh,
        in_specs=(
            rows, rows, P(), P(), P(), matrix, matrix, P(None, "tp"), by_tp, matrix, by_tp, matrix,
            by_tp, by_tp, turned, P(), matrix, matrix, turned,
        ),
        out_specs=(
            rows, rows, P(), matrix, matrix, P(None, "tp"), by_tp, matrix, by_tp, matrix, by_tp,
            by_tp, turned, P(), matrix, matrix, turned,
        ),
        check_vma=False,
    )
```

time: 1090 us -> 917 us (0.84)
  Pallas kernels: 95.7 us -> 215 us
  waiting for transfers between devices: 411 us -> 315 us
  matrix products: 131 us -> 42.2 us
  starting transfers between devices: 212 us -> 158 us
  local copies, waits for them, and re-layouts: 77.9 us -> 32.9 us
  other arithmetic: 144 us -> 129 us
  between operations: 3.71 us -> 16.4 us
    pallas_call x4 -> x15, Pallas kernels: 67.4 us -> 189 us  [the longest x6 64.4 us: grad_product(): pl.pallas_call(kernel, grid_spec=pltpu.PrefetchScalarGridSpec(num_scalar_...]
    ppermute x48 -> x30, waiting for transfers between devices: 245 us -> 167 us  [the longest x6 55.1 us: line_sum(): lax.ppermute(leftward, 'tp', [(s, s - 1) for s in range(max(count - step,...]
    dot_general x12 -> x6, matrix products: 51.9 us -> 5.3 us  [dot_tn(): lax.dot_general(a, b, (((0,), (0,)), ((), ())), preferred_element_type=F32)]
    ppermute x76 -> x62, waiting for transfers between devices: 157 us -> 119 us  [flip(): lax.ppermute(value, axis, [(i, i ^ 1 << bit) for i in range(lax.axis_size...]
    unnamed x264 -> x140, local copies, waits for them, and re-layouts: 43.6 us -> 7.4 us
    dot_general x3 -> x0, matrix products: 34.7 us -> none  [dot_nt(): lax.dot_general(a, b, (((1,), (1,)), ((), ())), preferred_element_type=F32)]
    ppermute x48 -> x30, starting transfers between devices: 118 us -> 83.7 us  [the longest x6 44.3 us: line_sum(): lax.ppermute(rightward, 'tp', [(s, s + 1) for s in range(min(step, count...]
    all_to_all x0 -> x1, waiting for transfers between devices: none -> 23.9 us  [recur_back(): lax.all_to_all(mixed_cot, 'tp', split_axis=1, concat_axis=0, tiled=True)]
  transfers between devices with their start and end apart: 139 -> 114, of which waited for: 50 -> 36; matrix products, arithmetic and copies ran while one was open for 20% -> 17% of each run, Pallas kernels for 8% -> 18%
where the time goes in v2:
time: 917 us; the launch traced here: 909 us
  waiting for transfers between devices  315 us (34%)
  Pallas kernels  215 us (23%)
  starting transfers between devices  158 us (17%)
  other arithmetic  129 us (14%)
  matrix products  42.2 us (5%)
  local copies, waits for them, and re-layouts  32.9 us (4%)
  between operations  16.4 us (2%)
    ppermute x62, waiting for transfers between devices, flip(): lax.ppermute(value, axis, [(i, i ^ 1 << bit) for i in range(lax.axis_size...  119 us
    pallas_call x6, Pallas kernels, grad_product(): pl.pallas_call(kernel, grid_spec=pltpu.PrefetchScalarGridSpec(num_scalar_...  64.4 us
    ppermute x6, waiting for transfers between devices, line_sum(): lax.ppermute(leftward, 'tp', [(s, s - 1) for s in range(max(count - step,...  55.1 us
    ppermute x6, waiting for transfers between devices, line_gather(): lax.ppermute(leftward, 'tp', [(s, s - 1) for s in range(1, count - step +...  54.8 us
    ppermute x62, starting transfers between devices, flip(): lax.ppermute(value, axis, [(i, i ^ 1 << bit) for i in range(lax.axis_size...  45.2 us
    pallas_call x3, Pallas kernels, back_product(): pl.pallas_call(kernel, grid=(width // cut,), in_specs=[const_spec((rows,...  45 us
    ppermute x6, starting transfers between devices, line_sum(): lax.ppermute(rightward, 'tp', [(s, s + 1) for s in range(min(step, count...  44.3 us
    ppermute x6, waiting for transfers between devices, line_sum(): lax.ppermute(rightward, 'tp', [(s, s + 1) for s in range(min(step, count...  43 us
  transfers between devices with their start and end apart: 114, of which 36 were waited for; matrix products, arithmetic and copies ran while one was open for 17% of the time, Pallas kernels for 18%

profile of v2, /device:TPU:0, one launch (start us, length us, event | category | flops | bytes accessed | tf_op | source)
XLA Modules:
  0.0 908.9 jit_solution(4784340505887841681)
XLA Ops:
  15.3 8.5 collective-permute-done.refs_2_
  63.2 5.3 collective-permute-start.1
  77.0 5.4 collective-permute-done.19.refs_2_
  85.1 14.2 %collective-permute-done.16.refs_6_ = bf16[320,640]{1,0:T(8,128)(2,1)} collective-permute-done((bf16[320,640]{1,0:T(8,128)(2,1)}, bf16[320,640]{1,0:T(8,128)(2,1)}, u32[]{:S(2)}, u32[]{:S(2)}) %collective-permute-start.16) | collective-permute-done | bytes 409632 | tf_op jit(solution)/shard_map/ppermute | solution.py:22
  112.4 5.6 collective-permute-done.23.refs_6_
  133.2 13.6 %recur_forward.1 = (f32[768,640]{1,0:T(8,128)}, bf16[768,768]{1,0:T(8,128)(2,1)}, f32[768,640]{1,0:T(8,128)}, f32[768,640]{1,0:T(8,128)}, f32[768,640]{1,0:T(8,1...) custom-call(s32[8]{0:T(128)} %pad_add_fusion.info_ref, f32[784,640]{1,0:T(8,128)} %fusion.91.branch_ref, ...), custom_call_target="tpu_custom_call" | custom-call | flops 577044480 | bytes 20971520 | tf_op jit(solution)/shard_map/recur_forward/pallas_call | solution.py:412
  146.8 6.4 fusion.82.gate_ref
  162.7 5.4 mix_forward.1
  173.8 5.3 convert_multiply_fusion.2
  179.1 14.4 %collective-permute-done.37 = bf16[768,640]{1,0:T(8,128)(2,1)} collective-permute-done((bf16[768,640]{1,0:T(8,128)(2,1)}, bf16[768,640]{1,0:T(8,128)(2,1)}, u32[]{:S(2)}, u32[]{:S(2)}) %collective-permute-start.37) | collective-permute-done | bytes 983072 | tf_op jit(solution)/shard_map/ppermute | solution.py:224
  202.6 13.8 %fusion.92.cot_ref = f32[768,1920]{1,0:T(8,128)} fusion(bf16[768,2560]{1,0:T(8,128)(2,1)} %get-tuple-element.366.left_ref, bf16[2560,1920]{1,0:T(8,128)(2,1)} %all-gather.6.cloned.1.call-done.refs_1_), kind=kOutput, calls=%fused_computation.241 | convolution fusion | flops 7549747200 | bytes 19660800 | tf_op jit(solution)/shard_map/dot_general | solution.py:302
  217.8 9.8 %collective-permute-done.43.refs_6_ = bf16[320,1280]{1,0:T(8,128)(2,1)} collective-permute-done((bf16[320,1280]{1,0:T(8,128)(2,1)}, bf16[320,1280]{1,0:T(8,128)(2,1)}, u32[]{:S(2)}, u32[]{:S(2)}) %collective-permute-start.43) | collective-permute-done | bytes 819232 | tf_op jit(solution)/shard_map/ppermute | solution.py:22
  236.2 19.6 %collective-permute-done.52 = bf16[768,640]{1,0:T(8,128)(2,1)} collective-permute-done((bf16[768,640]{1,0:T(8,128)(2,1)S(1)}, bf16[768,640]{1,0:T(8,128)(2,1)}, u32[]{:S(2)}, u32[]{:S(2)}) %collective-permute-start.52) | collective-permute-done | bytes 983072 | tf_op jit(solution)/shard_map/ppermute | solution.py:225
  255.8 5.8 assemble.8.refs_4_
  261.6 5.8 assemble.9.refs_5_
  271.4 18.0 %mix_product.1 = f32[768,2560]{1,0:T(8,128)} custom-call(bf16[768,640]{1,0:T(8,128)(2,1)} %get-tuple-element.530.refs_0_, bf16[768,640]{1,0:T(8,128)(2,1)} %get-tuple-element.529.refs_1_, bf16[768,640]{1,0:T(8,128)(2,1)} %get-tuple-element.528.refs_2_, bf16[768,640]{1,0:T(8,128)(2,1)} %get-tuple-element.527.refs_3_, bf16[2560,1280]{1,0:T(8,128)(2,1)} %assemble.8.refs_4_, ...), custom_call_target="tpu_custom_call" | custom-call | flops 10066329600 | bytes 31457280 | tf_op jit(solution)/shard_map/mix_product/pallas_call | solution.py:489
  297.5 23.1 %hidden_forward.1 = (bf16[768,1920]{1,0:T(8,128)(2,1)}, bf16[768,1920]{1,0:T(8,128)(2,1)}, bf16[768,1920]{1,0:T(8,128)(2,1)}) custom-call(bf16[768,2560]{1,0:T(8,128)(2,1)} %multiply_convert_fusion.x_ref.left_ref, bf16[2560,1920]{1,0:T(8,128)(2,1)} %all-gather.8.cloned.1.call-done.gate_ref.refs_2_, ...), custom_call_target="tpu_custom_call" | custom-call | flops 15099494400 | bytes 19660800 | tf_op jit(solution)/shard_map/hidden_forward/pallas_call | solution.py:800
  320.6 22.2 %back_product.3 = bf16[768,2560]{1,0:T(8,128)(2,1)} custom-call(bf16[768,1920]{1,0:T(8,128)(2,1)} %get-tuple-element.315.refs_0_.right_ref, bf16[768,1920]{1,0:T(8,128)(2,1)} %get-tuple-element.326.refs_1_.right_ref, bf16[2560,1920]{1,0:T(8,128)(2,1)} %all-gather.8.cloned.1.call-done.gate_ref.refs_2_, ...), custom_call_target="tpu_custom_call" | custom-call | flops 15099494400 | bytes 19660800 | tf_op jit(solution)/shard_map/back_product/pallas_call | solution.py:833
  347.4 12.6 %back_product.4 = bf16[768,2560]{1,0:T(8,128)(2,1)} custom-call(bf16[768,1920]{1,0:T(8,128)(2,1)} %get-tuple-element.367.refs_0_.right_ref, bf16[2560,1920]{1,0:T(8,128)(2,1)} %all-gather.6.cloned.1.call-done.refs_1_), custom_call_target="tpu_custom_call" | custom-call | flops 7549747200 | bytes 9830400 | tf_op jit(solution)/shard_map/back_product/pallas_call | solution.py:833
  360.0 8.1 collective-permute-done.53
  373.0 5.1 collective-permute-start.55
  378.7 13.8 %grad_product.6 = (bf16[1280,1920]{1,0:T(8,128)(2,1)}, bf16[1280,1920]{1,0:T(8,128)(2,1)}) custom-call(s32[5]{0:T(128)} %stack.37.table_ref, bf16[768,2560]{1,0:T(8,128)(2,1)} %multiply_convert_fusion.x_ref.left_ref, bf16[768,1920]{1,0:T(8,128)(2,1)} %get-tuple-element.315.refs_0_.right_ref), custom_call_target="tpu_custom_call" | custom-call | flops 7549747200 | bytes 16711680 | tf_op jit(solution)/shard_map/grad_product/pallas_call | solution.py:878
  392.5 5.1 collective-permute-done.55
  402.1 6.0 collective-permute-start.57
  410.5 13.8 %grad_product.7 = (bf16[1280,1920]{1,0:T(8,128)(2,1)}, bf16[1280,1920]{1,0:T(8,128)(2,1)}) custom-call(s32[5]{0:T(128)} %stack.38.table_ref, bf16[768,2560]{1,0:T(8,128)(2,1)} %multiply_convert_fusion.x_ref.left_ref, bf16[768,1920]{1,0:T(8,128)(2,1)} %get-tuple-element.326.refs_1_.right_ref), custom_call_target="tpu_custom_call" | custom-call | flops 7549747200 | bytes 16711680 | tf_op jit(solution)/shard_map/grad_product/pallas_call | solution.py:878
  432.1 5.2 fusion.84
  447.4 7.7 all-to-all-start
  455.0 23.9 %all-to-all-done = bf16[192,4,640]{2,0,1:T(8,128)(2,1)S(1)} async-done(((bf16[192,4,640]{2,0,1:T(8,128)(2,1)}), bf16[192,4,640]{2,0,1:T(8,128)(2,1)S(1)}, u32[]{:S(2)}, u32[]{:S(2)}) %all-to-all-start) | async-done | bytes 983072 | tf_op jit(solution)/shard_map/all_to_all | solution.py:1107
  480.0 7.3 mix_backward.1
  496.2 10.7 %gates_backward.1 = (f32[768,640]{1,0:T(8,128)}, bf16[768,128]{1,0:T(8,128)(2,1)}, bf16[768,640]{1,0:T(8,128)(2,1)}, bf16[768,640]{1,0:T(8,128)(2,1)}, f32[24,640]{1,0:T(8,128)}) custom-call(s32[8]{0:T(128)} %pad_add_fusion.info_ref, f32[768,640]{1,0:T(8,128)} %get-tuple-element.336.prod_ref, f32[768,640]{1,0:T(8,128)} %get-tuple-element.337.state_ref, ...), custom_call_target="tpu_custom_call" | custom-call | flops 503316480 | bytes 20971520 | tf_op jit(solution)/shard_map/gates_backward/pallas_call | solution.py:656
  507.7 6.2 convert_add_fusion.2
  521.1 6.2 convert_add_fusion.1
  532.2 6.6 conv_backward.1
  538.8 10.3 %back_product.5 = bf16[768,2560]{1,0:T(8,128)(2,1)} custom-call(bf16[768,640]{1,0:T(8,128)(2,1)} %get-tuple-element.385.refs_0_.right_ref, bf16[768,640]{1,0:T(8,128)(2,1)} %get-tuple-element.389.refs_1_.right_ref, bf16[2560,640]{1,0:T(8,128)(2,1)} %assemble.6.refs_2_, bf16[2560,640]{1,0:T(8,128)(2,1)} %assemble.5.refs_3_), custom_call_target="tpu_custom_call" | custom-call | flops 5033164800 | bytes 6553600 | tf_op jit(solution)/shard_map/back_product/pallas_call | solution.py:833
  556.9 13.4 %grad_product.8 = (bf16[1280,1920]{1,0:T(8,128)(2,1)}, bf16[1280,1920]{1,0:T(8,128)(2,1)}) custom-call(s32[5]{0:T(128)} %stack.37.table_ref, bf16[768,2560]{1,0:T(8,128)(2,1)} %get-tuple-element.366.left_ref, bf16[768,1920]{1,0:T(8,128)(2,1)} %get-tuple-element.367.refs_0_.right_ref), custom_call_target="tpu_custom_call" | custom-call | flops 7549747200 | bytes 16711680 | tf_op jit(solution)/shard_map/grad_product/pallas_call | solution.py:878
  573.4 7.9 collective-permute-done.67
  606.7 7.6 grad_product.9
  614.3 8.1 grad_product.10
  622.5 20.7 %collective-permute-done.72 = bf16[192,2560]{1,0:T(8,128)(2,1)} collective-permute-done((bf16[192,2560]{1,0:T(8,128)(2,1)}, bf16[192,2560]{1,0:T(8,128)(2,1)}, u32[]{:S(2)}, u32[]{:S(2)}) %collective-permute-start.72) | collective-permute-done | bytes 983072 | tf_op jit(solution)/shard_map/ppermute | solution.py:208
  647.6 25.6 %collective-permute-start.78 = (bf16[192,2560]{1,0:T(8,128)(2,1)}, bf16[192,2560]{1,0:T(8,128)(2,1)S(1)}, u32[]{:S(2)}, u32[]{:S(2)}) collective-permute-start(bf16[192,2560]{1,0:T(8,128)(2,1)} %get-tuple-element.396), channel_id=1, source_target_pairs={{0,1},{1,2},{2,3},{4,5},{5,6},{6,7},{8,9},{9,10},{10,11},{12,13},{... | collective-permute-start | bytes 2949128 | tf_op jit(solution)/shard_map/ppermute | solution.py:208
  680.7 7.6 grad_product.11
  689.1 6.8 convert_add_fusion
  697.6 51.5 %collective-permute-done.79 = bf16[192,2560]{1,0:T(8,128)(2,1)S(1)} collective-permute-done((bf16[192,2560]{1,0:T(8,128)(2,1)}, bf16[192,2560]{1,0:T(8,128)(2,1)S(1)}, u32[]{:S(2)}, u32[]{:S(2)}) %collective-permute-start.79) | collective-permute-done | bytes 983072 | tf_op jit(solution)/shard_map/ppermute | solution.py:211
  766.3 10.8 %collective-permute-done.86 = bf16[640,640]{1,0:T(8,128)(2,1)} collective-permute-done((bf16[640,640]{1,0:T(8,128)(2,1)S(1)}, bf16[640,640]{1,0:T(8,128)(2,1)}, u32[]{:S(2)}, u32[]{:S(2)}) %collective-permute-start.86) | collective-permute-done | bytes 819232 | tf_op jit(solution)/shard_map/ppermute | solution.py:22
  785.6 16.9 %collective-permute-done.84 = bf16[192,2560]{1,0:T(8,128)(2,1)} collective-permute-done((bf16[192,2560]{1,0:T(8,128)(2,1)}, bf16[192,2560]{1,0:T(8,128)(2,1)}, u32[]{:S(2)}, u32[]{:S(2)}) %collective-permute-start.84) | collective-permute-done | bytes 983072 | tf_op jit(solution)/shard_map/ppermute | solution.py:225
  824.5 38.0 %collective-permute-done.96 = bf16[320,640]{1,0:T(8,128)(2,1)S(1)} collective-permute-done((bf16[320,640]{1,0:T(8,128)(2,1)S(1)}, bf16[320,640]{1,0:T(8,128)(2,1)S(1)}, u32[]{:S(2)}, u32[]{:S(2)}) %collective-permute-start.96) | collective-permute-done | bytes 409632 | tf_op jit(solution)/shard_map/ppermute | solution.py:22
  871.3 4.9 fusion.4
  878.3 13.7 %collective-permute-done.103 = bf16[192,2560]{1,0:T(8,128)(2,1)S(1)} collective-permute-done((bf16[192,2560]{1,0:T(8,128)(2,1)S(1)}, bf16[192,2560]{1,0:T(8,128)(2,1)S(1)}, u32[]{:S(2)}, u32[]{:S(2)}) %collective-permute-start.103) | collective-permute-done | bytes 983072 | tf_op jit(solution)/shard_map/ppermute | solution.py:225
  (538 shorter events, 308.4 us)
Async XLA Ops:
  7.2 191.3 %all-gather.6.cloned.1.call-start = ((), (), s32[]{:S(2)}) async-start(), calls=%async_computation.2 | async-start | bytes 11059200 | tf_op jit(solution)/shard_map/all_gather | solution.py:1000
  23.8 273.7 %all-gather.10.cloned.1.call-start = ((), (), s32[]{:S(2)}) async-start(), calls=%async_computation.4 | async-start | bytes 11059200 | tf_op jit(solution)/shard_map/all_gather | solution.py:1000
  27.0 270.5 %all-gather.8.cloned.1.call-start = ((), (), s32[]{:S(2)}) async-start(), calls=%async_computation.3 | async-start | bytes 11059200 | tf_op jit(solution)/shard_map/all_gather | solution.py:1000
  28.3 34.9 %collective-permute-start.14 = (bf16[320,640]{1,0:T(8,128)(2,1)}, bf16[320,640]{1,0:T(8,128)(2,1)}, u32[]{:S(2)}, u32[]{:S(2)}) collective-permute-start(bf16[320,640]{1,0:T(8,128)(2,1)} %maximum_select_fusion.4.refs_0_), channel_id=1, source_target_pairs={{0,16},{16,0},{1,17},{17,1},{2,18},{18,2},{3,19},{19,3},{4,20},{20... | collective-permute-start | bytes 1228808 | tf_op jit(solution)/shard_map/ppermute | solution.py:22
  68.5 30.8 %collective-permute-start.16 = (bf16[320,640]{1,0:T(8,128)(2,1)}, bf16[320,640]{1,0:T(8,128)(2,1)}, u32[]{:S(2)}, u32[]{:S(2)}) collective-permute-start(bf16[320,640]{1,0:T(8,128)(2,1)} %collective-permute-done.14.refs_4_), channel_id=1, source_target_pairs={{0,8},{4,12},{8,0},{12,4},{1,9},{5,13},{9,1},{13,5},{2,10},{6,14},... | collective-permute-start | bytes 1228808 | tf_op jit(solution)/shard_map/ppermute | solution.py:22
  121.9 31.3 %collective-permute-start.6 = (bf16[320,1280]{1,0:T(8,128)(2,1)}, bf16[320,1280]{1,0:T(8,128)(2,1)}, u32[]{:S(2)}, u32[]{:S(2)}) collective-permute-start(bf16[320,1280]{1,0:T(8,128)(2,1)} %pad_maximum_fusion.3.refs_0_), channel_id=1, source_target_pairs={{0,4},{4,0},{8,12},{12,8},{1,5},{5,1},{9,13},{13,9},{2,6},{6,2},{1... | collective-permute-start | bytes 2457608 | tf_op jit(solution)/shard_map/ppermute | solution.py:22
  122.9 31.0 %collective-permute-start.5 = (bf16[320,1280]{1,0:T(8,128)(2,1)}, bf16[320,1280]{1,0:T(8,128)(2,1)}, u32[]{:S(2)}, u32[]{:S(2)}) collective-permute-start(bf16[320,1280]{1,0:T(8,128)(2,1)} %pad_maximum_fusion.3.refs_0_), channel_id=1, source_target_pairs={{0,8},{4,12},{8,0},{12,4},{1,9},{5,13},{9,1},{13,5},{2,10},{6,14},... | collective-permute-start | bytes 2457608 | tf_op jit(solution)/shard_map/ppermute | solution.py:22
  124.5 29.3 %collective-permute-start.10 = (bf16[320,1280]{1,0:T(8,128)(2,1)}, bf16[320,1280]{1,0:T(8,128)(2,1)}, u32[]{:S(2)}, u32[]{:S(2)}) collective-permute-start(bf16[320,1280]{1,0:T(8,128)(2,1)} %pad_maximum_fusion.4.refs_0_), channel_id=1, source_target_pairs={{0,4},{4,0},{8,12},{12,8},{1,5},{5,1},{9,13},{13,9},{2,6},{6,2},{1... | collective-permute-start | bytes 2457608 | tf_op jit(solution)/shard_map/ppermute | solution.py:22
  124.8 30.3 %collective-permute-start.9 = (bf16[320,1280]{1,0:T(8,128)(2,1)}, bf16[320,1280]{1,0:T(8,128)(2,1)}, u32[]{:S(2)}, u32[]{:S(2)}) collective-permute-start(bf16[320,1280]{1,0:T(8,128)(2,1)} %pad_maximum_fusion.4.refs_0_), channel_id=1, source_target_pairs={{0,16},{16,0},{1,17},{17,1},{2,18},{18,2},{3,19},{19,3},{4,20},{20... | collective-permute-start | bytes 2457608 | tf_op jit(solution)/shard_map/ppermute | solution.py:22
  161.4 37.1 %collective-permute-start.39 = (bf16[320,1280]{1,0:T(8,128)(2,1)}, bf16[320,1280]{1,0:T(8,128)(2,1)}, u32[]{:S(2)}, u32[]{:S(2)}) collective-permute-start(bf16[320,1280]{1,0:T(8,128)(2,1)} %pad_maximum_fusion.3.refs_0_), channel_id=1, source_target_pairs={{0,16},{16,0},{1,17},{17,1},{2,18},{18,2},{3,19},{19,3},{4,20},{20... | collective-permute-start | bytes 2457608 | tf_op jit(solution)/shard_map/ppermute | solution.py:22
  162.1 38.5 %collective-permute-start.42 = (bf16[320,1280]{1,0:T(8,128)(2,1)}, bf16[320,1280]{1,0:T(8,128)(2,1)}, u32[]{:S(2)}, u32[]{:S(2)}) collective-permute-start(bf16[320,1280]{1,0:T(8,128)(2,1)} %pad_maximum_fusion.4.refs_0_), channel_id=1, source_target_pairs={{0,8},{4,12},{8,0},{12,4},{1,9},{5,13},{9,1},{13,5},{2,10},{6,14},... | collective-permute-start | bytes 2457608 | tf_op jit(solution)/shard_map/ppermute | solution.py:22
  162.1 39.3 %collective-permute-start.41 = (bf16[320,1280]{1,0:T(8,128)(2,1)}, bf16[320,1280]{1,0:T(8,128)(2,1)}, u32[]{:S(2)}, u32[]{:S(2)}) collective-permute-start(bf16[320,1280]{1,0:T(8,128)(2,1)} %collective-permute-done.5.refs_2_), channel_id=1, source_target_pairs={{0,4},{4,0},{8,12},{12,8},{1,5},{5,1},{9,13},{13,9},{2,6},{6,2},{1... | collective-permute-start | bytes 2457608 | tf_op jit(solution)/shard_map/ppermute | solution.py:22
  168.1 25.4 %collective-permute-start.37 = (bf16[768,640]{1,0:T(8,128)(2,1)}, bf16[768,640]{1,0:T(8,128)(2,1)}, u32[]{:S(2)}, u32[]{:S(2)}) collective-permute-start(bf16[768,640]{1,0:T(8,128)(2,1)} %get-tuple-element.406.right_ref), channel_id=1, source_target_pairs={{0,1},{1,2},{2,3},{4,5},{5,6},{6,7},{8,9},{9,10},{10,11},{12,13},{... | collective-permute-start | bytes 2949128 | tf_op jit(solution)/shard_map/ppermute | solution.py:224
  172.5 26.1 %collective-permute-start.38 = (bf16[768,640]{1,0:T(8,128)(2,1)}, bf16[768,640]{1,0:T(8,128)(2,1)}, u32[]{:S(2)}, u32[]{:S(2)}) collective-permute-start(bf16[768,640]{1,0:T(8,128)(2,1)} %get-tuple-element.406.right_ref), channel_id=1, source_target_pairs={{1,0},{2,1},{3,2},{5,4},{6,5},{7,6},{9,8},{10,9},{11,10},{13,12},{... | collective-permute-start | bytes 2949128 | tf_op jit(solution)/shard_map/ppermute | solution.py:225
  198.6 29.0 %collective-permute-start.43 = (bf16[320,1280]{1,0:T(8,128)(2,1)}, bf16[320,1280]{1,0:T(8,128)(2,1)}, u32[]{:S(2)}, u32[]{:S(2)}) collective-permute-start(bf16[320,1280]{1,0:T(8,128)(2,1)} %collective-permute-done.9.refs_4_), channel_id=1, source_target_pairs={{0,8},{4,12},{8,0},{12,4},{1,9},{5,13},{9,1},{13,5},{2,10},{6,14},... | collective-permute-start | bytes 2457608 | tf_op jit(solution)/shard_map/ppermute | solution.py:22
  200.6 27.9 %collective-permute-start.45 = (bf16[768,640]{1,0:T(8,128)(2,1)}, bf16[768,640]{1,0:T(8,128)(2,1)S(1)}, u32[]{:S(2)}, u32[]{:S(2)}) collective-permute-start(bf16[768,640]{1,0:T(8,128)(2,1)} %collective-permute-done.37), channel_id=1, source_target_pairs={{1,2},{2,3},{5,6},{6,7},{9,10},{10,11},{13,14},{14,15},{17,18},{18... | collective-permute-start | bytes 2949128 | tf_op jit(solution)/shard_map/ppermute | solution.py:224
  201.3 27.2 %collective-permute-start.46 = (bf16[768,640]{1,0:T(8,128)(2,1)}, bf16[768,640]{1,0:T(8,128)(2,1)S(1)}, u32[]{:S(2)}, u32[]{:S(2)}) collective-permute-start(bf16[768,640]{1,0:T(8,128)(2,1)} %collective-permute-done.38), channel_id=1, source_target_pairs={{1,0},{2,1},{5,4},{6,5},{9,8},{10,9},{13,12},{14,13},{17,16},{18,1... | collective-permute-start | bytes 2949128 | tf_op jit(solution)/shard_map/ppermute | solution.py:225
  229.7 26.1 %collective-permute-start.52 = (bf16[768,640]{1,0:T(8,128)(2,1)S(1)}, bf16[768,640]{1,0:T(8,128)(2,1)}, u32[]{:S(2)}, u32[]{:S(2)}) collective-permute-start(bf16[768,640]{1,0:T(8,128)(2,1)S(1)} %collective-permute-done.46), channel_id=1, source_target_pairs={{1,0},{5,4},{9,8},{13,12},{17,16},{21,20},{25,24},{29,28}} | collective-permute-start | bytes 2949128 | tf_op jit(solution)/shard_map/ppermute | solution.py:225
  400.8 28.3 %collective-permute-start.59 = (bf16[1280,1920]{1,0:T(8,128)(2,1)}, bf16[1280,1920]{1,0:T(8,128)(2,1)}, u32[]{:S(2)}, u32[]{:S(2)}) collective-permute-start(bf16[1280,1920]{1,0:T(8,128)(2,1)} %get-tuple-element.323), channel_id=1, source_target_pairs={{0,4},{4,0},{8,12},{12,8},{1,5},{5,1},{9,13},{13,9},{2,6},{6,2},{1... | collective-permute-start | bytes 14745608 | tf_op jit(solution)/shard_map/ppermute | solution.py:22
  400.8 27.1 %collective-permute-start.58 = (bf16[192,2560]{1,0:T(8,128)(2,1)}, bf16[192,2560]{1,0:T(8,128)(2,1)}, u32[]{:S(2)}, u32[]{:S(2)}) collective-permute-start(bf16[192,2560]{1,0:T(8,128)(2,1)} %get-tuple-element.321), channel_id=1, source_target_pairs={{1,0},{2,1},{3,2},{5,4},{6,5},{7,6},{9,8},{10,9},{11,10},{13,12},{... | collective-permute-start | bytes 2949128 | tf_op jit(solution)/shard_map/ppermute | solution.py:211
  402.1 27.0 %collective-permute-start.57 = (bf16[192,2560]{1,0:T(8,128)(2,1)}, bf16[192,2560]{1,0:T(8,128)(2,1)}, u32[]{:S(2)}, u32[]{:S(2)}) collective-permute-start(bf16[192,2560]{1,0:T(8,128)(2,1)} %get-tuple-element.320), channel_id=1, source_target_pairs={{0,1},{1,2},{2,3},{4,5},{5,6},{6,7},{8,9},{9,10},{10,11},{12,13},{... | collective-permute-start | bytes 2949128 | tf_op jit(solution)/shard_map/ppermute | solution.py:208
  447.4 31.6 %all-to-all-start = ((bf16[192,4,640]{2,0,1:T(8,128)(2,1)}), bf16[192,4,640]{2,0,1:T(8,128)(2,1)S(1)}, u32[]{:S(2)}, u32[]{:S(2)}) async-start(bf16[192,4,640]{2,0,1:T(8,128)(2,1)} %bitcast.64), calls=%async_computation | async-start | bytes 1966080 | tf_op jit(solution)/shard_map/all_to_all | solution.py:1107
  455.0 115.2 %reduce-scatter.2.cloned.1.call-start = ((), (), s32[]{:S(2)}) async-start(), calls=%async_computation.5 | async-start | bytes 4915200 | tf_op jit(solution)/shard_map/reduce_scatter | solution.py:1112
  487.3 185.9 %all-gather.14.cloned.1.call-start = ((), (), s32[]{:S(2)}) async-start(), calls=%async_computation.7 | async-start | bytes 4915200 | tf_op jit(solution)/shard_map/all_gather | solution.py:1113
  487.3 33.8 %collective-permute-start.70 = (bf16[1280,1920]{1,0:T(8,128)(2,1)}, bf16[1280,1920]{1,0:T(8,128)(2,1)}, u32[]{:S(2)}, u32[]{:S(2)}) collective-permute-start(bf16[1280,1920]{1,0:T(8,128)(2,1)} %get-tuple-element.361), channel_id=1, source_target_pairs={{0,4},{4,0},{8,12},{12,8},{1,5},{5,1},{9,13},{13,9},{2,6},{6,2},{1... | collective-permute-start | bytes 14745608 | tf_op jit(solution)/shard_map/ppermute | solution.py:22
  513.9 59.5 %collective-permute-start.69 = (bf16[640,1920]{1,0:T(8,128)(2,1)}, bf16[640,1920]{1,0:T(8,128)(2,1)S(1)}, u32[]{:S(2)}, u32[]{:S(2)}) collective-permute-start(bf16[640,1920]{1,0:T(8,128)(2,1)} %get-tuple-element.502), channel_id=1, source_target_pairs={{0,16},{16,0},{1,17},{17,1},{2,18},{18,2},{3,19},{19,3},{4,20},{20... | collective-permute-start | bytes 7372808 | tf_op jit(solution)/shard_map/ppermute | solution.py:22
  515.5 266.0 %all-gather.12.cloned.1.call-start = ((), (), s32[]{:S(2)}) async-start(), calls=%async_computation.6 | async-start | bytes 4915200 | tf_op jit(solution)/shard_map/all_gather | solution.py:1149
  527.3 57.9 %collective-permute-start.71 = (bf16[640,1920]{1,0:T(8,128)(2,1)}, bf16[640,1920]{1,0:T(8,128)(2,1)}, u32[]{:S(2)}, u32[]{:S(2)}) collective-permute-start(bf16[640,1920]{1,0:T(8,128)(2,1)} %get-tuple-element.500), channel_id=1, source_target_pairs={{0,8},{4,12},{8,0},{12,4},{1,9},{5,13},{9,1},{13,5},{2,10},{6,14},... | collective-permute-start | bytes 7372808 | tf_op jit(solution)/shard_map/ppermute | solution.py:22
  552.0 29.2 %collective-permute-start.67 = (bf16[192,2560]{1,0:T(8,128)(2,1)}, bf16[192,2560]{1,0:T(8,128)(2,1)}, u32[]{:S(2)}, u32[]{:S(2)}) collective-permute-start(bf16[192,2560]{1,0:T(8,128)(2,1)} %get-tuple-element.352), channel_id=1, source_target_pairs={{0,1},{4,5},{8,9},{12,13},{16,17},{20,21},{24,25},{28,29}} | collective-permute-start | bytes 2949128 | tf_op jit(solution)/shard_map/ppermute | solution.py:208
  589.3 53.9 %collective-permute-start.76 = (bf16[1280,1920]{1,0:T(8,128)(2,1)}, bf16[1280,1920]{1,0:T(8,128)(2,1)}, u32[]{:S(2)}, u32[]{:S(2)}) collective-permute-start(bf16[1280,1920]{1,0:T(8,128)(2,1)} %get-tuple-element.382), channel_id=1, source_target_pairs={{0,4},{4,0},{8,12},{12,8},{1,5},{5,1},{9,13},{13,9},{2,6},{6,2},{1... | collective-permute-start | bytes 14745608 | tf_op jit(solution)/shard_map/ppermute | solution.py:22
  592.6 50.6 %collective-permute-start.75 = (bf16[320,1920]{1,0:T(8,128)(2,1)}, bf16[320,1920]{1,0:T(8,128)(2,1)}, u32[]{:S(2)}, u32[]{:S(2)}) collective-permute-start(bf16[320,1920]{1,0:T(8,128)(2,1)} %fusion.8), channel_id=1, source_target_pairs={{0,16},{16,0},{1,17},{17,1},{2,18},{18,2},{3,19},{19,3},{4,20},{20... | collective-permute-start | bytes 3686408 | tf_op jit(solution)/shard_map/ppermute | solution.py:22
  594.4 48.8 %collective-permute-start.74 = (bf16[320,1920]{1,0:T(8,128)(2,1)}, bf16[320,1920]{1,0:T(8,128)(2,1)}, u32[]{:S(2)}, u32[]{:S(2)}) collective-permute-start(bf16[320,1920]{1,0:T(8,128)(2,1)} %fusion.9), channel_id=1, source_target_pairs={{0,8},{4,12},{8,0},{12,4},{1,9},{5,13},{9,1},{13,5},{2,10},{6,14},... | collective-permute-start | bytes 3686408 | tf_op jit(solution)/shard_map/ppermute | solution.py:22
  596.2 26.2 %collective-permute-start.73 = (bf16[192,2560]{1,0:T(8,128)(2,1)}, bf16[192,2560]{1,0:T(8,128)(2,1)}, u32[]{:S(2)}, u32[]{:S(2)}) collective-permute-start(bf16[192,2560]{1,0:T(8,128)(2,1)} %get-tuple-element.376), channel_id=1, source_target_pairs={{2,1},{3,2},{6,5},{7,6},{10,9},{11,10},{14,13},{15,14},{18,17},{19... | collective-permute-start | bytes 2949128 | tf_op jit(solution)/shard_map/ppermute | solution.py:211
  597.8 45.3 %collective-permute-start.72 = (bf16[192,2560]{1,0:T(8,128)(2,1)}, bf16[192,2560]{1,0:T(8,128)(2,1)}, u32[]{:S(2)}, u32[]{:S(2)}) collective-permute-start(bf16[192,2560]{1,0:T(8,128)(2,1)} %get-tuple-element.373), channel_id=1, source_target_pairs={{0,1},{1,2},{4,5},{5,6},{8,9},{9,10},{12,13},{13,14},{16,17},{17,1... | collective-permute-start | bytes 2949128 | tf_op jit(solution)/shard_map/ppermute | solution.py:208
  647.6 101.6 %collective-permute-start.78 = (bf16[192,2560]{1,0:T(8,128)(2,1)}, bf16[192,2560]{1,0:T(8,128)(2,1)S(1)}, u32[]{:S(2)}, u32[]{:S(2)}) collective-permute-start(bf16[192,2560]{1,0:T(8,128)(2,1)} %get-tuple-element.396), channel_id=1, source_target_pairs={{0,1},{1,2},{2,3},{4,5},{5,6},{6,7},{8,9},{9,10},{10,11},{12,13},{... | collective-permute-start | bytes 2949128 | tf_op jit(solution)/shard_map/ppermute | solution.py:208
  674.8 74.3 %collective-permute-start.80 = (bf16[1280,640]{1,0:T(8,128)(2,1)}, bf16[1280,640]{1,0:T(8,128)(2,1)}, u32[]{:S(2)}, u32[]{:S(2)}) collective-permute-start(bf16[1280,640]{1,0:T(8,128)(2,1)} %get-tuple-element.399), channel_id=1, source_target_pairs={{0,4},{4,0},{8,12},{12,8},{1,5},{5,1},{9,13},{13,9},{2,6},{6,2},{1... | collective-permute-start | bytes 4915208 | tf_op jit(solution)/shard_map/ppermute | solution.py:22
  674.9 74.3 %collective-permute-start.81 = (bf16[1280,640]{1,0:T(8,128)(2,1)}, bf16[1280,640]{1,0:T(8,128)(2,1)}, u32[]{:S(2)}, u32[]{:S(2)}) collective-permute-start(bf16[1280,640]{1,0:T(8,128)(2,1)} %get-tuple-element.401), channel_id=1, source_target_pairs={{0,4},{4,0},{8,12},{12,8},{1,5},{5,1},{9,13},{13,9},{2,6},{6,2},{1... | collective-permute-start | bytes 4915208 | tf_op jit(solution)/shard_map/ppermute | solution.py:22
  679.0 70.1 %collective-permute-start.79 = (bf16[192,2560]{1,0:T(8,128)(2,1)}, bf16[192,2560]{1,0:T(8,128)(2,1)S(1)}, u32[]{:S(2)}, u32[]{:S(2)}) collective-permute-start(bf16[192,2560]{1,0:T(8,128)(2,1)} %get-tuple-element.397), channel_id=1, source_target_pairs={{1,0},{2,1},{3,2},{5,4},{6,5},{7,6},{9,8},{10,9},{11,10},{13,12},{... | collective-permute-start | bytes 2949128 | tf_op jit(solution)/shard_map/ppermute | solution.py:211
  695.9 89.6 %collective-permute-start.85 = (bf16[640,1920]{1,0:T(8,128)(2,1)}, bf16[640,1920]{1,0:T(8,128)(2,1)}, u32[]{:S(2)}, u32[]{:S(2)}) collective-permute-start(bf16[640,1920]{1,0:T(8,128)(2,1)} %get-tuple-element.498), channel_id=1, source_target_pairs={{0,16},{16,0},{1,17},{17,1},{2,18},{18,2},{3,19},{19,3},{4,20},{20... | collective-permute-start | bytes 7372808 | tf_op jit(solution)/shard_map/ppermute | solution.py:22
  756.9 45.6 %collective-permute-start.89 = (bf16[1280,640]{1,0:T(8,128)(2,1)}, bf16[1280,640]{1,0:T(8,128)(2,1)}, u32[]{:S(2)}, u32[]{:S(2)}) collective-permute-start(bf16[1280,640]{1,0:T(8,128)(2,1)} %get-tuple-element.433), channel_id=1, source_target_pairs={{0,4},{4,0},{8,12},{12,8},{1,5},{5,1},{9,13},{13,9},{2,6},{6,2},{1... | collective-permute-start | bytes 4915208 | tf_op jit(solution)/shard_map/ppermute | solution.py:22
  761.8 40.7 %collective-permute-start.83 = (bf16[192,2560]{1,0:T(8,128)(2,1)}, bf16[192,2560]{1,0:T(8,128)(2,1)}, u32[]{:S(2)}, u32[]{:S(2)}) collective-permute-start(bf16[192,2560]{1,0:T(8,128)(2,1)} %fusion.14), channel_id=1, source_target_pairs={{0,1},{1,2},{2,3},{4,5},{5,6},{6,7},{8,9},{9,10},{10,11},{12,13},{... | collective-permute-start | bytes 2949128 | tf_op jit(solution)/shard_map/ppermute | solution.py:224
  777.1 25.4 %collective-permute-start.84 = (bf16[192,2560]{1,0:T(8,128)(2,1)}, bf16[192,2560]{1,0:T(8,128)(2,1)}, u32[]{:S(2)}, u32[]{:S(2)}) collective-permute-start(bf16[192,2560]{1,0:T(8,128)(2,1)} %fusion.14), channel_id=1, source_target_pairs={{1,0},{2,1},{3,2},{5,4},{6,5},{7,6},{9,8},{10,9},{11,10},{13,12},{... | collective-permute-start | bytes 2949128 | tf_op jit(solution)/shard_map/ppermute | solution.py:225
  802.5 60.0 %collective-permute-start.93 = (bf16[192,2560]{1,0:T(8,128)(2,1)}, bf16[192,2560]{1,0:T(8,128)(2,1)S(1)}, u32[]{:S(2)}, u32[]{:S(2)}) collective-permute-start(bf16[192,2560]{1,0:T(8,128)(2,1)} %collective-permute-done.83), channel_id=1, source_target_pairs={{1,2},{2,3},{5,6},{6,7},{9,10},{10,11},{13,14},{14,15},{17,18},{18... | collective-permute-start | bytes 2949128 | tf_op jit(solution)/shard_map/ppermute | solution.py:224
  809.0 53.5 %collective-permute-start.95 = (bf16[320,1920]{1,0:T(8,128)(2,1)S(1)}, bf16[320,1920]{1,0:T(8,128)(2,1)S(1)}, u32[]{:S(2)}, u32[]{:S(2)}) collective-permute-start(bf16[320,1920]{1,0:T(8,128)(2,1)S(1)} %fusion.7), channel_id=1, source_target_pairs={{0,8},{4,12},{8,0},{12,4},{1,9},{5,13},{9,1},{13,5},{2,10},{6,14},... | collective-permute-start | bytes 3686408 | tf_op jit(solution)/shard_map/ppermute | solution.py:22
  814.8 47.7 %collective-permute-start.94 = (bf16[192,2560]{1,0:T(8,128)(2,1)}, bf16[192,2560]{1,0:T(8,128)(2,1)S(1)}, u32[]{:S(2)}, u32[]{:S(2)}) collective-permute-start(bf16[192,2560]{1,0:T(8,128)(2,1)} %collective-permute-done.84), channel_id=1, source_target_pairs={{1,0},{2,1},{5,4},{6,5},{9,8},{10,9},{13,12},{14,13},{17,16},{18,1... | collective-permute-start | bytes 2949128 | tf_op jit(solution)/shard_map/ppermute | solution.py:225
  818.0 44.5 %collective-permute-start.98 = (bf16[640,640]{1,0:T(8,128)(2,1)S(1)}, bf16[640,640]{1,0:T(8,128)(2,1)S(1)}, u32[]{:S(2)}, u32[]{:S(2)}) collective-permute-start(bf16[640,640]{1,0:T(8,128)(2,1)S(1)} %get-tuple-element.518), channel_id=1, source_target_pairs={{0,8},{4,12},{8,0},{12,4},{1,9},{5,13},{9,1},{13,5},{2,10},{6,14},... | collective-permute-start | bytes 2457608 | tf_op jit(solution)/shard_map/ppermute | solution.py:22
  822.3 40.2 %collective-permute-start.96 = (bf16[320,640]{1,0:T(8,128)(2,1)S(1)}, bf16[320,640]{1,0:T(8,128)(2,1)S(1)}, u32[]{:S(2)}, u32[]{:S(2)}) collective-permute-start(bf16[320,640]{1,0:T(8,128)(2,1)S(1)} %fusion.23), channel_id=1, source_target_pairs={{0,8},{4,12},{8,0},{12,4},{1,9},{5,13},{9,1},{13,5},{2,10},{6,14},... | collective-permute-start | bytes 1228808 | tf_op jit(solution)/shard_map/ppermute | solution.py:22
  865.2 26.8 %collective-permute-start.102 = (bf16[192,2560]{1,0:T(8,128)(2,1)S(1)}, bf16[192,2560]{1,0:T(8,128)(2,1)S(1)}, u32[]{:S(2)}, u32[]{:S(2)}) collective-permute-start(bf16[192,2560]{1,0:T(8,128)(2,1)S(1)} %collective-permute-done.93), channel_id=1, source_target_pairs={{2,3},{6,7},{10,11},{14,15},{18,19},{22,23},{26,27},{30,31}} | collective-permute-start | bytes 2949128 | tf_op jit(solution)/shard_map/ppermute | solution.py:224
  (137 other events, 1833.5 us)
Sparse Core Ops, SparseCore 0:
  23.9 85.6 all-gather.5
  111.5 86.5 all-gather.9
  200.1 68.1 all-gather.7
  487.4 78.7 reduce-scatter.1
  567.6 101.6 all-gather.13
  670.8 95.9 all-gather.11

commit v3 on v2

--- a/solution.py
+++ b/solution.py
@@ -1,4 +1,4 @@
-from functools import partial
+from types import SimpleNamespace
 
 import jax
 import jax.numpy as jnp
@@ -11,15 +11,39 @@
 HALF = BLOCK // 2
 ROWS = 192
 MIB = 1024 * 1024
+COST_SHARE = 1.0
 VMEM_MIB = 60
 F32 = jnp.float32
 BF16 = jnp.bfloat16
 
 
+def cost(flops, bytes_accessed, transcendentals):
+    return pl.CostEstimate(
+        flops=int(flops * COST_SHARE),
+        bytes_accessed=int(bytes_accessed * COST_SHARE),
+        transcendentals=int(transcendentals * COST_SHARE),
+    )
+
+
+CTX = ("far", "near")
+CHIPS = ("fsdp", "far")
+
+
 def flip(value, position):
-    ctx_bits = lax.axis_size("ctx").bit_length() - 1
-    axis, bit = ("ctx", position) if position < ctx_bits else ("fsdp", position - ctx_bits)
-    return lax.ppermute(value, axis, [(i, i ^ (1 << bit)) for i in range(lax.axis_size(axis))])
+    for axis in ("near", "far", "fsdp"):
+        count = lax.axis_size(axis)
+        if 1 << position < count:
+            return lax.ppermute(value, axis, [(i, i ^ 1 << position) for i in range(count)])
+        position -= count.bit_length() - 1
+    raise ValueError(position)
+
+
+def ctx_size():
+    return lax.axis_size("far") * lax.axis_size("near")
+
+
+def ctx_index():
+    return lax.axis_index("far") * lax.axis_size("near") + lax.axis_index("near")
 
 
 def partner(value, bit=0):
@@ -27,11 +51,11 @@
 
 
 def cube_bits():
-    return (lax.axis_size("fsdp") * lax.axis_size("ctx")).bit_length() - 1
+    return (lax.axis_size("fsdp") * ctx_size()).bit_length() - 1
 
 
 def cube_index():
-    return lax.axis_index("fsdp") * lax.axis_size("ctx") + lax.axis_index("ctx")
+    return lax.axis_index("fsdp") * ctx_size() + ctx_index()
 
 
 def slow_order(backward):
@@ -39,9 +63,8 @@
     return order[::-1] if backward else order
 
 
-def leap(value, mask):
-    count = 1 << cube_bits()
-    return lax.ppermute(value, ("fsdp", "ctx"), [(i, i ^ mask) for i in range(count)])
+def after(value, event):
+    return lax.optimization_barrier((value, event))[0]
 
 
 class Later:
@@ -53,6 +76,7 @@
     def __init__(self):
         self.live = []
         self.event = None
+        self.free = False
 
     def now(self, value):
         if self.event is None:
@@ -80,7 +104,7 @@
                 pass
         flown = [isinstance(value, Later) for _, _, value in waiting]
         leaves, tree = jax.tree.flatten([v for (_, _, v), late in zip(waiting, flown) if not late])
-        if leaves:
+        if leaves and not self.free:
             leaves = lax.optimization_barrier(tuple(leaves))
             self.event = min(leaves, key=lambda leaf: leaf.size)
         values = iter(jax.tree.unflatten(tree, leaves))
@@ -107,45 +131,44 @@
         pairs = [(work, value) for (work, _), value in zip(found, values)]
 
 
-def gather(kept, name, shard, backward, floating=False):
-    pieces = fresh = {0: shard}
-    done = {}
+def gather(kept, name, shard, backward, slow=False):
+    held, masks = shard, [0]
     for number, position in enumerate(slow_order(backward)):
-        found = {mask | 1 << position: flip(piece, position) for mask, piece in pieces.items()}
-        near = {mask | 1: flip(piece, 0) for mask, piece in fresh.items()}
-        found, near = yield Later((found, near)) if floating and number else (found, near)
-        if floating and number == 0:
-            yield ()
-        pieces, fresh = {**pieces, **found}, found
-        done.update(near)
-    near = yield {mask | 1: flip(piece, 0) for mask, piece in fresh.items()}
-    pieces.update(done)
-    pieces.update(near)
-    kept[name] = assemble([pieces[mask] for mask in sorted(pieces)])
-
-
-def gather_direct(kept, name, shard, floating=False):
-    count = 1 << cube_bits()
-    flying = {mask: leap(shard, mask) for mask in range(2, count, 2)}, flip(shard, 0)
-    pieces, near = yield Later(flying) if floating else flying
-    far = {mask | 1: flip(piece, 0) for mask, piece in pieces.items()}
-    if not floating:
-        far = yield far
-    pieces = {**pieces, **far, 0: shard, 1: near}
-    kept[name] = assemble([pieces[mask] for mask in sorted(pieces)])
-
-
-def assemble(pieces):
-    count, (rows, columns) = len(pieces), pieces[0].shape
+        if not slow:
+            arrived = yield flip(held, position)
+        elif number == 0:
+            arrived = yield Later(flip(held, position))
+        else:
+            half = held.shape[0] // 2
+            first = yield flip(held[:half], position)
+            second = yield flip(held[half:], position)
+            arrived = jnp.concatenate([first, second])
+        held = jnp.concatenate([held, arrived])
+        masks = masks + [mask | 1 << position for mask in masks]
+    arrived = flip(held, 0)
+    if not slow:
+        arrived = yield arrived
+    whole = assemble([held, arrived], [masks, [mask | 1 for mask in masks]])
+    setattr(kept, name, whole if not slow else (yield whole))
+
+
+def assemble(sources, masks):
+    count, many = len(sources), sum(len(some) for some in masks)
+    rows, columns = sources[0].shape[0] // len(masks[0]), sources[0].shape[1]
 
     def kernel(me_ref, *refs):
-        sources, target, sems = refs[:count], refs[count], refs[count + 1]
+        target, sems = refs[count], refs[count + 1]
         copies = []
-        for mask in range(count):
-            start = pl.multiple_of((me_ref[0] ^ mask) * rows, 16)
-            copies.append(
-                pltpu.make_async_copy(sources[mask], target.at[pl.ds(start, rows)], sems.at[mask])
-            )
+        for source, some in zip(refs, masks):
+            for n, mask in enumerate(some):
+                start = pl.multiple_of((me_ref[0] ^ mask) * rows, 16)
+                copies.append(
+                    pltpu.make_async_copy(
+                        source.at[pl.ds(n * rows, rows)],
+                        target.at[pl.ds(start, rows)],
+                        sems.at[len(copies)],
+                    )
+                )
         for copy in copies:
             copy.start()
         for copy in copies:
@@ -156,37 +179,14 @@
         in_specs=[pl.BlockSpec(memory_space=pltpu.SMEM)]
         + [pl.BlockSpec(memory_space=pl.ANY)] * count,
         out_specs=pl.BlockSpec(memory_space=pltpu.VMEM),
-        out_shape=jax.ShapeDtypeStruct((count * rows, columns), pieces[0].dtype),
-        scratch_shapes=[pltpu.SemaphoreType.DMA((count,))],
+        out_shape=jax.ShapeDtypeStruct((many * rows, columns), sources[0].dtype),
+        scratch_shapes=[pltpu.SemaphoreType.DMA((many,))],
         compiler_params=pltpu.CompilerParams(vmem_limit_bytes=VMEM_MIB * MIB),
-        cost_estimate=pl.CostEstimate(
-            flops=0, bytes_accessed=4 * count * rows * columns, transcendentals=0
+        cost_estimate=cost(
+            flops=0, bytes_accessed=4 * many * rows * columns, transcendentals=0
         ),
         name="assemble",
-    )(cube_index().astype(jnp.int32).reshape(1), *pieces)
-
-
-def scatter_masks(backward):
-    order = slow_order(backward)[::-1]
-    top = len(order) - 1
-    return order, [
-        sum(1 << position for n, position in enumerate(order) if number >> (top - n) & 1)
-        for number in range(1 << len(order))
-    ]
-
-
-def scatter(kept, name, sent, held, backward, floating=0):
-    order, _ = scatter_masks(backward)
-    arrived = flip(sent, 0)
-    if floating < 2:
-        arrived = yield arrived
-    for number, position in enumerate(order):
-        half = held.shape[0] // 2
-        outgoing = held[half:].astype(F32) + arrived[half:].astype(F32)
-        held = held[:half].astype(F32) + arrived[:half].astype(F32)
-        arrived = flip(outgoing.astype(BF16), position)
-        arrived = yield Later(arrived) if floating and number == 0 else arrived
-    kept[name] = held.astype(F32) + arrived.astype(F32)
+    )(cube_index().astype(jnp.int32).reshape(1), *sources)
 
 
 def line_sum(win, partial_sums):
@@ -204,7 +204,9 @@
         if step > 1:
             rightward = rightward + from_left.astype(F32)
             leftward = leftward + from_right.astype(F32)
-        rightward, leftward = win.lead((rightward.astype(BF16), leftward.astype(BF16)))
+        rightward, leftward = rightward.astype(BF16), leftward.astype(BF16)
+        if win is not None:
+            rightward, leftward = win.lead((rightward, leftward))
         from_left = lax.ppermute(
             rightward, "tp", [(s, s + 1) for s in range(min(step, count - 1))]
         )
@@ -215,11 +217,15 @@
     return chunk(mine) + from_left.astype(F32) + from_right.astype(F32)
 
 
-def line_gather(win, share):
+def line_gather(win, share, gate=None):
     count, mine = lax.axis_size("tp"), lax.axis_index("tp")
     left, right = {0: share}, {0: share}
     for step in range(1, count):
-        rightward, leftward = win.lead((left[step - 1], right[step - 1]))
+        rightward, leftward = left[step - 1], right[step - 1]
+        if gate is not None and step == 1:
+            rightward = leftward = after(rightward, gate)
+        if win is not None:
+            rightward, leftward = win.lead((rightward, leftward))
         left[step], right[step] = yield (
             lax.ppermute(rightward, "tp", [(s, s + 1) for s in range(step - 1, count - 1)]),
             lax.ppermute(leftward, "tp", [(s, s - 1) for s in range(1, count - step + 1)]),
@@ -240,15 +246,21 @@
 
 
 def shifted(value, steps):
-    count = lax.axis_size("ctx")
+    count = ctx_size()
     pairs = [(s, s + steps) for s in range(count) if 0 <= s + steps < count]
-    return lax.ppermute(value, "ctx", pairs)
+    return lax.ppermute(value, CTX, pairs)
+
+
+def shifted_partner(value):
+    count, many = ctx_size(), lax.axis_size("tp")
+    pairs = [((c + 1) * many + t, c * many + (t ^ 1)) for c in range(count - 1) for t in range(many)]
+    return lax.ppermute(value, CTX + ("tp",), pairs)
 
 
 def carried(ends, backward):
     sign = -1 if backward else 1
     pairs = [
-        shifted(ends, sign * distance) for distance in range(lax.axis_size("ctx") - 1, 0, -1)
+        shifted(ends, sign * distance) for distance in range(ctx_size() - 1, 0, -1)
     ]
     state = pairs[0][1]
     for pair in pairs[1:]:
@@ -433,7 +445,7 @@
             pltpu.VMEM((8, channels), F32),
         ],
         compiler_params=params(),
-        cost_estimate=pl.CostEstimate(
+        cost_estimate=cost(
             flops=4 * tokens * BLOCK * channels + 150 * tokens * channels,
             bytes_accessed=20 * MIB,
             transcendentals=6 * tokens * channels,
@@ -460,7 +472,7 @@
             jax.ShapeDtypeStruct((tokens, channels), BF16),
         ],
         compiler_params=params(),
-        cost_estimate=pl.CostEstimate(
+        cost_estimate=cost(
             flops=20 * tokens * channels,
             bytes_accessed=9 * MIB,
             transcendentals=tokens * channels,
@@ -495,7 +507,7 @@
         out_specs=columns,
         out_shape=jax.ShapeDtypeStruct((tokens, width), F32),
         compiler_params=params(),
-        cost_estimate=pl.CostEstimate(
+        cost_estimate=cost(
             flops=2 * many * tokens * width * channels,
             bytes_accessed=30 * MIB,
             transcendentals=0,
@@ -571,7 +583,7 @@
         ],
         scratch_shapes=[pltpu.VMEM((ROWS, channels), F32)] + [pltpu.VMEM((8, channels), F32)] * 3,
         compiler_params=params(),
-        cost_estimate=pl.CostEstimate(
+        cost_estimate=cost(
             flops=60 * tokens * channels,
             bytes_accessed=14 * MIB,
             transcendentals=tokens * channels,
@@ -683,7 +695,7 @@
         ],
         scratch_shapes=[pltpu.VMEM((ROWS, channels), F32)] * 3 + [pltpu.VMEM((8, channels), F32)],
         compiler_params=params(),
-        cost_estimate=pl.CostEstimate(
+        cost_estimate=cost(
             flops=4 * tokens * BLOCK * channels,
             bytes_accessed=20 * MIB,
             transcendentals=5 * tokens * channels,
@@ -776,17 +788,18 @@
             pltpu.VMEM((8, channels), F32),
         ],
         compiler_params=params(),
-        cost_estimate=pl.CostEstimate(
+        cost_estimate=cost(
             flops=40 * tokens * channels, bytes_accessed=8 * MIB, transcendentals=0
         ),
         name="conv_backward",
     )(info, own, coming, trail, branch, taps)
 
 
-def hidden_forward(normed, gate_w, value_w, hidden_cot):
+def hidden_forward(normed, weights, hidden_cot):
     rows, width = normed.shape
-    units = gate_w.shape[1]
+    units = weights.shape[1] // 2
     cut = 384
+    many = units // cut
 
     def kernel(x_ref, gate_ref, value_ref, cot_ref, hidden_ref, gate_cot_ref, value_cot_ref):
         both = dot(x_ref[...], jnp.concatenate([gate_ref[...], value_ref[...]], axis=1))
@@ -799,29 +812,54 @@
     columns = pl.BlockSpec((rows, cut), lambda i: (0, i))
     return pl.pallas_call(
         kernel,
-        grid=(units // cut,),
+        grid=(many,),
         in_specs=[
             const_spec((rows, width)),
             pl.BlockSpec((width, cut), lambda i: (0, i)),
-            pl.BlockSpec((width, cut), lambda i: (0, i)),
+            pl.BlockSpec((width, cut), lambda i: (0, i + many)),
             columns,
         ],
         out_specs=[columns] * 3,
         out_shape=[jax.ShapeDtypeStruct((rows, units), BF16)] * 3,
         compiler_params=params(),
-        cost_estimate=pl.CostEstimate(
+        cost_estimate=cost(
             flops=4 * rows * width * units,
             bytes_accessed=4 * width * units,
             transcendentals=rows * units,
         ),
         name="hidden_forward",
-    )(normed, gate_w, value_w, hidden_cot)
+    )(normed, weights, weights, hidden_cot)
+
+
+def down_backward(cot, weights):
+    rows, width = cot.shape
+    units = weights.shape[1]
+    cut = 640
+
+    def kernel(x_ref, weight_ref, out_ref):
+        out_ref[...] = dot(x_ref[...], weight_ref[...])
+
+    return pl.pallas_call(
+        kernel,
+        grid=(units // cut,),
+        in_specs=[
+            const_spec((rows, width)),
+            pl.BlockSpec((width, cut), lambda i: (0, i)),
+        ],
+        out_specs=pl.BlockSpec((rows, cut), lambda i: (0, i)),
+        out_shape=jax.ShapeDtypeStruct((rows, units), F32),
+        compiler_params=params(),
+        cost_estimate=cost(
+            flops=2 * rows * width * units, bytes_accessed=4 * width * units, transcendentals=0
+        ),
+        name="down_backward",
+    )(cot, weights)
 
 
 def back_product(cots, weights):
     count = len(cots)
-    width, columns = weights[0].shape
-    rows = cots[0].shape[0]
+    width = weights[0][0].shape[0]
+    rows, columns = cots[0].shape
     cut = 512
 
     def kernel(*refs):
@@ -834,69 +872,54 @@
         kernel,
         grid=(width // cut,),
         in_specs=[const_spec((rows, columns))] * count
-        + [pl.BlockSpec((cut, columns), lambda i: (i, 0))] * count,
+        + [
+            pl.BlockSpec((cut, columns), lambda i, number=number: (i, number))
+            for _, number in weights
+        ],
         out_specs=pl.BlockSpec((rows, cut), lambda i: (0, i)),
         out_shape=jax.ShapeDtypeStruct((rows, width), BF16),
         compiler_params=params(),
-        cost_estimate=pl.CostEstimate(
+        cost_estimate=cost(
             flops=2 * count * rows * width * columns,
             bytes_accessed=2 * count * width * columns,
             transcendentals=0,
         ),
         name="back_product",
-    )(*cots, *weights)
-
-
-def grad_product(left, right, backward):
+    )(*cots, *[array for array, _ in weights])
+
+
+def plain_grad(left, rights, tail=None):
     tokens, width = left.shape
-    columns = right.shape[1]
-    _, masks = scatter_masks(backward)
-    many = len(masks)
-    rows = width // many // 2
-    me = cube_index().astype(jnp.int32)
-    if 2 * rows % 128:
-        whole = dot_tn(left, right).astype(BF16)
-
-        def laid(other):
-            return jnp.concatenate(
-                [
-                    lax.dynamic_slice_in_dim(whole, (me ^ mask ^ other) * rows, rows)
-                    for mask in masks
-                ]
-            )
-
-        return laid(1), laid(0)
-
-    def kernel(table_ref, left_ref, right_ref, sent_ref, held_ref):
-        both = dot_tn(left_ref[...], right_ref[...]).astype(BF16)
-        first = table_ref[many] == 0
-        sent_ref[...] = jnp.where(first, both[rows:], both[:rows])
-        held_ref[...] = jnp.where(first, both[:rows], both[rows:])
-
-    table = jnp.stack([(me ^ mask) >> 1 for mask in masks] + [me & 1])
-    out_spec = pl.BlockSpec((rows, columns), lambda i, table: (i, 0))
+    tails = [] if tail is None else [tail]
+    columns = sum(one.shape[1] for one in [*rights, *tails])
+    cut = 512
+
+    def kernel(left_ref, *refs):
+        out_ref = refs[-1]
+        begin = 0
+        for right_ref in refs[: len(rights)]:
+            end = begin + right_ref.shape[1]
+            out_ref[:, begin:end] = dot_tn(left_ref[...], right_ref[...]).astype(BF16)
+            begin = end
+        for tail_ref in refs[len(rights) : -1]:
+            out_ref[:, begin:] = tail_ref[...]
+
     return pl.pallas_call(
         kernel,
-        grid_spec=pltpu.PrefetchScalarGridSpec(
-            num_scalar_prefetch=1,
-            grid=(many,),
-            in_specs=[
-                pl.BlockSpec((tokens, 2 * rows), lambda i, table: (0, table[i])),
-                pl.BlockSpec(
-                    (tokens, columns), lambda i, table: (0, 0), pipeline_mode=pl.Buffered(1)
-                ),
-            ],
-            out_specs=[out_spec, out_spec],
-        ),
-        out_shape=[jax.ShapeDtypeStruct((width // 2, columns), BF16)] * 2,
+        grid=(width // cut,),
+        in_specs=[pl.BlockSpec((tokens, cut), lambda i: (0, i))]
+        + [const_spec(right.shape) for right in rights]
+        + [pl.BlockSpec((cut, one.shape[1]), lambda i: (i, 0)) for one in tails],
+        out_specs=pl.BlockSpec((cut, columns), lambda i: (i, 0)),
+        out_shape=jax.ShapeDtypeStruct((width, columns), BF16),
         compiler_params=params(),
-        cost_estimate=pl.CostEstimate(
+        cost_estimate=cost(
             flops=2 * tokens * width * columns,
             bytes_accessed=2 * width * columns + 2 * tokens * (width + columns),
             transcendentals=0,
         ),
-        name="grad_product",
-    )(table, left, right)
+        name="plain_grad",
+    )(left, *rights, *tails)
 
 
 def norm_scale(values):
@@ -932,11 +955,10 @@
 ):
     tokens, width = residual.shape
     channels = convbias.shape[0]
-    shard_rows = gatelinear.shape[0]
     tp_count, mine = lax.axis_size("tp"), lax.axis_index("tp")
     is_odd = mine % 2 == 1
     share = tokens // tp_count
-    win, kept = Windows(), {}
+    win, kept = Windows(), SimpleNamespace()
 
     def canon(values):
         rolled = jnp.concatenate([values[..., HALF:], values[..., :HALF]], axis=-1)
@@ -959,7 +981,7 @@
         jnp.where(chosen[:, None] == catalog[None, :], seq_lengths[None, :], 0), axis=1
     )
     bounds = jnp.cumsum(lengths)
-    base = (lax.axis_index("ctx") * tokens).astype(jnp.int32)
+    base = (ctx_index() * tokens).astype(jnp.int32)
     info = jnp.concatenate([bounds.astype(jnp.int32), base[None], jnp.zeros((4,), jnp.int32)])
     live = (base + jnp.arange(tokens, dtype=jnp.int32) < bounds[2]).astype(F32)[:, None]
 
@@ -970,50 +992,47 @@
     recur_low = canon(recurlinear.astype(BF16))
     small_gates = jnp.concatenate(
         [canon(inputgate.astype(BF16)), canon(decaygate.astype(BF16))], axis=0
-    ).reshape(shard_rows, -1)
+    ).reshape(recur_low.shape[0], -1)
     own_taps = canon(jnp.concatenate([convkernel, convbias[None], jnp.zeros((3, channels), F32)]))
     lead = 16
 
-    def gather_pieces(shard, backward):
-        pieces = {0: shard}
-        for position in slow_order(backward) + [0]:
-            found = {mask | 1 << position: flip(piece, position) for mask, piece in pieces.items()}
-            pieces.update(found)
-        return [pieces[mask] for mask in sorted(pieces)]
-
-    gate_pieces = gather_pieces(canon(gatelinear.astype(BF16)), False)
-    recur_pieces = gather_pieces(recur_low, True)
-    borrowed, earlier, borrowed_taps = (
-        partner(recur_low[:, channels - HALF :]),
-        shifted(residual[tokens - lead :], 1),
-        partner(own_taps[:, channels - HALF :]),
+    every = ("fsdp",) + CTX
+
+    def gather_extra():
+        borrowed, earlier = yield (
+            partner(recur_low[:, channels - HALF :]), shifted(residual[tokens - lead :], 1)
+        )
+        extra = jnp.concatenate([borrowed, small_gates], axis=1)
+        kept.extra = lax.all_gather(extra, every, axis=0, tiled=True)
+        borrowed, kept.normed = yield (
+            partner(own_taps[:, channels - HALF :]),
+            pre_norm(jnp.concatenate([earlier, residual])),
+        )
+        kept.taps = jnp.concatenate([own_taps, borrowed], axis=1)
+
+    def join_weights():
+        kept.join = yield mlpgate.astype(BF16), mlpvalue.astype(BF16)
+        kept.join = yield jnp.concatenate(kept.join, axis=1)
+
+    def gather_out():
+        parts = yield from line_gather(None, canon(outlinear.astype(BF16).T))
+        first, rest = parts[:half], parts[half:]
+        yield from together(
+            gather(kept, "out_first", jnp.concatenate(first, axis=1), False, True),
+            gather(kept, "out_rest", jnp.concatenate(rest, axis=1), True, True),
+        )
+
+    half = tp_count // 2
+    win.step(
+        (-4, gather(kept, "gate", canon(gatelinear.astype(BF16)), False)),
+        (-4, gather(kept, "recur", recur_low, True)),
+        (-4, gather_extra()),
+        (-3, join_weights()),
     )
-    extra_pieces = gather_pieces(jnp.concatenate([borrowed, small_gates], axis=1), True)
-    kept["gate"], kept["recur"], kept["extra"] = (
-        assemble(gate_pieces), assemble(recur_pieces), assemble(extra_pieces)
-    )
-    kept["taps"] = jnp.concatenate([own_taps, borrowed_taps], axis=1)
-    kept["normed"] = pre_norm(jnp.concatenate([earlier, residual]))
-    win.event = recur_pieces[2]
-
-    def gathered(shard):
-        return lax.all_gather(win.now(shard), ("fsdp", "ctx"), axis=0, tiled=True)
-
-    down_full = gathered(mlpdown.astype(BF16).T)
-    hgate_full = gathered(mlpgate.astype(BF16))
-    value_full = gathered(mlpvalue.astype(BF16))
-
-    out_low = win.now(canon(outlinear.astype(BF16).T))
-    left, right = {0: out_low}, {0: out_low}
-    for step in range(1, tp_count):
-        left[step] = lax.ppermute(
-            left[step - 1], "tp", [(n, n + 1) for n in range(step - 1, tp_count - 1)]
-        )
-        right[step] = lax.ppermute(
-            right[step - 1], "tp", [(n, n - 1) for n in range(1, tp_count - step + 1)]
-        )
-    out_parts = in_line(left, right)
-    half = tp_count // 2
+    win.step((-3, gather_out()))
+    down_full = lax.all_gather(win.now(mlpdown.astype(BF16).T), every, axis=0, tiled=True)
+    for _ in range(len(slow_order(False)) - 1):
+        win.step()
 
     vectors = canon(
         jnp.stack([inputbias, decaybias, -8.0 * jax.nn.softplus(decayparam)] + [inputbias] * 5)
@@ -1026,130 +1045,163 @@
         )
 
     def recur():
-        gates = kept["extra"][:, HALF:].reshape(1 << cube_bits(), 2, -1, channels)
-        kept["gates"] = gate_weights(gates, 0), gate_weights(gates, 1)
-        normed = kept["normed"]
-        branch = dot(normed, kept["recur"])
-        gate_pre = dot(normed[lead:], kept["gate"])
-        forward = recur_forward(
-            info, branch, dot(normed, kept["extra"][:, :HALF]), kept["taps"], *kept["gates"],
-            vectors,
-        )
-        kept["branch"], kept["gate_pre"], kept["forward"] = yield branch, gate_pre, forward
-        *_, prod, state, ends = kept["forward"]
+        normed = kept.normed
+        kept.branch, kept.gate_pre = yield (
+            dot(normed, kept.recur), dot(normed[lead:], kept.gate)
+        )
+        gates = kept.extra[:, HALF:].reshape(1 << cube_bits(), 2, -1, channels)
+        kept.gates = gate_weights(gates, 0), gate_weights(gates, 1)
+        kept.forward = yield recur_forward(
+            info, kept.branch, dot(normed, kept.extra[:, :HALF]), kept.taps,
+            *kept.gates, vectors,
+        )
+        *_, prod, state, ends = kept.forward
         arriving = carried(ends, False)
-        kept["arriving"], (kept["states"], kept["mixed"]) = yield (
-            arriving, mix_forward(prod, state, kept["gate_pre"], arriving)
-        )
-        kept["mixed_all"] = yield from line_gather(win, kept["mixed"])
-
-    def gather_out():
-        first, rest = out_parts[:half], out_parts[half:]
-        yield from together(
-            gather(kept, "out_first", jnp.concatenate(first, axis=1), False, True),
-            gather(kept, "out_rest", jnp.concatenate(rest, axis=1), True, True),
-        )
-
-    win.step((-3, gather_out()), (-2, recur()))
+        kept.arriving, (kept.states, kept.mixed) = yield (
+            arriving, mix_forward(prod, state, kept.gate_pre, arriving)
+        )
+        kept.mixed_all = yield from line_gather(win, kept.mixed)
+
+    win.step((-2, recur()))
     win.step()
+    win.step()
+    joined = lax.all_gather(win.now(kept.join), every, axis=0, tiled=True)
 
     upstream = cotangent.astype(F32) * live
     upstream_low = upstream.astype(BF16)
 
     def start_hidden_cot():
-        kept["down"] = win.now(down_full)
-        kept["hidden_cot"] = yield dot(upstream_low, kept["down"])
+        kept.down = win.now(down_full)
+        kept.hidden_cot = yield down_backward(upstream_low, kept.down)
 
     for step in range(1, tp_count):
-        win.step(*[start_hidden_cot()] * (step == tp_count - 2))
+        win.step(*[start_hidden_cot()] * (step == 1))
 
     def feed_forward():
-        out = kept["out_first"], kept["out_rest"]
-        middle = mix_product(kept["mixed_all"], out, residual)
+        out = kept.out_first, kept.out_rest
+        middle = mix_product(kept.mixed_all, out, residual)
         normed_two = (middle * norm_scale(middle) * postgain).astype(BF16)
-        kept["middle"], kept["two"], kept["out"] = yield middle, normed_two, out
-        weights = win.now((hgate_full, value_full))
-        hidden, gate_cot, value_cot = hidden_forward(kept["two"], *weights, kept["hidden_cot"])
-        part = back_product([gate_cot, value_cot], weights)
-        kept["hidden"], kept["gate_cot"], kept["value_cot"], kept["part"] = yield (
+        kept.middle, kept.two, kept.out = yield middle, normed_two, out
+        kept.joined = joined_now = win.now(joined)
+        hidden, gate_cot, value_cot = hidden_forward(kept.two, joined_now, kept.hidden_cot)
+        part = back_product([gate_cot, value_cot], [(joined_now, 0), (joined_now, 1)])
+        kept.hidden, kept.gate_cot, kept.value_cot, kept.part = yield (
             hidden, gate_cot, value_cot, part
         )
 
-    while "out_rest" not in kept:
+    while not hasattr(kept, "out_rest"):
         win.step()
     win.step(feed_forward())
-    while "out" not in kept:
+    while not hasattr(kept, "out"):
         win.step()
 
     def sum_two():
-        kept["two_cot"] = yield from line_sum(win, kept["part"])
+        kept.two_cot = yield from line_sum(win, kept.part)
 
     def down_sum():
-        kept["down_part"] = yield back_product([kept["hidden"]], [kept["down"]])
-
-    def weight_grad(name, left, right, backward, floating=0):
-        sent, held = yield grad_product(*win.now((left, right)), backward)
-        yield from scatter(kept, name, sent, held, backward, floating)
-
-    win.step((1, sum_two()), (2, down_sum()))
-    win.step((2, weight_grad("hgate_grad", kept["two"], kept["gate_cot"], False, 1)))
-    win.step((2, weight_grad("value_grad", kept["two"], kept["value_cot"], True, 2)))
+        kept.down_part = yield back_product([kept.hidden], [(kept.down, 0)])
+
+    def two_operands():
+        return kept.two, (kept.gate_cot, kept.value_cot)
+
+    def sum_offloaded(name, whole, windows):
+        result = lax.psum_scatter(win.now(whole), every, scatter_dimension=0, tiled=True)
+        for _ in range(windows):
+            yield ()
+        setattr(kept, name, (yield result))
+
+    def plain_weight_grad(name, operands, windows, before=0):
+        whole = yield plain_grad(*win.now(operands()))
+        for _ in range(before):
+            yield ()
+        yield from sum_offloaded(name, whole, windows)
+
+    def down_operands():
+        return upstream_low, (kept.hidden,)
+
+    def take_mixed():
+        mixed = [my_rows(mixed) for mixed in win.now(kept.mixed_all)]
+        kept.mixed_mine = yield jnp.concatenate(mixed, axis=1)
+
+    win.step((1, sum_two()), (2, plain_weight_grad("two_grad", two_operands, 4)))
+    win.step((2, down_sum()), (2, take_mixed()))
+    win.step((2, plain_weight_grad("down_grad", down_operands, 3, 3)))
     for _ in range(tp_count - 4):
         win.step()
 
     def recur_back():
-        conv, _, pre_in, pre_dec, decays, *_ = kept["forward"]
-        two_cot, middle = kept["two_cot"], my_rows(kept["middle"])
+        conv, _, pre_in, pre_dec, decays, *_ = kept.forward
+        two_cot, middle = kept.two_cot, my_rows(kept.middle)
         cot = my_rows(upstream) + norm_cot(middle, postgain, two_cot)
         gain = jnp.sum(two_cot * middle * norm_scale(middle), axis=0)
         low = cot.astype(BF16)
-        mixed_cot = jnp.concatenate([dot(low, out).astype(BF16) for out in kept["out"]], axis=1)
+        mixed_cot = jnp.concatenate([dot(low, out).astype(BF16) for out in kept.out], axis=1)
         mixed_cot = lax.all_to_all(mixed_cot, "tp", split_axis=1, concat_axis=0, tiled=True)
+        out_whole = plain_grad(low, (kept.mixed_mine,))
+        kept.cot, gain, mixed_cot, kept.out_whole = yield (
+            cot, gain, mixed_cot, out_whole
+        )
         gate_pre_cot, rev_prod, rev_state, rev_ends = mix_backward(
-            mixed_cot, kept["gate_pre"], kept["states"], decays
-        )
-        part, low, _ = lax.optimization_barrier((kept["down_part"], low, rev_ends))
-        kept["down_sum"] = lax.psum_scatter(part, "tp", scatter_dimension=0, tiled=True)
-        kept["low_all"] = lax.all_gather(low, "tp", axis=0, tiled=True)
-        returning = carried(rev_ends, True)
-        own, going, input_low, decay_low, gate_sums = gates_backward(
-            info, rev_prod, rev_state, returning, kept["states"], kept["arriving"], pre_in,
-            pre_dec, conv, *kept["gates"], vectors,
+            mixed_cot, kept.gate_pre, kept.states, decays
+        )
+        kept.gate_pre_cot, rev_prod, rev_state, returning = yield (
+            gate_pre_cot, rev_prod, rev_state, carried(rev_ends, True)
+        )
+        own, going, kept.lows, gate_sums = yield pick(
+            gates_backward(
+                info, rev_prod, rev_state, returning, kept.states, kept.arriving, pre_in,
+                pre_dec, conv, *kept.gates, vectors,
+            )
         )
         coming = partner(going)
         trail = shifted(own[:8], -1)
-        trail_coming = shifted(partner(going[:16]), -1)[:8].astype(F32)
+        trail_coming = shifted_partner(going[:16])[:8].astype(F32)
+        kept.trail = trail
         trail = jnp.concatenate(
             [trail[:, : channels - HALF], trail[:, channels - HALF :] + trail_coming], axis=1
         )
         branch_low, conv_sums = conv_backward(
-            info, own, coming, trail, kept["branch"], kept["taps"]
-        )
-        part = back_product([gate_pre_cot, branch_low], [kept["gate"], kept["recur"]])
-        (
-            kept["cot"], kept["gain_two"], kept["gate_pre_cot"], kept["branch_low"], kept["lows"],
-            kept["sums"], kept["part"],
-        ) = yield (
-            cot, gain, gate_pre_cot, branch_low, (input_low, decay_low), (conv_sums, gate_sums),
-            part,
-        )
-
-    win.step((1, recur_back()))
+            info, own, coming, trail, kept.branch, kept.taps
+        )
+        part = back_product(
+            [kept.gate_pre_cot, branch_low], [(kept.gate, 0), (kept.recur, 0)]
+        )
+        values = residual.astype(F32)
+        gain = jnp.stack([jnp.sum(part.astype(F32) * values * norm_scale(values), axis=0), gain])
+        kept.gains, kept.branch_low, kept.sums, kept.part = yield (
+            gain, branch_low, (conv_sums, gate_sums), part
+        )
+
+    def pick(results):
+        own, going, input_low, decay_low, sums = results
+        return own, going, (input_low, decay_low), sums
+
+    def sum_down():
+        kept.down_sum = yield from line_sum(None, kept.down_part)
+
+    def sum_out():
+        yield from sum_offloaded("out_grad", kept.out_whole, 4)
+
+    def finish_output():
+        total = my_rows(kept.middle) + kept.down_sum
+        kept.output = yield from line_gather(
+            None, (my_rows(live) * total).astype(BF16), kept.trail
+        )
+
+    win.step((1, recur_back()), (1, sum_down()))
+    win.step((2, sum_out()))
+    win.step()
+    win.step((1, finish_output()))
 
     residual_mine = my_rows(residual).astype(F32)
 
     def finish():
-        kept["normed_cot"] = yield from line_sum(win, kept["part"])
-        cot = kept["cot"] + norm_cot(residual_mine, pregain, kept["normed_cot"])
-        kept["residual_grad"] = yield from line_gather(win, cot.astype(BF16))
-
-    def finish_output():
-        total = my_rows(kept["middle"]) + win.now(kept["down_sum"]).astype(F32)
-        low = yield (my_rows(live) * total).astype(BF16)
-        kept["output"] = lax.all_gather(low, "tp", axis=0, tiled=True)
+        kept.normed_cot = yield from line_sum(win, kept.part)
+        cot = kept.cot + norm_cot(residual_mine, pregain, kept.normed_cot)
+        kept.residual_grad = yield from line_gather(win, cot.astype(BF16))
 
     def gate_grads(cotan):
-        conv_low = kept["forward"][1]
+        conv_low = kept.forward[1]
         whole = jnp.concatenate(
             [
                 dot_tn(conv_low[:, begin : begin + BLOCK], cotan[:, begin : begin + BLOCK])
@@ -1162,65 +1214,46 @@
         ).reshape(1 << cube_bits(), -1, channels)
 
     def small_grads():
-        small = jnp.concatenate([gate_grads(cotan) for cotan in win.now(kept["lows"])], axis=1)
-        me, masks = cube_index(), scatter_masks(False)[1]
-        sent, held = yield [
-            jnp.concatenate(
-                [
-                    lax.dynamic_index_in_dim(small, me ^ mask ^ other, keepdims=False)
-                    for mask in masks
-                ]
-            ).astype(BF16)
-            for other in (1, 0)
-        ]
-        yield from scatter(kept, "small", sent, held, False)
-
-    def cube_sum(name, values):
+        small = jnp.concatenate([gate_grads(cotan) for cotan in win.now(kept.lows)], axis=1)
+        kept.small = yield small.astype(BF16).reshape(width, -1)
+
+    def sum_rows():
+        parts = jnp.sum(jnp.concatenate(kept.sums).reshape(8, 8, channels), axis=1)
+        values = jnp.concatenate([parts, kept.gains.reshape(-1, channels)])
         for position in range(cube_bits()):
-            values = values + (yield flip(values, position))
-        kept[name] = values
-
-    def sum_gains():
-        cot = kept["normed_cot"]
-        gain = jnp.sum(cot * residual_mine * norm_scale(residual_mine), axis=0)
-        values = jnp.stack([gain, kept["gain_two"]])
-        for number in range(cube_bits() + tp_count.bit_length() - 1):
-            if number < cube_bits():
-                values = values + flip(values, number)
-            else:
-                values = values + partner(values, number - cube_bits())
-            if number % 2:
-                values = yield values
-        kept["gains"] = values
-
-    win.step(
-        (1, finish()),
-        (2, finish_output()),
-        (2, weight_grad("down_grad", upstream_low, kept["hidden"], False, 1)),
-    )
-    normed = kept["normed"][lead:]
-    win.step(
-        (2, weight_grad("gate_grad", normed, kept["gate_pre_cot"], False)),
-        (2, weight_grad("recur_grad", normed, kept["branch_low"], True)),
-        (2, cube_sum(
-            "parts", jnp.sum(jnp.concatenate(kept["sums"]).reshape(8, 8, channels), axis=1)
-        )),
-    )
-    win.step(
-        (2, weight_grad("out_grad", kept["low_all"], kept["mixed"], True)), (2, small_grads())
-    )
-    win.step((2, sum_gains()))
+            values = values + flip(values, position)
+        values = yield values
+        kept.parts, gains = values[:8], values[8:]
+        for bit in range(tp_count.bit_length() - 1):
+            gains = gains + (yield partner(gains, bit))
+        kept.gains = gains.reshape(2, width)
+
+    def out_total():
+        whole = win.now(kept.out_grad)
+        parts = [whole[:, n : n + channels] for n in range(0, tp_count * channels, channels)]
+        kept.out_grad = yield from line_sum(None, jnp.concatenate(parts))
+
+    def first_operands():
+        return kept.normed[lead:], (kept.gate_pre_cot, kept.branch_low), kept.small
+
+    win.step((1, finish()), (2, small_grads()))
+    win.step((2, plain_weight_grad("first_grad", first_operands, 3)))
+    win.step((2, sum_rows()))
+    win.step()
+    win.step((2, out_total()))
     while win.live:
         win.step()
 
-    gate_rows = inputgate.shape[0]
-    small_own, parts = uncanon(kept["small"]), uncanon(kept["parts"])
+    gate_rows, units = inputgate.shape[0], mlpgate.shape[1]
+    first_grad = kept.first_grad.astype(F32)
+    small_own = uncanon(first_grad[:, 2 * channels :].reshape(-1, channels))
+    parts = uncanon(kept.parts)
     return (
-        kept["output"],
-        jnp.concatenate(kept["residual_grad"]),
-        kept["gains"][0],
-        uncanon(kept["gate_grad"]),
-        uncanon(kept["recur_grad"]),
+        jnp.concatenate(kept.output),
+        jnp.concatenate(kept.residual_grad),
+        kept.gains[0],
+        uncanon(first_grad[:, :channels]),
+        uncanon(first_grad[:, channels : 2 * channels]),
         parts[0:4],
         parts[4],
         small_own[:gate_rows],
@@ -1228,20 +1261,26 @@
         small_own[gate_rows:],
         parts[6],
         parts[7] * (-8.0 * jax.nn.sigmoid(decayparam)),
-        uncanon(kept["out_grad"]).T,
-        kept["gains"][1],
-        kept["hgate_grad"],
-        kept["value_grad"],
-        kept["down_grad"].T,
+        uncanon(kept.out_grad.astype(F32)).T,
+        kept.gains[1],
+        kept.two_grad[:, :units].astype(F32),
+        kept.two_grad[:, units:].astype(F32),
+        kept.down_grad.astype(F32).T,
     )
 
 
 def solution(mesh):
-    rows, by_tp = P(("fsdp", "ctx"), None), P("tp")
-    matrix, turned = P(("fsdp", "ctx"), "tp"), P("tp", ("fsdp", "ctx"))
+    sizes = dict(mesh.shape)
+    finer = jax.sharding.Mesh(
+        mesh.devices.reshape(sizes["fsdp"], sizes["ctx"] // 2, 2, sizes["tp"]),
+        ("fsdp", "far", "near", "tp"),
+    )
+    every = ("fsdp",) + CTX
+    rows, by_tp = P(every, None), P("tp")
+    matrix, turned = P(every, "tp"), P("tp", every)
     return jax.shard_map(
         per_device,
-        mesh=mesh,
+        mesh=finer,
         in_specs=(
             rows, rows, P(), P(), P(), matrix, matrix, P(None, "tp"), by_tp, matrix, by_tp, matrix,
             by_tp, by_tp, turned, P(), matrix, matrix, turned,

time: 917 us -> 793 us (0.86)
  waiting for transfers between devices: 315 us -> 189 us
  matrix products: 42.2 us -> 24.5 us
  local copies, waits for them, and re-layouts: 32.9 us -> 42.1 us
    ppermute x77 -> x26, waiting for transfers between devices: 123 us -> 61.8 us  [the longest x17 57 us: flip(): lax.ppermute(value, axis, [(i, i ^ 1 << position) for i in range(count)])]
    ppermute x77 -> x26, starting transfers between devices: 71.1 us -> 27.3 us  [the longest x17 14 us: flip(): lax.ppermute(value, axis, [(i, i ^ 1 << position) for i in range(count)])]
    ppermute x6 -> x12, waiting for transfers between devices: 55.1 us -> 17.6 us  [line_sum(): lax.ppermute(leftward, 'tp', [(s, s - 1) for s in range(max(count - step,...]
    add x20 -> x5, other arithmetic: 32.5 us -> 0.17 us  [the longest x1 0.14 us: line_sum(): return chunk(mine) + from_left.astype(F32) + from_right.astype(F32)]
    all_to_all x1, waiting for transfers between devices: 23.9 us -> 0.01 us  [recur_back(): lax.all_to_all(mixed_cot, 'tp', split_axis=1, concat_axis=0, tiled=True)]
    ppermute x6 -> x12, starting transfers between devices: 11 us -> 33.2 us  [line_gather(): lax.ppermute(rightward, 'tp', [(s, s + 1) for s in range(step - 1, count...]
    dot_general x6 -> x5, matrix products: 36.9 us -> 16 us  [dot(): return jnp.dot(a, b, preferred_element_type=F32)]
    concatenate x5 -> x15, other arithmetic: 3.59 us -> 24.3 us  [the longest x6 16.6 us: gather(): held = jnp.concatenate([held, arrived])]
  transfers between devices with their start and end apart: 114 -> 87, of which waited for: 36 -> 31; matrix products, arithmetic and copies ran while one was open for 17% -> 23% of each run, Pallas kernels for 18% -> 22%
where the time goes in v3:
time: 793 us; the launch traced here: 784 us
  Pallas kernels  221 us (28%)
  waiting for transfers between devices  189 us (24%)
  starting transfers between devices  162 us (20%)
  other arithmetic  129 us (16%)
  local copies, waits for them, and re-layouts  42.1 us (5%)
  matrix products  24.5 us (3%)
  between operations  16.6 us (2%)
    ppermute x12, starting transfers between devices, line_sum(): lax.ppermute(rightward, 'tp', [(s, s + 1) for s in range(min(step, count...  57.5 us
    ppermute x17, waiting for transfers between devices, flip(): lax.ppermute(value, axis, [(i, i ^ 1 << position) for i in range(count)])  57 us
    pallas_call x4, Pallas kernels, plain_grad(): pl.pallas_call(kernel, grid=(width // cut,), in_specs=[pl.BlockSpec((toke...  54.1 us
    ppermute x12, waiting for transfers between devices, line_gather(): lax.ppermute(leftward, 'tp', [(s, s - 1) for s in range(1, count - step +...  53.9 us
    pallas_call x3, Pallas kernels, back_product(): pl.pallas_call(kernel, grid=(width // cut,), in_specs=[const_spec((rows,...  46.7 us
    ppermute x12, waiting for transfers between devices, line_sum(): lax.ppermute(rightward, 'tp', [(s, s + 1) for s in range(min(step, count...  38.1 us
    ppermute x12, starting transfers between devices, line_gather(): lax.ppermute(rightward, 'tp', [(s, s + 1) for s in range(step - 1, count...  33.2 us
    pallas_call x1, Pallas kernels, hidden_forward(): pl.pallas_call(kernel, grid=(many,), in_specs=[const_spec((rows, width)),...  23.1 us
  transfers between devices with their start and end apart: 87, of which 31 were waited for; matrix products, arithmetic and copies ran while one was open for 23% of the time, Pallas kernels for 22%

profile of v3, /device:TPU:0, one launch (start us, length us, event | category | flops | bytes accessed | tf_op | source)
XLA Modules:
  0.0 784.2 jit_solution(1180639854805591733)
XLA Ops:
  25.7 5.3 collective-permute-start.7
  48.7 15.1 %collective-permute-done.5 = bf16[640,640]{1,0:T(8,128)(2,1)} collective-permute-done((bf16[640,640]{1,0:T(8,128)(2,1)}, bf16[640,640]{1,0:T(8,128)(2,1)}, u32[]{:S(2)}, u32[]{:S(2)}) %collective-permute-start.5) | collective-permute-done | bytes 819232 | tf_op jit(solution)/shard_map/ppermute | solution.py:36
  81.1 8.8 %collective-permute-done.12 = bf16[320,640]{1,0:T(8,128)(2,1)} collective-permute-done((bf16[320,640]{1,0:T(8,128)(2,1)}, bf16[320,640]{1,0:T(8,128)(2,1)}, u32[]{:S(2)}, u32[]{:S(2)}) %collective-permute-start.12) | collective-permute-done | bytes 409632 | tf_op jit(solution)/shard_map/ppermute | solution.py:231
  96.7 4.8 assemble.5.refs_2_
  102.4 6.6 fusion.55.branch_ref
  122.7 13.5 %recur_forward.1 = (f32[768,640]{1,0:T(8,128)}, bf16[768,768]{1,0:T(8,128)(2,1)}, f32[768,640]{1,0:T(8,128)}, f32[768,640]{1,0:T(8,128)}, f32[768,640]{1,0:T(8,1...) custom-call(s32[8]{0:T(128)} %pad_add_fusion.info_ref, f32[784,640]{1,0:T(8,128)} %fusion.55.branch_ref, ...), custom_call_target="tpu_custom_call" | custom-call | flops 577044480 | bytes 20971520 | tf_op jit(solution)/shard_map/recur_forward/pallas_call | solution.py:424
  142.9 5.0 mix_forward.1
  159.4 7.9 %convert_multiply_fusion.4 = (f32[768,2560]{1,0:T(8,128)}, bf16[768,2560]{1,0:T(8,128)(2,1)}) fusion(bf16[768,2560]{1,0:T(8,128)(2,1)} %param.20, f32[768]{0:T(1024)S(1)} %fusion.33), kind=kLoop, calls=%fused_computation.12 | loop fusion | flops 5898240 | bytes 15731712 | tf_op jit(solution)/shard_map/mul | solution.py:1070
  167.3 14.2 %down_backward.1.cot_ref = f32[768,1920]{1,0:T(8,128)} custom-call(bf16[768,2560]{1,0:T(8,128)(2,1)} %get-tuple-element.304.x_ref.left_ref, bf16[2560,1920]{1,0:T(8,128)(2,1)} %all-gather.6.cloned.1.call-done.weight_ref.refs_1_), custom_call_target="tpu_custom_call" | custom-call | flops 7549747200 | bytes 19660800 | tf_op jit(solution)/shard_map/down_backward/pallas_call | solution.py:842
  188.9 24.7 %collective-permute-done.24 = bf16[320,1280]{1,0:T(8,128)(2,1)S(1)} collective-permute-done((bf16[320,1280]{1,0:T(8,128)(2,1)}, bf16[320,1280]{1,0:T(8,128)(2,1)S(1)}, u32[]{:S(2)}, u32[]{:S(2)}) %collective-permute-start.24) | collective-permute-done | bytes 819232 | tf_op jit(solution)/shard_map/ppermute | solution.py:36
  218.7 5.9 pad_maximum_fusion.3.refs_0_
  227.5 5.8 assemble.7.refs_5_
  233.4 5.8 assemble.6.refs_4_
  239.2 13.4 %collective-permute-done.31 = bf16[768,640]{1,0:T(8,128)(2,1)} collective-permute-done((bf16[768,640]{1,0:T(8,128)(2,1)}, bf16[768,640]{1,0:T(8,128)(2,1)}, u32[]{:S(2)}, u32[]{:S(2)}) %collective-permute-start.31) | collective-permute-done | bytes 983072 | tf_op jit(solution)/shard_map/ppermute | solution.py:231
  257.1 18.2 %mix_product.1 = f32[768,2560]{1,0:T(8,128)} custom-call(bf16[768,640]{1,0:T(8,128)(2,1)} %get-tuple-element.294.refs_0_, bf16[768,640]{1,0:T(8,128)(2,1)} %get-tuple-element.295.refs_1_, bf16[768,640]{1,0:T(8,128)(2,1)} %get-tuple-element.296.refs_2_, bf16[768,640]{1,0:T(8,128)(2,1)} %get-tuple-element.297.refs_3_, bf16[2560,1280]{1,0:T(8,128)(2,1)} %assemble.6.refs_4_, ...), custom_call_target="tpu_custom_call" | custom-call | flops 10066329600 | bytes 31457280 | tf_op jit(solution)/shard_map/mix_product/pallas_call | solution.py:501
  283.4 23.1 %hidden_forward.1 = (bf16[768,1920]{1,0:T(8,128)(2,1)}, bf16[768,1920]{1,0:T(8,128)(2,1)}, bf16[768,1920]{1,0:T(8,128)(2,1)}) custom-call(bf16[768,2560]{1,0:T(8,128)(2,1)} %multiply_convert_fusion.x_ref.left_ref, bf16[2560,3840]{1,0:T(8,128)(2,1)} %all-gather.8.cloned.1.call-done.gate_ref.value_ref.refs_2_.refs_3_, ...), custom_call_target="tpu_custom_call" | custom-call | flops 15099494400 | bytes 19660800 | tf_op jit(solution)/shard_map/hidden_forward/pallas_call | solution.py:813
  306.5 22.2 %back_product.3 = bf16[768,2560]{1,0:T(8,128)(2,1)} custom-call(bf16[768,1920]{1,0:T(8,128)(2,1)} %get-tuple-element.286.refs_0_, bf16[768,1920]{1,0:T(8,128)(2,1)} %get-tuple-element.288.refs_1_, bf16[2560,3840]{1,0:T(8,128)(2,1)} %all-gather.8.cloned.1.call-done.gate_ref.value_ref.refs_2_.refs_3_, ...), custom_call_target="tpu_custom_call" | custom-call | flops 15099494400 | bytes 19660800 | tf_op jit(solution)/shard_map/back_product/pallas_call | solution.py:871
  333.5 22.3 %plain_grad.4 = bf16[2560,3840]{1,0:T(8,128)(2,1)} custom-call(bf16[768,2560]{1,0:T(8,128)(2,1)} %multiply_convert_fusion.x_ref.left_ref, bf16[768,1920]{1,0:T(8,128)(2,1)} %get-tuple-element.286.refs_0_, bf16[768,1920]{1,0:T(8,128)(2,1)} %get-tuple-element.288.refs_1_), custom_call_target="tpu_custom_call" | custom-call | flops 15099494400 | bytes 29491200 | tf_op jit(solution)/shard_map/plain_grad/pallas_call | solution.py:907
  362.0 14.1 %back_product.4 = bf16[768,2560]{1,0:T(8,128)(2,1)} custom-call(bf16[768,1920]{1,0:T(8,128)(2,1)} %get-tuple-element.305.refs_0_, bf16[2560,1920]{1,0:T(8,128)(2,1)} %all-gather.6.cloned.1.call-done.weight_ref.refs_1_), custom_call_target="tpu_custom_call" | custom-call | flops 7549747200 | bytes 9830400 | tf_op jit(solution)/shard_map/back_product/pallas_call | solution.py:871
  388.1 7.1 collective-permute-start.36
  397.5 12.5 %plain_grad.5 = bf16[2560,1920]{1,0:T(8,128)(2,1)} custom-call(bf16[768,2560]{1,0:T(8,128)(2,1)} %get-tuple-element.304.x_ref.left_ref, bf16[768,1920]{1,0:T(8,128)(2,1)} %get-tuple-element.305.refs_0_), custom_call_target="tpu_custom_call" | custom-call | flops 7549747200 | bytes 16711680 | tf_op jit(solution)/shard_map/plain_grad/pallas_call | solution.py:907
  417.6 5.0 fusion.44
  427.3 5.2 all-to-all-start
  440.3 8.5 %plain_grad.6 = bf16[2560,2560]{1,0:T(8,128)(2,1)} custom-call(bf16[192,2560]{1,0:T(8,128)(2,1)} %copy-done.15, bf16[192,2560]{1,0:T(8,128)(2,1)} %pad_maximum_fusion.9.refs_0_), custom_call_target="tpu_custom_call" | custom-call | flops 2516582400 | bytes 15073280 | tf_op jit(solution)/shard_map/plain_grad/pallas_call | solution.py:907
  448.8 18.8 %collective-permute-done.38 = bf16[192,2560]{1,0:T(8,128)(2,1)S(1)} collective-permute-done((bf16[192,2560]{1,0:T(8,128)(2,1)}, bf16[192,2560]{1,0:T(8,128)(2,1)S(1)}, u32[]{:S(2)}, u32[]{:S(2)}) %collective-permute-start.38) | collective-permute-done | bytes 983072 | tf_op jit(solution)/shard_map/ppermute | solution.py:210
  473.5 4.9 collective-permute-start.43
  478.4 7.4 mix_backward.1
  501.4 5.7 collective-permute-start.45
  507.1 11.7 %gates_backward.1 = (f32[768,640]{1,0:T(8,128)}, bf16[768,128]{1,0:T(8,128)(2,1)}, bf16[768,640]{1,0:T(8,128)(2,1)}, bf16[768,640]{1,0:T(8,128)(2,1)}, f32[24,640]{1,0:T(8,128)}) custom-call(s32[8]{0:T(128)} %pad_add_fusion.info_ref, f32[768,640]{1,0:T(8,128)} %get-tuple-element.321.prod_ref, f32[768,640]{1,0:T(8,128)} %get-tuple-element.322.state_ref, ...), custom_call_target="tpu_custom_call" | custom-call | flops 503316480 | bytes 20971520 | tf_op jit(solution)/shard_map/gates_backward/pallas_call | solution.py:668
  518.8 7.1 collective-permute-done.46
  541.3 5.5 collective-permute-start.50
  548.1 6.6 conv_backward.1
  554.7 10.4 %back_product.5 = bf16[768,2560]{1,0:T(8,128)(2,1)} custom-call(bf16[768,640]{1,0:T(8,128)(2,1)} %get-tuple-element.366.refs_0_, bf16[768,640]{1,0:T(8,128)(2,1)} %get-tuple-element.368.refs_1_, bf16[2560,640]{1,0:T(8,128)(2,1)} %assemble.5.refs_2_, bf16[2560,640]{1,0:T(8,128)(2,1)} %assemble.4.refs_3_), custom_call_target="tpu_custom_call" | custom-call | flops 5033164800 | bytes 6553600 | tf_op jit(solution)/shard_map/back_product/pallas_call | solution.py:871
  573.2 6.8 collective-permute-start.54
  591.4 7.3 collective-permute-done.53
  606.3 4.9 collective-permute-start.58
  615.8 10.8 %plain_grad.7 = bf16[2560,1408]{1,0:T(8,128)(2,1)} custom-call(bf16[768,2560]{1,0:T(8,128)(2,1)} %slice.296.left_ref, bf16[768,640]{1,0:T(8,128)(2,1)} %get-tuple-element.366.refs_0_, bf16[768,640]{1,0:T(8,128)(2,1)} %get-tuple-element.368.refs_1_, bf16[2560,128]{1,0:T(8,128)(2,1)} %convert_element_type.335.refs_2_), custom_call_target="tpu_custom_call" | custom-call | flops 5536481280 | bytes 13303808 | tf_op jit(solution)/shard_map/plain_grad/pallas_call | solution.py:907
  626.6 6.4 collective-permute-done.58
  633.0 8.2 %collective-permute-done.57 = bf16[192,2560]{1,0:T(8,128)(2,1)} collective-permute-done((bf16[192,2560]{1,0:T(8,128)(2,1)}, bf16[192,2560]{1,0:T(8,128)(2,1)}, u32[]{:S(2)}, u32[]{:S(2)}) %collective-permute-start.57) | collective-permute-done | bytes 983072 | tf_op jit(solution)/shard_map/ppermute | solution.py:231
  646.0 5.5 collective-permute-start.60
  652.9 5.0 collective-permute-done.63
  657.9 4.8 collective-permute-done.64
  662.8 6.9 collective-permute-done.61
  677.9 6.0 collective-permute-start.65
  685.0 17.5 %collective-permute-done.67 = f32[8,640]{1,0:T(8,128)S(1)} collective-permute-done((f32[8,640]{1,0:T(8,128)S(1)}, f32[8,640]{1,0:T(8,128)S(1)}, u32[]{:S(2)}, u32[]{:S(2)}) %collective-permute-start.67) | collective-permute-done | bytes 20512 | tf_op jit(solution)/shard_map/ppermute | solution.py:50
  720.4 15.9 %collective-permute-done.69 = bf16[192,2560]{1,0:T(8,128)(2,1)} collective-permute-done((bf16[192,2560]{1,0:T(8,128)(2,1)S(1)}, bf16[192,2560]{1,0:T(8,128)(2,1)}, u32[]{:S(2)}, u32[]{:S(2)}) %collective-permute-start.69) | collective-permute-done | bytes 983072 | tf_op jit(solution)/shard_map/ppermute | solution.py:231
  745.4 6.9 collective-permute-start.75
  762.6 5.2 collective-permute-start.77
  (497 shorter events, 296.1 us)
Async XLA Ops:
  7.2 67.6 %all-gather.4.cloned.1.call-start = ((), (), s32[]{:S(2)}) async-start(), calls=%async_computation.5 | async-start | bytes 1474560 | tf_op jit(solution)/shard_map/all_gather | solution.py:1006
  18.2 30.4 %collective-permute-start.8 = (bf16[320,640]{1,0:T(8,128)(2,1)}, bf16[320,640]{1,0:T(8,128)(2,1)}, u32[]{:S(2)}, u32[]{:S(2)}) collective-permute-start(bf16[320,640]{1,0:T(8,128)(2,1)} %maximum_select_fusion.1), channel_id=1, source_target_pairs={{1,0},{2,1},{3,2},{5,4},{6,5},{7,6},{9,8},{10,9},{11,10},{13,12},{... | collective-permute-start | bytes 1228808 | tf_op jit(solution)/shard_map/ppermute | solution.py:231
  25.7 22.9 %collective-permute-start.7 = (bf16[320,640]{1,0:T(8,128)(2,1)}, bf16[320,640]{1,0:T(8,128)(2,1)}, u32[]{:S(2)}, u32[]{:S(2)}) collective-permute-start(bf16[320,640]{1,0:T(8,128)(2,1)} %maximum_select_fusion.1), channel_id=1, source_target_pairs={{0,1},{1,2},{2,3},{4,5},{5,6},{6,7},{8,9},{9,10},{10,11},{12,13},{... | collective-permute-start | bytes 1228808 | tf_op jit(solution)/shard_map/ppermute | solution.py:230
  32.9 134.5 %all-gather.6.cloned.1.call-start = ((), (), s32[]{:S(2)}) async-start(), calls=%async_computation.6 | async-start | bytes 11059200 | tf_op jit(solution)/shard_map/all_gather | solution.py:1033
  37.7 26.1 %collective-permute-start.5 = (bf16[640,640]{1,0:T(8,128)(2,1)}, bf16[640,640]{1,0:T(8,128)(2,1)}, u32[]{:S(2)}, u32[]{:S(2)}) collective-permute-start(bf16[640,640]{1,0:T(8,128)(2,1)} %pad_maximum_fusion.12), channel_id=1, source_target_pairs={{0,8},{8,0},{1,9},{9,1},{2,10},{10,2},{3,11},{11,3},{4,12},{12,4},... | collective-permute-start | bytes 2457608 | tf_op jit(solution)/shard_map/ppermute | solution.py:36
  40.9 25.1 %collective-permute-start.4 = (bf16[640,640]{1,0:T(8,128)(2,1)}, bf16[640,640]{1,0:T(8,128)(2,1)}, u32[]{:S(2)}, u32[]{:S(2)}) collective-permute-start(bf16[640,640]{1,0:T(8,128)(2,1)} %pad_maximum_fusion.11), channel_id=1, source_target_pairs={{0,16},{16,0},{1,17},{17,1},{2,18},{18,2},{3,19},{19,3},{4,20},{20... | collective-permute-start | bytes 2457608 | tf_op jit(solution)/shard_map/ppermute | solution.py:36
  66.0 217.4 %all-gather.8.cloned.1.call-start = ((), (), s32[]{:S(2)}) async-start(), calls=%async_computation.7 | async-start | bytes 22118400 | tf_op jit(solution)/shard_map/all_gather | solution.py:1068
  67.5 22.5 %collective-permute-start.10 = (bf16[1280,640]{1,0:T(8,128)(2,1)S(1)}, bf16[1280,640]{1,0:T(8,128)(2,1)}, u32[]{:S(2)}, u32[]{:S(2)}) collective-permute-start(bf16[1280,640]{1,0:T(8,128)(2,1)S(1)} %pad_maximum_fusion.7.refs_0_), channel_id=1, source_target_pairs={{0,4},{4,0},{1,5},{5,1},{2,6},{6,2},{3,7},{7,3},{8,12},{12,8},{9,1... | collective-permute-start | bytes 4915208 | tf_op jit(solution)/shard_map/ppermute | solution.py:36
  90.0 23.6 %collective-permute-start.13 = (bf16[320,640]{1,0:T(8,128)(2,1)}, bf16[320,640]{1,0:T(8,128)(2,1)}, u32[]{:S(2)}, u32[]{:S(2)}) collective-permute-start(bf16[320,640]{1,0:T(8,128)(2,1)} %collective-permute-done.11), channel_id=1, source_target_pairs={{2,3},{6,7},{10,11},{14,15},{18,19},{22,23},{26,27},{30,31}} | collective-permute-start | bytes 1228808 | tf_op jit(solution)/shard_map/ppermute | solution.py:230
  91.4 22.2 %collective-permute-start.14 = (bf16[320,640]{1,0:T(8,128)(2,1)}, bf16[320,640]{1,0:T(8,128)(2,1)}, u32[]{:S(2)}, u32[]{:S(2)}) collective-permute-start(bf16[320,640]{1,0:T(8,128)(2,1)} %collective-permute-done.12), channel_id=1, source_target_pairs={{1,0},{5,4},{9,8},{13,12},{17,16},{21,20},{25,24},{29,28}} | collective-permute-start | bytes 1228808 | tf_op jit(solution)/shard_map/ppermute | solution.py:231
  116.7 31.2 %collective-permute-start.15 = (bf16[320,1280]{1,0:T(8,128)(2,1)}, bf16[320,1280]{1,0:T(8,128)(2,1)}, u32[]{:S(2)}, u32[]{:S(2)}) collective-permute-start(bf16[320,1280]{1,0:T(8,128)(2,1)} %pad_maximum_fusion.13), channel_id=1, source_target_pairs={{0,8},{8,0},{1,9},{9,1},{2,10},{10,2},{3,11},{11,3},{4,12},{12,4},... | collective-permute-start | bytes 2457608 | tf_op jit(solution)/shard_map/ppermute | solution.py:36
  119.1 28.9 %collective-permute-start.16 = (bf16[320,1280]{1,0:T(8,128)(2,1)}, bf16[320,1280]{1,0:T(8,128)(2,1)}, u32[]{:S(2)}, u32[]{:S(2)}) collective-permute-start(bf16[320,1280]{1,0:T(8,128)(2,1)} %pad_maximum_fusion.14), channel_id=1, source_target_pairs={{0,16},{16,0},{1,17},{17,1},{2,18},{18,2},{3,19},{19,3},{4,20},{20... | collective-permute-start | bytes 2457608 | tf_op jit(solution)/shard_map/ppermute | solution.py:36
  148.0 379.2 %reduce-scatter.5.cloned.1.call-start = ((), (), s32[]{:S(2)}) async-start(), calls=%async_computation.8 | async-start | bytes 22118400 | tf_op jit(solution)/shard_map/reduce_scatter | solution.py:1108
  149.3 32.2 %collective-permute-start.20 = (bf16[320,1280]{1,0:T(8,128)(2,1)}, bf16[320,1280]{1,0:T(8,128)(2,1)}, u32[]{:S(2)}, u32[]{:S(2)}) collective-permute-start(bf16[320,1280]{1,0:T(8,128)(2,1)} %pad_maximum_fusion.13), channel_id=1, source_target_pairs={{0,16},{16,0},{1,17},{17,1},{2,18},{18,2},{3,19},{19,3},{4,20},{20... | collective-permute-start | bytes 2457608 | tf_op jit(solution)/shard_map/ppermute | solution.py:36
  151.1 31.9 %collective-permute-start.21 = (bf16[320,1280]{1,0:T(8,128)(2,1)}, bf16[320,1280]{1,0:T(8,128)(2,1)}, u32[]{:S(2)}, u32[]{:S(2)}) collective-permute-start(bf16[320,1280]{1,0:T(8,128)(2,1)} %pad_maximum_fusion.14), channel_id=1, source_target_pairs={{0,8},{8,0},{1,9},{9,1},{2,10},{10,2},{3,11},{11,3},{4,12},{12,4},... | collective-permute-start | bytes 2457608 | tf_op jit(solution)/shard_map/ppermute | solution.py:36
  153.5 29.5 %collective-permute-start.23 = (bf16[768,640]{1,0:T(8,128)(2,1)S(1)}, bf16[768,640]{1,0:T(8,128)(2,1)S(1)}, u32[]{:S(2)}, u32[]{:S(2)}) collective-permute-start(bf16[768,640]{1,0:T(8,128)(2,1)S(1)} %copy-done.47), channel_id=1, source_target_pairs={{1,0},{2,1},{3,2},{5,4},{6,5},{7,6},{9,8},{10,9},{11,10},{13,12},{... | collective-permute-start | bytes 2949128 | tf_op jit(solution)/shard_map/ppermute | solution.py:231
  154.8 28.2 %collective-permute-start.22 = (bf16[768,640]{1,0:T(8,128)(2,1)S(1)}, bf16[768,640]{1,0:T(8,128)(2,1)S(1)}, u32[]{:S(2)}, u32[]{:S(2)}) collective-permute-start(bf16[768,640]{1,0:T(8,128)(2,1)S(1)} %copy-done.47), channel_id=1, source_target_pairs={{0,1},{1,2},{2,3},{4,5},{5,6},{6,7},{8,9},{9,10},{10,11},{12,13},{... | collective-permute-start | bytes 2949128 | tf_op jit(solution)/shard_map/ppermute | solution.py:230
  183.0 32.5 %collective-permute-start.26 = (bf16[768,640]{1,0:T(8,128)(2,1)S(1)}, bf16[768,640]{1,0:T(8,128)(2,1)}, u32[]{:S(2)}, u32[]{:S(2)}) collective-permute-start(bf16[768,640]{1,0:T(8,128)(2,1)S(1)} %collective-permute-done.22), channel_id=1, source_target_pairs={{1,2},{2,3},{5,6},{6,7},{9,10},{10,11},{13,14},{14,15},{17,18},{18... | collective-permute-start | bytes 2949128 | tf_op jit(solution)/shard_map/ppermute | solution.py:230
  184.6 30.9 %collective-permute-start.27 = (bf16[768,640]{1,0:T(8,128)(2,1)S(1)}, bf16[768,640]{1,0:T(8,128)(2,1)}, u32[]{:S(2)}, u32[]{:S(2)}) collective-permute-start(bf16[768,640]{1,0:T(8,128)(2,1)S(1)} %collective-permute-done.23), channel_id=1, source_target_pairs={{1,0},{2,1},{5,4},{6,5},{9,8},{10,9},{13,12},{14,13},{17,16},{18,1... | collective-permute-start | bytes 2949128 | tf_op jit(solution)/shard_map/ppermute | solution.py:231
  186.3 27.4 %collective-permute-start.24 = (bf16[320,1280]{1,0:T(8,128)(2,1)}, bf16[320,1280]{1,0:T(8,128)(2,1)S(1)}, u32[]{:S(2)}, u32[]{:S(2)}) collective-permute-start(bf16[320,1280]{1,0:T(8,128)(2,1)} %collective-permute-done.15), channel_id=1, source_target_pairs={{0,16},{16,0},{1,17},{17,1},{2,18},{18,2},{3,19},{19,3},{4,20},{20... | collective-permute-start | bytes 2457608 | tf_op jit(solution)/shard_map/ppermute | solution.py:36
  186.4 29.1 %collective-permute-start.25 = (bf16[320,1280]{1,0:T(8,128)(2,1)}, bf16[320,1280]{1,0:T(8,128)(2,1)S(1)}, u32[]{:S(2)}, u32[]{:S(2)}) collective-permute-start(bf16[320,1280]{1,0:T(8,128)(2,1)} %collective-permute-done.16), channel_id=1, source_target_pairs={{0,8},{8,0},{1,9},{9,1},{2,10},{10,2},{3,11},{11,3},{4,12},{12,4},... | collective-permute-start | bytes 2457608 | tf_op jit(solution)/shard_map/ppermute | solution.py:36
  226.2 26.4 %collective-permute-start.31 = (bf16[768,640]{1,0:T(8,128)(2,1)}, bf16[768,640]{1,0:T(8,128)(2,1)}, u32[]{:S(2)}, u32[]{:S(2)}) collective-permute-start(bf16[768,640]{1,0:T(8,128)(2,1)} %collective-permute-done.27), channel_id=1, source_target_pairs={{1,0},{5,4},{9,8},{13,12},{17,16},{21,20},{25,24},{29,28}} | collective-permute-start | bytes 2949128 | tf_op jit(solution)/shard_map/ppermute | solution.py:231
  331.2 25.5 %collective-permute-start.32 = (bf16[192,2560]{1,0:T(8,128)(2,1)S(1)}, bf16[192,2560]{1,0:T(8,128)(2,1)S(1)}, u32[]{:S(2)}, u32[]{:S(2)}) collective-permute-start(bf16[192,2560]{1,0:T(8,128)(2,1)S(1)} %get-tuple-element.282), channel_id=1, source_target_pairs={{0,1},{4,5},{8,9},{12,13},{16,17},{20,21},{24,25},{28,29}} | collective-permute-start | bytes 2949128 | tf_op jit(solution)/shard_map/ppermute | solution.py:210
  332.6 23.2 %collective-permute-start.33 = (bf16[192,2560]{1,0:T(8,128)(2,1)}, bf16[192,2560]{1,0:T(8,128)(2,1)S(1)}, u32[]{:S(2)}, u32[]{:S(2)}) collective-permute-start(bf16[192,2560]{1,0:T(8,128)(2,1)} %get-tuple-element.283), channel_id=1, source_target_pairs={{3,2},{7,6},{11,10},{15,14},{19,18},{23,22},{27,26},{31,30}} | collective-permute-start | bytes 2949128 | tf_op jit(solution)/shard_map/ppermute | solution.py:213
  359.0 24.5 %collective-permute-start.34 = (bf16[192,2560]{1,0:T(8,128)(2,1)S(1)}, bf16[192,2560]{1,0:T(8,128)(2,1)}, u32[]{:S(2)}, u32[]{:S(2)}) collective-permute-start(bf16[192,2560]{1,0:T(8,128)(2,1)S(1)} %get-tuple-element.291), channel_id=1, source_target_pairs={{0,1},{1,2},{4,5},{5,6},{8,9},{9,10},{12,13},{13,14},{16,17},{17,1... | collective-permute-start | bytes 2949128 | tf_op jit(solution)/shard_map/ppermute | solution.py:210
  386.8 26.8 %collective-permute-start.37 = (bf16[192,2560]{1,0:T(8,128)(2,1)}, bf16[192,2560]{1,0:T(8,128)(2,1)S(1)}, u32[]{:S(2)}, u32[]{:S(2)}) collective-permute-start(bf16[192,2560]{1,0:T(8,128)(2,1)} %get-tuple-element.303), channel_id=1, source_target_pairs={{1,0},{2,1},{3,2},{5,4},{6,5},{7,6},{9,8},{10,9},{11,10},{13,12},{... | collective-permute-start | bytes 2949128 | tf_op jit(solution)/shard_map/ppermute | solution.py:213
  388.1 26.4 %collective-permute-start.36 = (bf16[192,2560]{1,0:T(8,128)(2,1)S(1)}, bf16[192,2560]{1,0:T(8,128)(2,1)S(1)}, u32[]{:S(2)}, u32[]{:S(2)}) collective-permute-start(bf16[192,2560]{1,0:T(8,128)(2,1)S(1)} %get-tuple-element.301), channel_id=1, source_target_pairs={{0,1},{1,2},{2,3},{4,5},{5,6},{6,7},{8,9},{9,10},{10,11},{12,13},{... | collective-permute-start | bytes 2949128 | tf_op jit(solution)/shard_map/ppermute | solution.py:210
  427.3 40.3 %all-to-all-start = ((bf16[192,4,640]{2,0,1:T(8,128)(2,1)}), bf16[192,4,640]{2,0,1:T(8,128)(2,1)S(1)}, u32[]{:S(2)}, u32[]{:S(2)}) async-start(bf16[192,4,640]{2,0,1:T(8,128)(2,1)} %bitcast.37), calls=%async_computation | async-start | bytes 1966080 | tf_op jit(solution)/shard_map/all_to_all | solution.py:1139
  432.5 194.1 %reduce-scatter.7.cloned.1.call-start = ((), (), s32[]{:S(2)}) async-start(), calls=%async_computation.9 | async-start | bytes 14745600 | tf_op jit(solution)/shard_map/reduce_scatter | solution.py:1108
  436.2 31.4 %collective-permute-start.38 = (bf16[192,2560]{1,0:T(8,128)(2,1)}, bf16[192,2560]{1,0:T(8,128)(2,1)S(1)}, u32[]{:S(2)}, u32[]{:S(2)}) collective-permute-start(bf16[192,2560]{1,0:T(8,128)(2,1)} %get-tuple-element.452), channel_id=1, source_target_pairs={{0,1},{4,5},{8,9},{12,13},{16,17},{20,21},{24,25},{28,29}} | collective-permute-start | bytes 2949128 | tf_op jit(solution)/shard_map/ppermute | solution.py:210
  468.6 202.4 %reduce-scatter.9.cloned.1.call-start = ((), (), s32[]{:S(2)}) async-start(), calls=%async_computation.10 | async-start | bytes 11059200 | tf_op jit(solution)/shard_map/reduce_scatter | solution.py:1108
  473.5 22.6 %collective-permute-start.43 = (bf16[192,2560]{1,0:T(8,128)(2,1)}, bf16[192,2560]{1,0:T(8,128)(2,1)}, u32[]{:S(2)}, u32[]{:S(2)}) collective-permute-start(bf16[192,2560]{1,0:T(8,128)(2,1)} %get-tuple-element.450), channel_id=1, source_target_pairs={{0,1},{1,2},{4,5},{5,6},{8,9},{9,10},{12,13},{13,14},{16,17},{17,1... | collective-permute-start | bytes 2949128 | tf_op jit(solution)/shard_map/ppermute | solution.py:210
  500.1 25.8 %collective-permute-start.46 = (bf16[192,2560]{1,0:T(8,128)(2,1)}, bf16[192,2560]{1,0:T(8,128)(2,1)S(1)}, u32[]{:S(2)}, u32[]{:S(2)}) collective-permute-start(bf16[192,2560]{1,0:T(8,128)(2,1)} %get-tuple-element.447), channel_id=1, source_target_pairs={{1,0},{2,1},{3,2},{5,4},{6,5},{7,6},{9,8},{10,9},{11,10},{13,12},{... | collective-permute-start | bytes 2949128 | tf_op jit(solution)/shard_map/ppermute | solution.py:213
  501.4 25.8 %collective-permute-start.45 = (bf16[192,2560]{1,0:T(8,128)(2,1)}, bf16[192,2560]{1,0:T(8,128)(2,1)S(1)}, u32[]{:S(2)}, u32[]{:S(2)}) collective-permute-start(bf16[192,2560]{1,0:T(8,128)(2,1)} %get-tuple-element.448), channel_id=1, source_target_pairs={{0,1},{1,2},{2,3},{4,5},{5,6},{6,7},{8,9},{9,10},{10,11},{12,13},{... | collective-permute-start | bytes 2949128 | tf_op jit(solution)/shard_map/ppermute | solution.py:210
  527.2 226.9 %reduce-scatter.11.cloned.1.call-start = ((), (), s32[]{:S(2)}) async-start(), calls=%async_computation.11 | async-start | bytes 8110080 | tf_op jit(solution)/shard_map/reduce_scatter | solution.py:1108
  540.0 28.9 %collective-permute-start.51 = (bf16[192,2560]{1,0:T(8,128)(2,1)}, bf16[192,2560]{1,0:T(8,128)(2,1)}, u32[]{:S(2)}, u32[]{:S(2)}) collective-permute-start(bf16[192,2560]{1,0:T(8,128)(2,1)} %multiply_convert_fusion.1), channel_id=1, source_target_pairs={{1,0},{2,1},{3,2},{5,4},{6,5},{7,6},{9,8},{10,9},{11,10},{13,12},{... | collective-permute-start | bytes 2949128 | tf_op jit(solution)/shard_map/ppermute | solution.py:231
  541.3 27.6 %collective-permute-start.50 = (bf16[192,2560]{1,0:T(8,128)(2,1)}, bf16[192,2560]{1,0:T(8,128)(2,1)}, u32[]{:S(2)}, u32[]{:S(2)}) collective-permute-start(bf16[192,2560]{1,0:T(8,128)(2,1)} %multiply_convert_fusion.1), channel_id=1, source_target_pairs={{0,1},{1,2},{2,3},{4,5},{5,6},{6,7},{8,9},{9,10},{10,11},{12,13},{... | collective-permute-start | bytes 2949128 | tf_op jit(solution)/shard_map/ppermute | solution.py:230
  568.9 22.5 %collective-permute-start.52 = (bf16[192,2560]{1,0:T(8,128)(2,1)}, bf16[192,2560]{1,0:T(8,128)(2,1)}, u32[]{:S(2)}, u32[]{:S(2)}) collective-permute-start(bf16[192,2560]{1,0:T(8,128)(2,1)} %collective-permute-done.50), channel_id=1, source_target_pairs={{1,2},{2,3},{5,6},{6,7},{9,10},{10,11},{13,14},{14,15},{17,18},{18... | collective-permute-start | bytes 2949128 | tf_op jit(solution)/shard_map/ppermute | solution.py:230
  570.5 28.2 %collective-permute-start.53 = (bf16[192,2560]{1,0:T(8,128)(2,1)}, bf16[192,2560]{1,0:T(8,128)(2,1)}, u32[]{:S(2)}, u32[]{:S(2)}) collective-permute-start(bf16[192,2560]{1,0:T(8,128)(2,1)} %collective-permute-done.51), channel_id=1, source_target_pairs={{1,0},{2,1},{5,4},{6,5},{9,8},{10,9},{13,12},{14,13},{17,16},{18,1... | collective-permute-start | bytes 2949128 | tf_op jit(solution)/shard_map/ppermute | solution.py:231
  573.2 28.7 %collective-permute-start.54 = (bf16[192,2560]{1,0:T(8,128)(2,1)}, bf16[192,2560]{1,0:T(8,128)(2,1)S(1)}, u32[]{:S(2)}, u32[]{:S(2)}) collective-permute-start(bf16[192,2560]{1,0:T(8,128)(2,1)} %get-tuple-element.350), channel_id=1, source_target_pairs={{0,1},{4,5},{8,9},{12,13},{16,17},{20,21},{24,25},{28,29}} | collective-permute-start | bytes 2949128 | tf_op jit(solution)/shard_map/ppermute | solution.py:210
  606.3 26.7 %collective-permute-start.58 = (bf16[192,2560]{1,0:T(8,128)(2,1)}, bf16[192,2560]{1,0:T(8,128)(2,1)S(1)}, u32[]{:S(2)}, u32[]{:S(2)}) collective-permute-start(bf16[192,2560]{1,0:T(8,128)(2,1)} %get-tuple-element.361), channel_id=1, source_target_pairs={{0,1},{1,2},{4,5},{5,6},{8,9},{9,10},{12,13},{13,14},{16,17},{17,1... | collective-permute-start | bytes 2949128 | tf_op jit(solution)/shard_map/ppermute | solution.py:210
  612.0 29.2 %collective-permute-start.57 = (bf16[192,2560]{1,0:T(8,128)(2,1)}, bf16[192,2560]{1,0:T(8,128)(2,1)}, u32[]{:S(2)}, u32[]{:S(2)}) collective-permute-start(bf16[192,2560]{1,0:T(8,128)(2,1)} %collective-permute-done.53), channel_id=1, source_target_pairs={{1,0},{5,4},{9,8},{13,12},{17,16},{21,20},{25,24},{29,28}} | collective-permute-start | bytes 2949128 | tf_op jit(solution)/shard_map/ppermute | solution.py:231
  644.6 25.1 %collective-permute-start.61 = (bf16[192,2560]{1,0:T(8,128)(2,1)}, bf16[192,2560]{1,0:T(8,128)(2,1)S(1)}, u32[]{:S(2)}, u32[]{:S(2)}) collective-permute-start(bf16[192,2560]{1,0:T(8,128)(2,1)} %get-tuple-element.378), channel_id=1, source_target_pairs={{1,0},{2,1},{3,2},{5,4},{6,5},{7,6},{9,8},{10,9},{11,10},{13,12},{... | collective-permute-start | bytes 2949128 | tf_op jit(solution)/shard_map/ppermute | solution.py:213
  646.0 25.0 %collective-permute-start.60 = (bf16[192,2560]{1,0:T(8,128)(2,1)}, bf16[192,2560]{1,0:T(8,128)(2,1)}, u32[]{:S(2)}, u32[]{:S(2)}) collective-permute-start(bf16[192,2560]{1,0:T(8,128)(2,1)} %get-tuple-element.377), channel_id=1, source_target_pairs={{0,1},{1,2},{2,3},{4,5},{5,6},{6,7},{8,9},{9,10},{10,11},{12,13},{... | collective-permute-start | bytes 2949128 | tf_op jit(solution)/shard_map/ppermute | solution.py:210
  676.6 26.0 %collective-permute-start.66 = (bf16[192,2560]{1,0:T(8,128)(2,1)S(1)}, bf16[192,2560]{1,0:T(8,128)(2,1)S(1)}, u32[]{:S(2)}, u32[]{:S(2)}) collective-permute-start(bf16[192,2560]{1,0:T(8,128)(2,1)S(1)} %fusion.10), channel_id=1, source_target_pairs={{1,0},{2,1},{3,2},{5,4},{6,5},{7,6},{9,8},{10,9},{11,10},{13,12},{... | collective-permute-start | bytes 2949128 | tf_op jit(solution)/shard_map/ppermute | solution.py:231
  677.9 24.7 %collective-permute-start.65 = (bf16[192,2560]{1,0:T(8,128)(2,1)S(1)}, bf16[192,2560]{1,0:T(8,128)(2,1)}, u32[]{:S(2)}, u32[]{:S(2)}) collective-permute-start(bf16[192,2560]{1,0:T(8,128)(2,1)S(1)} %fusion.10), channel_id=1, source_target_pairs={{0,1},{1,2},{2,3},{4,5},{5,6},{6,7},{8,9},{9,10},{10,11},{12,13},{... | collective-permute-start | bytes 2949128 | tf_op jit(solution)/shard_map/ppermute | solution.py:230
  702.6 33.7 %collective-permute-start.68 = (bf16[192,2560]{1,0:T(8,128)(2,1)}, bf16[192,2560]{1,0:T(8,128)(2,1)}, u32[]{:S(2)}, u32[]{:S(2)}) collective-permute-start(bf16[192,2560]{1,0:T(8,128)(2,1)} %collective-permute-done.65), channel_id=1, source_target_pairs={{1,2},{2,3},{5,6},{6,7},{9,10},{10,11},{13,14},{14,15},{17,18},{18... | collective-permute-start | bytes 2949128 | tf_op jit(solution)/shard_map/ppermute | solution.py:230
  714.3 22.0 %collective-permute-start.69 = (bf16[192,2560]{1,0:T(8,128)(2,1)S(1)}, bf16[192,2560]{1,0:T(8,128)(2,1)}, u32[]{:S(2)}, u32[]{:S(2)}) collective-permute-start(bf16[192,2560]{1,0:T(8,128)(2,1)S(1)} %copy-done.45), channel_id=1, source_target_pairs={{1,0},{2,1},{5,4},{6,5},{9,8},{10,9},{13,12},{14,13},{17,16},{18,1... | collective-permute-start | bytes 2949128 | tf_op jit(solution)/shard_map/ppermute | solution.py:231
  (119 other events, 1317.0 us)
Sparse Core Ops, SparseCore 0:
  33.0 31.4 all-gather.3
  66.3 68.2 all-gather.5
  148.1 123.9 all-gather.7
  359.1 128.3 reduce-scatter.4
  490.9 95.3 reduce-scatter.6
  589.6 79.1 reduce-scatter.8
  672.4 65.5 reduce-scatter.10

commit v4 on v3

--- a/solution.py
+++ b/solution.py
@@ -148,27 +148,34 @@
     arrived = flip(held, 0)
     if not slow:
         arrived = yield arrived
-    whole = assemble([held, arrived], [masks, [mask | 1 for mask in masks]])
-    setattr(kept, name, whole if not slow else (yield whole))
-
-
-def assemble(sources, masks):
-    count, many = len(sources), sum(len(some) for some in masks)
-    rows, columns = sources[0].shape[0] // len(masks[0]), sources[0].shape[1]
+    group = [held, arrived], [masks, [mask | 1 for mask in masks]]
+    setattr(kept, name, (yield assemble([group])) if slow else group)
+
+
+def assemble(groups):
+    sources = [source for group, _ in groups for source in group]
+    count, many = len(sources), sum(len(some) for _, masks in groups for some in masks)
+    rows = sources[0].shape[0] // len(groups[0][1][0])
+    total = sum(len(some) for some in groups[0][1]) * rows
+    width = sum(group[0].shape[1] for group, _ in groups)
 
     def kernel(me_ref, *refs):
         target, sems = refs[count], refs[count + 1]
-        copies = []
-        for source, some in zip(refs, masks):
-            for n, mask in enumerate(some):
-                start = pl.multiple_of((me_ref[0] ^ mask) * rows, 16)
-                copies.append(
-                    pltpu.make_async_copy(
-                        source.at[pl.ds(n * rows, rows)],
-                        target.at[pl.ds(start, rows)],
-                        sems.at[len(copies)],
+        refs, copies, begin = list(refs), [], 0
+        for group, masks in groups:
+            columns = group[0].shape[1]
+            for some in masks:
+                source = refs.pop(0)
+                for n, mask in enumerate(some):
+                    start = pl.multiple_of((me_ref[0] ^ mask) * rows, 16)
+                    copies.append(
+                        pltpu.make_async_copy(
+                            source.at[pl.ds(n * rows, rows)],
+                            target.at[pl.ds(start, rows), pl.ds(begin, columns)],
+                            sems.at[len(copies)],
+                        )
                     )
-                )
+            begin += columns
         for copy in copies:
             copy.start()
         for copy in copies:
@@ -179,12 +186,10 @@
         in_specs=[pl.BlockSpec(memory_space=pltpu.SMEM)]
         + [pl.BlockSpec(memory_space=pl.ANY)] * count,
         out_specs=pl.BlockSpec(memory_space=pltpu.VMEM),
-        out_shape=jax.ShapeDtypeStruct((many * rows, columns), sources[0].dtype),
+        out_shape=jax.ShapeDtypeStruct((total, width), sources[0].dtype),
         scratch_shapes=[pltpu.SemaphoreType.DMA((many,))],
         compiler_params=pltpu.CompilerParams(vmem_limit_bytes=VMEM_MIB * MIB),
-        cost_estimate=cost(
-            flops=0, bytes_accessed=4 * many * rows * columns, transcendentals=0
-        ),
+        cost_estimate=cost(flops=0, bytes_accessed=4 * total * width, transcendentals=0),
         name="assemble",
     )(cube_index().astype(jnp.int32).reshape(1), *sources)
 
@@ -330,6 +335,10 @@
     return pl.BlockSpec((ROWS, columns), lambda i: (i, 0))
 
 
+def branch_spec(rows, channels):
+    return pl.BlockSpec((rows, channels), lambda i: (0, 1), pipeline_mode=pl.Buffered(1))
+
+
 SMEM_SPEC = pl.BlockSpec(memory_space=pltpu.SMEM)
 
 
@@ -339,11 +348,11 @@
     )
 
 
-def recur_forward(info, branch, extra, taps, gates_in, gates_decay, vectors):
-    channels = branch.shape[1]
+def recur_forward(info, both, extra, taps, gates_in, gates_decay, vectors):
+    channels = both.shape[1] // 2
     reach = channels + HALF
-    lead = branch.shape[0] % ROWS
-    tokens = branch.shape[0] - lead
+    tokens = both.shape[0] // ROWS * ROWS
+    last = both.shape[0] - 8
     tiles = ROWS // 8
 
     def kernel(
@@ -366,10 +375,11 @@
 
             def tile(t, _):
                 base = pl.multiple_of(t * 8, 8)
-                place = pl.multiple_of(lead + i * ROWS + base, 8)
+                place = pl.multiple_of(i * ROWS + base, 8)
+                earlier_place = jnp.where(place == 0, last, place - 8)
                 since = since_start(info_ref, i * ROWS + base)
                 current = source[pl.ds(place, 8), :]
-                before = source[pl.ds(pl.multiple_of(place - 8, 8), 8), :]
+                before = source[pl.ds(pl.multiple_of(earlier_place, 8), 8), :]
                 total = taps_ref[4:5, columns] + taps_ref[0:1, columns] * current
                 for k in range(1, 4):
                     earlier = moved(current, before, k, row_part)
@@ -415,10 +425,10 @@
                 jnp.broadcast_to(b[7:8, :], b.shape),
             )
 
-        last = lax.fori_loop(0, tiles, scan_tile, (carry_p[...], carry_s[...]), unroll=4)
-        carry_p[...] = last[0]
-        carry_s[...] = last[1]
-        ends_ref[...] = jnp.where(row == 0, last[0], last[1])
+        final = lax.fori_loop(0, tiles, scan_tile, (carry_p[...], carry_s[...]), unroll=4)
+        carry_p[...] = final[0]
+        carry_s[...] = final[1]
+        ends_ref[...] = jnp.where(row == 0, final[0], final[1])
 
     narrow = jax.ShapeDtypeStruct((tokens, channels), F32)
     return pl.pallas_call(
@@ -426,7 +436,7 @@
         grid=(tokens // ROWS,),
         in_specs=[
             SMEM_SPEC,
-            const_spec(branch.shape),
+            branch_spec(both.shape[0], channels),
             const_spec(extra.shape),
             const_spec((8, reach)),
             const_spec((BLOCK, channels)),
@@ -451,7 +461,7 @@
             transcendentals=6 * tokens * channels,
         ),
         name="recur_forward",
-    )(info, branch, extra, taps, gates_in, gates_decay, vectors)
+    )(info, both, extra, taps, gates_in, gates_decay, vectors)
 
 
 def mix_forward(prod, state, gate_pre, arriving):
@@ -490,11 +500,18 @@
 
     def kernel(*refs):
         out_refs = refs[many : many + wides]
-        res_ref, middle_ref = refs[many + wides :]
+        res_ref, middle_ref = refs[many + wides : many + wides + 2]
+        joined = refs[many + wides + 2 :]
+
+        @pl.when(pl.program_id(0) == 0)
+        def _():
+            for n in range(many):
+                begin = n % each * channels
+                joined[n // each][:, begin : begin + channels] = refs[n][...]
+
         total = res_ref[...].astype(F32)
-        for n in range(many):
-            begin = n % each * channels
-            total = total + dot_nt(refs[n][...], out_refs[n // each][:, begin : begin + channels])
+        for n in range(wides):
+            total = total + dot_nt(joined[n][...], out_refs[n][...])
         middle_ref[...] = total
 
     columns = pl.BlockSpec((tokens, cut), lambda i: (0, i))
@@ -506,6 +523,7 @@
         + [columns],
         out_specs=columns,
         out_shape=jax.ShapeDtypeStruct((tokens, width), F32),
+        scratch_shapes=[pltpu.VMEM((tokens, each * channels), BF16)] * wides,
         compiler_params=params(),
         cost_estimate=cost(
             flops=2 * many * tokens * width * channels,
@@ -707,10 +725,10 @@
     )
 
 
-def conv_backward(info, own, coming, trail, branch, taps):
+def conv_backward(info, own, coming, trail, both, taps):
     tokens, channels = own.shape
     tiles = ROWS // 8
-    lead = branch.shape[0] - tokens
+    end = both.shape[0] - 8
     borrowed = coming.shape[1]
 
     def kernel(
@@ -741,9 +759,9 @@
             since = since_start(info_ref, begin)
             since_next = since_start(info_ref, begin + 8)
             here, next_rows = cot[pl.ds(local, 8), :], cot[pl.ds(local + 8, 8), :]
-            place = pl.multiple_of(lead + begin, 8)
-            values = branch_ref[pl.ds(place, 8), :]
-            last = branch_ref[pl.ds(pl.multiple_of(place - 8, 8), 8), :]
+            values = branch_ref[pl.ds(begin, 8), :]
+            earlier_place = pl.multiple_of(jnp.where(begin == 0, end, begin - 8), 8)
+            last = branch_ref[pl.ds(earlier_place, 8), :]
             total = taps_ref[0:1, :channels] * here
             sums = [carry[0] + here * values]
             for k in range(1, 4):
@@ -774,7 +792,7 @@
             back(channels),
             back(borrowed),
             const_spec((8, channels)),
-            const_spec(branch.shape),
+            branch_spec(both.shape[0], channels),
             const_spec((8, taps.shape[1])),
         ],
         out_specs=[back(channels), pl.BlockSpec((40, channels), lambda i: (0, 0))],
@@ -792,7 +810,7 @@
             flops=40 * tokens * channels, bytes_accessed=8 * MIB, transcendentals=0
         ),
         name="conv_backward",
-    )(info, own, coming, trail, branch, taps)
+    )(info, own, coming, trail, both, taps)
 
 
 def hidden_forward(normed, weights, hidden_cot):
@@ -1006,7 +1024,7 @@
         kept.extra = lax.all_gather(extra, every, axis=0, tiled=True)
         borrowed, kept.normed = yield (
             partner(own_taps[:, channels - HALF :]),
-            pre_norm(jnp.concatenate([earlier, residual])),
+            pre_norm(jnp.concatenate([residual, earlier])),
         )
         kept.taps = jnp.concatenate([own_taps, borrowed], axis=1)
 
@@ -1046,19 +1064,17 @@
 
     def recur():
         normed = kept.normed
-        kept.branch, kept.gate_pre = yield (
-            dot(normed, kept.recur), dot(normed[lead:], kept.gate)
-        )
+        kept.first = assemble([kept.gate, kept.recur])
+        kept.first, kept.both = yield kept.first, dot(normed, kept.first)
         gates = kept.extra[:, HALF:].reshape(1 << cube_bits(), 2, -1, channels)
         kept.gates = gate_weights(gates, 0), gate_weights(gates, 1)
         kept.forward = yield recur_forward(
-            info, kept.branch, dot(normed, kept.extra[:, :HALF]), kept.taps,
-            *kept.gates, vectors,
+            info, kept.both, dot(normed, kept.extra[:, :HALF]), kept.taps, *kept.gates, vectors
         )
         *_, prod, state, ends = kept.forward
         arriving = carried(ends, False)
         kept.arriving, (kept.states, kept.mixed) = yield (
-            arriving, mix_forward(prod, state, kept.gate_pre, arriving)
+            arriving, mix_forward(prod, state, kept.both, arriving)
         )
         kept.mixed_all = yield from line_gather(win, kept.mixed)
 
@@ -1142,7 +1158,7 @@
             cot, gain, mixed_cot, out_whole
         )
         gate_pre_cot, rev_prod, rev_state, rev_ends = mix_backward(
-            mixed_cot, kept.gate_pre, kept.states, decays
+            mixed_cot, kept.both, kept.states, decays
         )
         kept.gate_pre_cot, rev_prod, rev_state, returning = yield (
             gate_pre_cot, rev_prod, rev_state, carried(rev_ends, True)
@@ -1156,15 +1172,15 @@
         coming = partner(going)
         trail = shifted(own[:8], -1)
         trail_coming = shifted_partner(going[:16])[:8].astype(F32)
-        kept.trail = trail
+        kept.coming = coming
         trail = jnp.concatenate(
             [trail[:, : channels - HALF], trail[:, channels - HALF :] + trail_coming], axis=1
         )
         branch_low, conv_sums = conv_backward(
-            info, own, coming, trail, kept.branch, kept.taps
+            info, own, coming, trail, kept.both, kept.taps
         )
         part = back_product(
-            [kept.gate_pre_cot, branch_low], [(kept.gate, 0), (kept.recur, 0)]
+            [kept.gate_pre_cot, branch_low], [(kept.first, 0), (kept.first, 1)]
         )
         values = residual.astype(F32)
         gain = jnp.stack([jnp.sum(part.astype(F32) * values * norm_scale(values), axis=0), gain])
@@ -1185,7 +1201,7 @@
     def finish_output():
         total = my_rows(kept.middle) + kept.down_sum
         kept.output = yield from line_gather(
-            None, (my_rows(live) * total).astype(BF16), kept.trail
+            None, (my_rows(live) * total).astype(BF16), kept.coming
         )
 
     win.step((1, recur_back()), (1, sum_down()))
@@ -1234,7 +1250,7 @@
         kept.out_grad = yield from line_sum(None, jnp.concatenate(parts))
 
     def first_operands():
-        return kept.normed[lead:], (kept.gate_pre_cot, kept.branch_low), kept.small
+        return kept.normed[:tokens], (kept.gate_pre_cot, kept.branch_low), kept.small
 
     win.step((1, finish()), (2, small_grads()))
     win.step((2, plain_weight_grad("first_grad", first_operands, 3)))

time: 793 us -> 795 us (level)
    pallas_call x4 -> x3, Pallas kernels: 20.1 us -> 18.3 us  [assemble(): pl.pallas_call(kernel, in_specs=[pl.BlockSpec(memory_space=pltpu.SMEM)] +...]
    dot_general x5 -> x4, matrix products: 16 us -> 14.6 us  [dot(): return jnp.dot(a, b, preferred_element_type=F32)]
where the time goes in v4:
time: 795 us; the launch traced here: 782 us
  Pallas kernels  218 us (27%)
  waiting for transfers between devices  191 us (24%)
  starting transfers between devices  162 us (20%)
  other arithmetic  131 us (16%)
  local copies, waits for them, and re-layouts  40.3 us (5%)
  matrix products  23.1 us (3%)
  between operations  16.6 us (2%)
    ppermute x12, starting transfers between devices, line_sum(): lax.ppermute(rightward, 'tp', [(s, s + 1) for s in range(min(step, count...  56.7 us
    ppermute x17, waiting for transfers between devices, flip(): lax.ppermute(value, axis, [(i, i ^ 1 << position) for i in range(count)])  55.7 us
    pallas_call x4, Pallas kernels, plain_grad(): pl.pallas_call(kernel, grid=(width // cut,), in_specs=[pl.BlockSpec((toke...  54.6 us
    ppermute x12, waiting for transfers between devices, line_gather(): lax.ppermute(leftward, 'tp', [(s, s - 1) for s in range(1, count - step +...  53.8 us
    pallas_call x3, Pallas kernels, back_product(): pl.pallas_call(kernel, grid=(width // cut,), in_specs=[const_spec((rows,...  46.7 us
    ppermute x12, waiting for transfers between devices, line_sum(): lax.ppermute(rightward, 'tp', [(s, s + 1) for s in range(min(step, count...  38.1 us
    ppermute x12, starting transfers between devices, line_gather(): lax.ppermute(rightward, 'tp', [(s, s + 1) for s in range(step - 1, count...  33.2 us
    pallas_call x1, Pallas kernels, hidden_forward(): pl.pallas_call(kernel, grid=(many,), in_specs=[const_spec((rows, width)),...  23 us
  transfers between devices with their start and end apart: 87, of which 31 were waited for; matrix products, arithmetic and copies ran while one was open for 23% of the time, Pallas kernels for 22%

profile of v4, /device:TPU:0, one launch (start us, length us, event | category | flops | bytes accessed | tf_op | source)
XLA Modules:
  0.0 782.2 jit_solution(13591382074081602379)
XLA Ops:
  25.7 5.3 collective-permute-start.7
  49.9 13.9 %collective-permute-done.5 = bf16[640,640]{1,0:T(8,128)(2,1)} collective-permute-done((bf16[640,640]{1,0:T(8,128)(2,1)}, bf16[640,640]{1,0:T(8,128)(2,1)}, u32[]{:S(2)}, u32[]{:S(2)}) %collective-permute-start.5) | collective-permute-done | bytes 819232 | tf_op jit(solution)/shard_map/ppermute | solution.py:36
  81.2 8.8 %collective-permute-done.12 = bf16[320,640]{1,0:T(8,128)(2,1)} collective-permute-done((bf16[320,640]{1,0:T(8,128)(2,1)}, bf16[320,640]{1,0:T(8,128)(2,1)}, u32[]{:S(2)}, u32[]{:S(2)}) %collective-permute-start.12) | collective-permute-done | bytes 409632 | tf_op jit(solution)/shard_map/ppermute | solution.py:236
  92.7 6.8 assemble.3.refs_2_.refs_3_
  99.6 9.8 %fusion.53.branch_ref.gate_ref = f32[784,1280]{1,0:T(8,128)} fusion(bf16[784,2560]{1,0:T(8,128)(2,1)S(1)} %copy-done.4, bf16[2560,1280]{1,0:T(8,128)(2,1)} %assemble.3.refs_2_.refs_3_), kind=kOutput, calls=%fused_computation.196 | convolution fusion | flops 5138022400 | bytes 14581760 | tf_op jit(solution)/shard_map/dot_general | solution.py:319
  119.1 13.6 %recur_forward.1 = (f32[768,640]{1,0:T(8,128)}, bf16[768,768]{1,0:T(8,128)(2,1)}, f32[768,640]{1,0:T(8,128)}, f32[768,640]{1,0:T(8,128)}, f32[768,640]{1,0:T(8,1...) custom-call(s32[8]{0:T(128)} %pad_add_fusion.info_ref, f32[784,1280]{1,0:T(8,128)} %fusion.53.branch_ref.gate_ref, ...), custom_call_target="tpu_custom_call" | custom-call | flops 577044480 | bytes 20971520 | tf_op jit(solution)/shard_map/recur_forward/pallas_call | solution.py:434
  159.4 7.9 %convert_multiply_fusion.4 = (f32[768,2560]{1,0:T(8,128)}, bf16[768,2560]{1,0:T(8,128)(2,1)}) fusion(bf16[768,2560]{1,0:T(8,128)(2,1)} %param.20, f32[768]{0:T(1024)S(1)} %fusion.33), kind=kLoop, calls=%fused_computation.12 | loop fusion | flops 5898240 | bytes 15731712 | tf_op jit(solution)/shard_map/mul | solution.py:1086
  167.4 14.2 %down_backward.1.cot_ref = f32[768,1920]{1,0:T(8,128)} custom-call(bf16[768,2560]{1,0:T(8,128)(2,1)} %get-tuple-element.303.x_ref.left_ref, bf16[2560,1920]{1,0:T(8,128)(2,1)} %all-gather.6.cloned.1.call-done.weight_ref.refs_1_), custom_call_target="tpu_custom_call" | custom-call | flops 7549747200 | bytes 19660800 | tf_op jit(solution)/shard_map/down_backward/pallas_call | solution.py:860
  189.0 24.4 %collective-permute-done.24 = bf16[320,1280]{1,0:T(8,128)(2,1)S(1)} collective-permute-done((bf16[320,1280]{1,0:T(8,128)(2,1)}, bf16[320,1280]{1,0:T(8,128)(2,1)S(1)}, u32[]{:S(2)}, u32[]{:S(2)}) %collective-permute-start.24) | collective-permute-done | bytes 819232 | tf_op jit(solution)/shard_map/ppermute | solution.py:36
  218.8 5.9 pad_maximum_fusion.3.refs_0_
  227.6 5.6 assemble.5.refs_5_
  233.2 5.9 assemble.4.refs_4_
  239.1 13.5 %collective-permute-done.31 = bf16[768,640]{1,0:T(8,128)(2,1)} collective-permute-done((bf16[768,640]{1,0:T(8,128)(2,1)}, bf16[768,640]{1,0:T(8,128)(2,1)}, u32[]{:S(2)}, u32[]{:S(2)}) %collective-permute-start.31) | collective-permute-done | bytes 983072 | tf_op jit(solution)/shard_map/ppermute | solution.py:236
  257.0 17.0 %mix_product.1 = f32[768,2560]{1,0:T(8,128)} custom-call(bf16[768,640]{1,0:T(8,128)(2,1)} %get-tuple-element.293.refs_0_, bf16[768,640]{1,0:T(8,128)(2,1)} %get-tuple-element.294.refs_1_, bf16[768,640]{1,0:T(8,128)(2,1)} %get-tuple-element.295.refs_2_, bf16[768,640]{1,0:T(8,128)(2,1)} %get-tuple-element.296.refs_3_, bf16[2560,1280]{1,0:T(8,128)(2,1)} %assemble.4.refs_4_, ...), custom_call_target="tpu_custom_call" | custom-call | flops 10066329600 | bytes 31457280 | tf_op jit(solution)/shard_map/mix_product/pallas_call | solution.py:518
  282.1 23.0 %hidden_forward.1 = (bf16[768,1920]{1,0:T(8,128)(2,1)}, bf16[768,1920]{1,0:T(8,128)(2,1)}, bf16[768,1920]{1,0:T(8,128)(2,1)}) custom-call(bf16[768,2560]{1,0:T(8,128)(2,1)} %multiply_convert_fusion.x_ref.left_ref, bf16[2560,3840]{1,0:T(8,128)(2,1)} %all-gather.8.cloned.1.call-done.gate_ref.value_ref.refs_2_.refs_3_, ...), custom_call_target="tpu_custom_call" | custom-call | flops 15099494400 | bytes 19660800 | tf_op jit(solution)/shard_map/hidden_forward/pallas_call | solution.py:831
  305.1 22.2 %back_product.3 = bf16[768,2560]{1,0:T(8,128)(2,1)} custom-call(bf16[768,1920]{1,0:T(8,128)(2,1)} %get-tuple-element.285.refs_0_, bf16[768,1920]{1,0:T(8,128)(2,1)} %get-tuple-element.287.refs_1_, bf16[2560,3840]{1,0:T(8,128)(2,1)} %all-gather.8.cloned.1.call-done.gate_ref.value_ref.refs_2_.refs_3_, ...), custom_call_target="tpu_custom_call" | custom-call | flops 15099494400 | bytes 19660800 | tf_op jit(solution)/shard_map/back_product/pallas_call | solution.py:889
  331.9 22.3 %plain_grad.4 = bf16[2560,3840]{1,0:T(8,128)(2,1)} custom-call(bf16[768,2560]{1,0:T(8,128)(2,1)} %multiply_convert_fusion.x_ref.left_ref, bf16[768,1920]{1,0:T(8,128)(2,1)} %get-tuple-element.285.refs_0_, bf16[768,1920]{1,0:T(8,128)(2,1)} %get-tuple-element.287.refs_1_), custom_call_target="tpu_custom_call" | custom-call | flops 15099494400 | bytes 29491200 | tf_op jit(solution)/shard_map/plain_grad/pallas_call | solution.py:925
  360.8 14.0 %back_product.4 = bf16[768,2560]{1,0:T(8,128)(2,1)} custom-call(bf16[768,1920]{1,0:T(8,128)(2,1)} %get-tuple-element.304.refs_0_, bf16[2560,1920]{1,0:T(8,128)(2,1)} %all-gather.6.cloned.1.call-done.weight_ref.refs_1_), custom_call_target="tpu_custom_call" | custom-call | flops 7549747200 | bytes 9830400 | tf_op jit(solution)/shard_map/back_product/pallas_call | solution.py:889
  386.8 6.9 collective-permute-start.36
  396.0 12.5 %plain_grad.5 = bf16[2560,1920]{1,0:T(8,128)(2,1)} custom-call(bf16[768,2560]{1,0:T(8,128)(2,1)} %get-tuple-element.303.x_ref.left_ref, bf16[768,1920]{1,0:T(8,128)(2,1)} %get-tuple-element.304.refs_0_), custom_call_target="tpu_custom_call" | custom-call | flops 7549747200 | bytes 16711680 | tf_op jit(solution)/shard_map/plain_grad/pallas_call | solution.py:925
  416.2 5.0 fusion.42
  425.8 5.2 all-to-all-start
  438.6 8.6 %plain_grad.6 = bf16[2560,2560]{1,0:T(8,128)(2,1)} custom-call(bf16[192,2560]{1,0:T(8,128)(2,1)} %copy-done.15, bf16[192,2560]{1,0:T(8,128)(2,1)} %pad_maximum_fusion.9.refs_0_), custom_call_target="tpu_custom_call" | custom-call | flops 2516582400 | bytes 15073280 | tf_op jit(solution)/shard_map/plain_grad/pallas_call | solution.py:925
  447.2 18.8 %collective-permute-done.38 = bf16[192,2560]{1,0:T(8,128)(2,1)S(1)} collective-permute-done((bf16[192,2560]{1,0:T(8,128)(2,1)}, bf16[192,2560]{1,0:T(8,128)(2,1)S(1)}, u32[]{:S(2)}, u32[]{:S(2)}) %collective-permute-start.38) | collective-permute-done | bytes 983072 | tf_op jit(solution)/shard_map/ppermute | solution.py:215
  471.8 4.9 collective-permute-start.43
  476.7 7.4 mix_backward.1
  499.5 5.7 collective-permute-start.45
  505.2 11.8 %gates_backward.1 = (f32[768,640]{1,0:T(8,128)}, bf16[768,128]{1,0:T(8,128)(2,1)}, bf16[768,640]{1,0:T(8,128)(2,1)}, bf16[768,640]{1,0:T(8,128)(2,1)}, f32[24,640]{1,0:T(8,128)}) custom-call(s32[8]{0:T(128)} %pad_add_fusion.info_ref, f32[768,640]{1,0:T(8,128)} %get-tuple-element.320.prod_ref, f32[768,640]{1,0:T(8,128)} %get-tuple-element.321.state_ref, ...), custom_call_target="tpu_custom_call" | custom-call | flops 503316480 | bytes 20971520 | tf_op jit(solution)/shard_map/gates_backward/pallas_call | solution.py:686
  517.0 7.3 collective-permute-done.46
  540.4 5.5 collective-permute-start.50
  545.9 6.6 conv_backward.1
  552.6 10.5 %back_product.5 = bf16[768,2560]{1,0:T(8,128)(2,1)} custom-call(bf16[768,640]{1,0:T(8,128)(2,1)} %get-tuple-element.366.refs_0_, bf16[768,640]{1,0:T(8,128)(2,1)} %get-tuple-element.368.refs_1_, bf16[2560,1280]{1,0:T(8,128)(2,1)} %assemble.3.refs_2_.refs_3_, bf16[2560,1280]{1,0:T(8,128)(2,1)} %assemble.3.refs_2_.refs_3_), custom_call_target="tpu_custom_call" | custom-call | flops 5033164800 | bytes 6553600 | tf_op jit(solution)/shard_map/back_product/pallas_call | solution.py:889
  571.5 6.3 collective-permute-start.54
  589.2 7.1 collective-permute-done.53
  603.9 4.9 collective-permute-start.58
  613.0 11.2 %plain_grad.7 = bf16[2560,1408]{1,0:T(8,128)(2,1)} custom-call(bf16[768,2560]{1,0:T(8,128)(2,1)} %slice.341.left_ref, bf16[768,640]{1,0:T(8,128)(2,1)} %get-tuple-element.366.refs_0_, bf16[768,640]{1,0:T(8,128)(2,1)} %get-tuple-element.368.refs_1_, bf16[2560,128]{1,0:T(8,128)(2,1)} %convert_element_type.335.refs_2_), custom_call_target="tpu_custom_call" | custom-call | flops 5536481280 | bytes 13303808 | tf_op jit(solution)/shard_map/plain_grad/pallas_call | solution.py:925
  624.2 6.6 collective-permute-done.58
  630.8 8.0 %collective-permute-done.57 = bf16[192,2560]{1,0:T(8,128)(2,1)} collective-permute-done((bf16[192,2560]{1,0:T(8,128)(2,1)}, bf16[192,2560]{1,0:T(8,128)(2,1)}, u32[]{:S(2)}, u32[]{:S(2)}) %collective-permute-start.57) | collective-permute-done | bytes 983072 | tf_op jit(solution)/shard_map/ppermute | solution.py:236
  643.6 5.7 collective-permute-start.60
  650.7 5.0 collective-permute-done.63
  660.5 6.9 collective-permute-done.61
  675.6 6.0 collective-permute-start.65
  682.7 17.7 %collective-permute-done.67 = f32[8,640]{1,0:T(8,128)S(1)} collective-permute-done((f32[8,640]{1,0:T(8,128)S(1)}, f32[8,640]{1,0:T(8,128)S(1)}, u32[]{:S(2)}, u32[]{:S(2)}) %collective-permute-start.67) | collective-permute-done | bytes 20512 | tf_op jit(solution)/shard_map/ppermute | solution.py:50
  702.1 4.7 collective-permute-start.70
  713.4 4.8 select_select_fusion.7
  718.2 16.0 %collective-permute-done.69 = bf16[192,2560]{1,0:T(8,128)(2,1)} collective-permute-done((bf16[192,2560]{1,0:T(8,128)(2,1)S(1)}, bf16[192,2560]{1,0:T(8,128)(2,1)}, u32[]{:S(2)}, u32[]{:S(2)}) %collective-permute-start.69) | collective-permute-done | bytes 983072 | tf_op jit(solution)/shard_map/ppermute | solution.py:236
  743.4 6.9 collective-permute-start.75
  760.7 5.1 collective-permute-start.77
  (493 shorter events, 291.8 us)
Async XLA Ops:
  7.2 67.6 %all-gather.4.cloned.1.call-start = ((), (), s32[]{:S(2)}) async-start(), calls=%async_computation.5 | async-start | bytes 1474560 | tf_op jit(solution)/shard_map/all_gather | solution.py:1024
  18.2 31.7 %collective-permute-start.8 = (bf16[320,640]{1,0:T(8,128)(2,1)}, bf16[320,640]{1,0:T(8,128)(2,1)}, u32[]{:S(2)}, u32[]{:S(2)}) collective-permute-start(bf16[320,640]{1,0:T(8,128)(2,1)} %maximum_select_fusion.1), channel_id=1, source_target_pairs={{1,0},{2,1},{3,2},{5,4},{6,5},{7,6},{9,8},{10,9},{11,10},{13,12},{... | collective-permute-start | bytes 1228808 | tf_op jit(solution)/shard_map/ppermute | solution.py:236
  25.7 24.2 %collective-permute-start.7 = (bf16[320,640]{1,0:T(8,128)(2,1)}, bf16[320,640]{1,0:T(8,128)(2,1)}, u32[]{:S(2)}, u32[]{:S(2)}) collective-permute-start(bf16[320,640]{1,0:T(8,128)(2,1)} %maximum_select_fusion.1), channel_id=1, source_target_pairs={{0,1},{1,2},{2,3},{4,5},{5,6},{6,7},{8,9},{9,10},{10,11},{12,13},{... | collective-permute-start | bytes 1228808 | tf_op jit(solution)/shard_map/ppermute | solution.py:235
  32.9 134.5 %all-gather.6.cloned.1.call-start = ((), (), s32[]{:S(2)}) async-start(), calls=%async_computation.6 | async-start | bytes 11059200 | tf_op jit(solution)/shard_map/all_gather | solution.py:1051
  37.7 26.1 %collective-permute-start.5 = (bf16[640,640]{1,0:T(8,128)(2,1)}, bf16[640,640]{1,0:T(8,128)(2,1)}, u32[]{:S(2)}, u32[]{:S(2)}) collective-permute-start(bf16[640,640]{1,0:T(8,128)(2,1)} %pad_maximum_fusion.12), channel_id=1, source_target_pairs={{0,8},{8,0},{1,9},{9,1},{2,10},{10,2},{3,11},{11,3},{4,12},{12,4},... | collective-permute-start | bytes 2457608 | tf_op jit(solution)/shard_map/ppermute | solution.py:36
  40.9 25.1 %collective-permute-start.4 = (bf16[640,640]{1,0:T(8,128)(2,1)}, bf16[640,640]{1,0:T(8,128)(2,1)}, u32[]{:S(2)}, u32[]{:S(2)}) collective-permute-start(bf16[640,640]{1,0:T(8,128)(2,1)} %pad_maximum_fusion.11), channel_id=1, source_target_pairs={{0,16},{16,0},{1,17},{17,1},{2,18},{18,2},{3,19},{19,3},{4,20},{20... | collective-permute-start | bytes 2457608 | tf_op jit(solution)/shard_map/ppermute | solution.py:36
  66.0 216.1 %all-gather.8.cloned.1.call-start = ((), (), s32[]{:S(2)}) async-start(), calls=%async_computation.7 | async-start | bytes 22118400 | tf_op jit(solution)/shard_map/all_gather | solution.py:1084
  67.5 22.5 %collective-permute-start.10 = (bf16[1280,640]{1,0:T(8,128)(2,1)S(1)}, bf16[1280,640]{1,0:T(8,128)(2,1)}, u32[]{:S(2)}, u32[]{:S(2)}) collective-permute-start(bf16[1280,640]{1,0:T(8,128)(2,1)S(1)} %pad_maximum_fusion.7.refs_2_), channel_id=1, source_target_pairs={{0,4},{4,0},{1,5},{5,1},{2,6},{6,2},{3,7},{7,3},{8,12},{12,8},{9,1... | collective-permute-start | bytes 4915208 | tf_op jit(solution)/shard_map/ppermute | solution.py:36
  112.5 35.2 %collective-permute-start.15 = (bf16[320,1280]{1,0:T(8,128)(2,1)}, bf16[320,1280]{1,0:T(8,128)(2,1)}, u32[]{:S(2)}, u32[]{:S(2)}) collective-permute-start(bf16[320,1280]{1,0:T(8,128)(2,1)} %pad_maximum_fusion.13), channel_id=1, source_target_pairs={{0,8},{8,0},{1,9},{9,1},{2,10},{10,2},{3,11},{11,3},{4,12},{12,4},... | collective-permute-start | bytes 2457608 | tf_op jit(solution)/shard_map/ppermute | solution.py:36
  115.0 32.6 %collective-permute-start.16 = (bf16[320,1280]{1,0:T(8,128)(2,1)}, bf16[320,1280]{1,0:T(8,128)(2,1)}, u32[]{:S(2)}, u32[]{:S(2)}) collective-permute-start(bf16[320,1280]{1,0:T(8,128)(2,1)} %pad_maximum_fusion.14), channel_id=1, source_target_pairs={{0,16},{16,0},{1,17},{17,1},{2,18},{18,2},{3,19},{19,3},{4,20},{20... | collective-permute-start | bytes 2457608 | tf_op jit(solution)/shard_map/ppermute | solution.py:36
  147.6 377.9 %reduce-scatter.5.cloned.1.call-start = ((), (), s32[]{:S(2)}) async-start(), calls=%async_computation.8 | async-start | bytes 22118400 | tf_op jit(solution)/shard_map/reduce_scatter | solution.py:1124
  149.3 32.3 %collective-permute-start.20 = (bf16[320,1280]{1,0:T(8,128)(2,1)}, bf16[320,1280]{1,0:T(8,128)(2,1)}, u32[]{:S(2)}, u32[]{:S(2)}) collective-permute-start(bf16[320,1280]{1,0:T(8,128)(2,1)} %pad_maximum_fusion.13), channel_id=1, source_target_pairs={{0,16},{16,0},{1,17},{17,1},{2,18},{18,2},{3,19},{19,3},{4,20},{20... | collective-permute-start | bytes 2457608 | tf_op jit(solution)/shard_map/ppermute | solution.py:36
  151.1 32.4 %collective-permute-start.21 = (bf16[320,1280]{1,0:T(8,128)(2,1)}, bf16[320,1280]{1,0:T(8,128)(2,1)}, u32[]{:S(2)}, u32[]{:S(2)}) collective-permute-start(bf16[320,1280]{1,0:T(8,128)(2,1)} %pad_maximum_fusion.14), channel_id=1, source_target_pairs={{0,8},{8,0},{1,9},{9,1},{2,10},{10,2},{3,11},{11,3},{4,12},{12,4},... | collective-permute-start | bytes 2457608 | tf_op jit(solution)/shard_map/ppermute | solution.py:36
  153.5 29.9 %collective-permute-start.23 = (bf16[768,640]{1,0:T(8,128)(2,1)S(1)}, bf16[768,640]{1,0:T(8,128)(2,1)S(1)}, u32[]{:S(2)}, u32[]{:S(2)}) collective-permute-start(bf16[768,640]{1,0:T(8,128)(2,1)S(1)} %copy-done.46), channel_id=1, source_target_pairs={{1,0},{2,1},{3,2},{5,4},{6,5},{7,6},{9,8},{10,9},{11,10},{13,12},{... | collective-permute-start | bytes 2949128 | tf_op jit(solution)/shard_map/ppermute | solution.py:236
  154.8 28.6 %collective-permute-start.22 = (bf16[768,640]{1,0:T(8,128)(2,1)S(1)}, bf16[768,640]{1,0:T(8,128)(2,1)S(1)}, u32[]{:S(2)}, u32[]{:S(2)}) collective-permute-start(bf16[768,640]{1,0:T(8,128)(2,1)S(1)} %copy-done.46), channel_id=1, source_target_pairs={{0,1},{1,2},{2,3},{4,5},{5,6},{6,7},{8,9},{9,10},{10,11},{12,13},{... | collective-permute-start | bytes 2949128 | tf_op jit(solution)/shard_map/ppermute | solution.py:235
  183.5 32.1 %collective-permute-start.26 = (bf16[768,640]{1,0:T(8,128)(2,1)S(1)}, bf16[768,640]{1,0:T(8,128)(2,1)}, u32[]{:S(2)}, u32[]{:S(2)}) collective-permute-start(bf16[768,640]{1,0:T(8,128)(2,1)S(1)} %collective-permute-done.22), channel_id=1, source_target_pairs={{1,2},{2,3},{5,6},{6,7},{9,10},{10,11},{13,14},{14,15},{17,18},{18... | collective-permute-start | bytes 2949128 | tf_op jit(solution)/shard_map/ppermute | solution.py:235
  185.1 30.5 %collective-permute-start.27 = (bf16[768,640]{1,0:T(8,128)(2,1)S(1)}, bf16[768,640]{1,0:T(8,128)(2,1)}, u32[]{:S(2)}, u32[]{:S(2)}) collective-permute-start(bf16[768,640]{1,0:T(8,128)(2,1)S(1)} %collective-permute-done.23), channel_id=1, source_target_pairs={{1,0},{2,1},{5,4},{6,5},{9,8},{10,9},{13,12},{14,13},{17,16},{18,1... | collective-permute-start | bytes 2949128 | tf_op jit(solution)/shard_map/ppermute | solution.py:236
  186.4 27.0 %collective-permute-start.24 = (bf16[320,1280]{1,0:T(8,128)(2,1)}, bf16[320,1280]{1,0:T(8,128)(2,1)S(1)}, u32[]{:S(2)}, u32[]{:S(2)}) collective-permute-start(bf16[320,1280]{1,0:T(8,128)(2,1)} %collective-permute-done.15), channel_id=1, source_target_pairs={{0,16},{16,0},{1,17},{17,1},{2,18},{18,2},{3,19},{19,3},{4,20},{20... | collective-permute-start | bytes 2457608 | tf_op jit(solution)/shard_map/ppermute | solution.py:36
  186.5 29.1 %collective-permute-start.25 = (bf16[320,1280]{1,0:T(8,128)(2,1)}, bf16[320,1280]{1,0:T(8,128)(2,1)S(1)}, u32[]{:S(2)}, u32[]{:S(2)}) collective-permute-start(bf16[320,1280]{1,0:T(8,128)(2,1)} %collective-permute-done.16), channel_id=1, source_target_pairs={{0,8},{8,0},{1,9},{9,1},{2,10},{10,2},{3,11},{11,3},{4,12},{12,4},... | collective-permute-start | bytes 2457608 | tf_op jit(solution)/shard_map/ppermute | solution.py:36
  226.3 26.4 %collective-permute-start.31 = (bf16[768,640]{1,0:T(8,128)(2,1)}, bf16[768,640]{1,0:T(8,128)(2,1)}, u32[]{:S(2)}, u32[]{:S(2)}) collective-permute-start(bf16[768,640]{1,0:T(8,128)(2,1)} %collective-permute-done.27), channel_id=1, source_target_pairs={{1,0},{5,4},{9,8},{13,12},{17,16},{21,20},{25,24},{29,28}} | collective-permute-start | bytes 2949128 | tf_op jit(solution)/shard_map/ppermute | solution.py:236
  329.9 25.4 %collective-permute-start.32 = (bf16[192,2560]{1,0:T(8,128)(2,1)S(1)}, bf16[192,2560]{1,0:T(8,128)(2,1)S(1)}, u32[]{:S(2)}, u32[]{:S(2)}) collective-permute-start(bf16[192,2560]{1,0:T(8,128)(2,1)S(1)} %get-tuple-element.281), channel_id=1, source_target_pairs={{0,1},{4,5},{8,9},{12,13},{16,17},{20,21},{24,25},{28,29}} | collective-permute-start | bytes 2949128 | tf_op jit(solution)/shard_map/ppermute | solution.py:215
  331.2 23.1 %collective-permute-start.33 = (bf16[192,2560]{1,0:T(8,128)(2,1)}, bf16[192,2560]{1,0:T(8,128)(2,1)S(1)}, u32[]{:S(2)}, u32[]{:S(2)}) collective-permute-start(bf16[192,2560]{1,0:T(8,128)(2,1)} %get-tuple-element.282), channel_id=1, source_target_pairs={{3,2},{7,6},{11,10},{15,14},{19,18},{23,22},{27,26},{31,30}} | collective-permute-start | bytes 2949128 | tf_op jit(solution)/shard_map/ppermute | solution.py:218
  357.5 24.7 %collective-permute-start.34 = (bf16[192,2560]{1,0:T(8,128)(2,1)S(1)}, bf16[192,2560]{1,0:T(8,128)(2,1)}, u32[]{:S(2)}, u32[]{:S(2)}) collective-permute-start(bf16[192,2560]{1,0:T(8,128)(2,1)S(1)} %get-tuple-element.290), channel_id=1, source_target_pairs={{0,1},{1,2},{4,5},{5,6},{8,9},{9,10},{12,13},{13,14},{16,17},{17,1... | collective-permute-start | bytes 2949128 | tf_op jit(solution)/shard_map/ppermute | solution.py:215
  385.5 26.6 %collective-permute-start.37 = (bf16[192,2560]{1,0:T(8,128)(2,1)}, bf16[192,2560]{1,0:T(8,128)(2,1)S(1)}, u32[]{:S(2)}, u32[]{:S(2)}) collective-permute-start(bf16[192,2560]{1,0:T(8,128)(2,1)} %get-tuple-element.302), channel_id=1, source_target_pairs={{1,0},{2,1},{3,2},{5,4},{6,5},{7,6},{9,8},{10,9},{11,10},{13,12},{... | collective-permute-start | bytes 2949128 | tf_op jit(solution)/shard_map/ppermute | solution.py:218
  386.8 26.3 %collective-permute-start.36 = (bf16[192,2560]{1,0:T(8,128)(2,1)S(1)}, bf16[192,2560]{1,0:T(8,128)(2,1)S(1)}, u32[]{:S(2)}, u32[]{:S(2)}) collective-permute-start(bf16[192,2560]{1,0:T(8,128)(2,1)S(1)} %get-tuple-element.300), channel_id=1, source_target_pairs={{0,1},{1,2},{2,3},{4,5},{5,6},{6,7},{8,9},{9,10},{10,11},{12,13},{... | collective-permute-start | bytes 2949128 | tf_op jit(solution)/shard_map/ppermute | solution.py:215
  425.8 40.2 %all-to-all-start = ((bf16[192,4,640]{2,0,1:T(8,128)(2,1)}), bf16[192,4,640]{2,0,1:T(8,128)(2,1)S(1)}, u32[]{:S(2)}, u32[]{:S(2)}) async-start(bf16[192,4,640]{2,0,1:T(8,128)(2,1)} %bitcast.36), calls=%async_computation | async-start | bytes 1966080 | tf_op jit(solution)/shard_map/all_to_all | solution.py:1155
  431.0 193.2 %reduce-scatter.7.cloned.1.call-start = ((), (), s32[]{:S(2)}) async-start(), calls=%async_computation.9 | async-start | bytes 14745600 | tf_op jit(solution)/shard_map/reduce_scatter | solution.py:1124
  434.6 31.3 %collective-permute-start.38 = (bf16[192,2560]{1,0:T(8,128)(2,1)}, bf16[192,2560]{1,0:T(8,128)(2,1)S(1)}, u32[]{:S(2)}, u32[]{:S(2)}) collective-permute-start(bf16[192,2560]{1,0:T(8,128)(2,1)} %get-tuple-element.452), channel_id=1, source_target_pairs={{0,1},{4,5},{8,9},{12,13},{16,17},{20,21},{24,25},{28,29}} | collective-permute-start | bytes 2949128 | tf_op jit(solution)/shard_map/ppermute | solution.py:215
  466.9 201.8 %reduce-scatter.9.cloned.1.call-start = ((), (), s32[]{:S(2)}) async-start(), calls=%async_computation.10 | async-start | bytes 11059200 | tf_op jit(solution)/shard_map/reduce_scatter | solution.py:1124
  471.8 22.5 %collective-permute-start.43 = (bf16[192,2560]{1,0:T(8,128)(2,1)}, bf16[192,2560]{1,0:T(8,128)(2,1)}, u32[]{:S(2)}, u32[]{:S(2)}) collective-permute-start(bf16[192,2560]{1,0:T(8,128)(2,1)} %get-tuple-element.450), channel_id=1, source_target_pairs={{0,1},{1,2},{4,5},{5,6},{8,9},{9,10},{12,13},{13,14},{16,17},{17,1... | collective-permute-start | bytes 2949128 | tf_op jit(solution)/shard_map/ppermute | solution.py:215
  498.2 26.0 %collective-permute-start.46 = (bf16[192,2560]{1,0:T(8,128)(2,1)}, bf16[192,2560]{1,0:T(8,128)(2,1)S(1)}, u32[]{:S(2)}, u32[]{:S(2)}) collective-permute-start(bf16[192,2560]{1,0:T(8,128)(2,1)} %get-tuple-element.447), channel_id=1, source_target_pairs={{1,0},{2,1},{3,2},{5,4},{6,5},{7,6},{9,8},{10,9},{11,10},{13,12},{... | collective-permute-start | bytes 2949128 | tf_op jit(solution)/shard_map/ppermute | solution.py:218
  499.5 26.0 %collective-permute-start.45 = (bf16[192,2560]{1,0:T(8,128)(2,1)}, bf16[192,2560]{1,0:T(8,128)(2,1)S(1)}, u32[]{:S(2)}, u32[]{:S(2)}) collective-permute-start(bf16[192,2560]{1,0:T(8,128)(2,1)} %get-tuple-element.448), channel_id=1, source_target_pairs={{0,1},{1,2},{2,3},{4,5},{5,6},{6,7},{8,9},{9,10},{10,11},{12,13},{... | collective-permute-start | bytes 2949128 | tf_op jit(solution)/shard_map/ppermute | solution.py:215
  525.6 226.5 %reduce-scatter.11.cloned.1.call-start = ((), (), s32[]{:S(2)}) async-start(), calls=%async_computation.11 | async-start | bytes 8110080 | tf_op jit(solution)/shard_map/reduce_scatter | solution.py:1124
  539.1 28.0 %collective-permute-start.51 = (bf16[192,2560]{1,0:T(8,128)(2,1)}, bf16[192,2560]{1,0:T(8,128)(2,1)}, u32[]{:S(2)}, u32[]{:S(2)}) collective-permute-start(bf16[192,2560]{1,0:T(8,128)(2,1)} %multiply_convert_fusion.1), channel_id=1, source_target_pairs={{1,0},{2,1},{3,2},{5,4},{6,5},{7,6},{9,8},{10,9},{11,10},{13,12},{... | collective-permute-start | bytes 2949128 | tf_op jit(solution)/shard_map/ppermute | solution.py:236
  540.4 26.7 %collective-permute-start.50 = (bf16[192,2560]{1,0:T(8,128)(2,1)}, bf16[192,2560]{1,0:T(8,128)(2,1)}, u32[]{:S(2)}, u32[]{:S(2)}) collective-permute-start(bf16[192,2560]{1,0:T(8,128)(2,1)} %multiply_convert_fusion.1), channel_id=1, source_target_pairs={{0,1},{1,2},{2,3},{4,5},{5,6},{6,7},{8,9},{9,10},{10,11},{12,13},{... | collective-permute-start | bytes 2949128 | tf_op jit(solution)/shard_map/ppermute | solution.py:235
  567.1 22.0 %collective-permute-start.52 = (bf16[192,2560]{1,0:T(8,128)(2,1)}, bf16[192,2560]{1,0:T(8,128)(2,1)}, u32[]{:S(2)}, u32[]{:S(2)}) collective-permute-start(bf16[192,2560]{1,0:T(8,128)(2,1)} %collective-permute-done.50), channel_id=1, source_target_pairs={{1,2},{2,3},{5,6},{6,7},{9,10},{10,11},{13,14},{14,15},{17,18},{18... | collective-permute-start | bytes 2949128 | tf_op jit(solution)/shard_map/ppermute | solution.py:235
  568.8 27.5 %collective-permute-start.53 = (bf16[192,2560]{1,0:T(8,128)(2,1)}, bf16[192,2560]{1,0:T(8,128)(2,1)}, u32[]{:S(2)}, u32[]{:S(2)}) collective-permute-start(bf16[192,2560]{1,0:T(8,128)(2,1)} %collective-permute-done.51), channel_id=1, source_target_pairs={{1,0},{2,1},{5,4},{6,5},{9,8},{10,9},{13,12},{14,13},{17,16},{18,1... | collective-permute-start | bytes 2949128 | tf_op jit(solution)/shard_map/ppermute | solution.py:236
  571.5 28.0 %collective-permute-start.54 = (bf16[192,2560]{1,0:T(8,128)(2,1)}, bf16[192,2560]{1,0:T(8,128)(2,1)S(1)}, u32[]{:S(2)}, u32[]{:S(2)}) collective-permute-start(bf16[192,2560]{1,0:T(8,128)(2,1)} %get-tuple-element.350), channel_id=1, source_target_pairs={{0,1},{4,5},{8,9},{12,13},{16,17},{20,21},{24,25},{28,29}} | collective-permute-start | bytes 2949128 | tf_op jit(solution)/shard_map/ppermute | solution.py:215
  603.9 27.0 %collective-permute-start.58 = (bf16[192,2560]{1,0:T(8,128)(2,1)}, bf16[192,2560]{1,0:T(8,128)(2,1)S(1)}, u32[]{:S(2)}, u32[]{:S(2)}) collective-permute-start(bf16[192,2560]{1,0:T(8,128)(2,1)} %get-tuple-element.361), channel_id=1, source_target_pairs={{0,1},{1,2},{4,5},{5,6},{8,9},{9,10},{12,13},{13,14},{16,17},{17,1... | collective-permute-start | bytes 2949128 | tf_op jit(solution)/shard_map/ppermute | solution.py:215
  608.8 22.0 %collective-permute-start.56 = (bf16[192,2560]{1,0:T(8,128)(2,1)}, bf16[192,2560]{1,0:T(8,128)(2,1)S(1)}, u32[]{:S(2)}, u32[]{:S(2)}) collective-permute-start(bf16[192,2560]{1,0:T(8,128)(2,1)} %collective-permute-done.52), channel_id=1, source_target_pairs={{2,3},{6,7},{10,11},{14,15},{18,19},{22,23},{26,27},{30,31}} | collective-permute-start | bytes 2949128 | tf_op jit(solution)/shard_map/ppermute | solution.py:235
  609.5 29.3 %collective-permute-start.57 = (bf16[192,2560]{1,0:T(8,128)(2,1)}, bf16[192,2560]{1,0:T(8,128)(2,1)}, u32[]{:S(2)}, u32[]{:S(2)}) collective-permute-start(bf16[192,2560]{1,0:T(8,128)(2,1)} %collective-permute-done.53), channel_id=1, source_target_pairs={{1,0},{5,4},{9,8},{13,12},{17,16},{21,20},{25,24},{29,28}} | collective-permute-start | bytes 2949128 | tf_op jit(solution)/shard_map/ppermute | solution.py:236
  642.1 25.3 %collective-permute-start.61 = (bf16[192,2560]{1,0:T(8,128)(2,1)}, bf16[192,2560]{1,0:T(8,128)(2,1)S(1)}, u32[]{:S(2)}, u32[]{:S(2)}) collective-permute-start(bf16[192,2560]{1,0:T(8,128)(2,1)} %get-tuple-element.378), channel_id=1, source_target_pairs={{1,0},{2,1},{3,2},{5,4},{6,5},{7,6},{9,8},{10,9},{11,10},{13,12},{... | collective-permute-start | bytes 2949128 | tf_op jit(solution)/shard_map/ppermute | solution.py:218
  643.6 25.1 %collective-permute-start.60 = (bf16[192,2560]{1,0:T(8,128)(2,1)}, bf16[192,2560]{1,0:T(8,128)(2,1)}, u32[]{:S(2)}, u32[]{:S(2)}) collective-permute-start(bf16[192,2560]{1,0:T(8,128)(2,1)} %get-tuple-element.377), channel_id=1, source_target_pairs={{0,1},{1,2},{2,3},{4,5},{5,6},{6,7},{8,9},{9,10},{10,11},{12,13},{... | collective-permute-start | bytes 2949128 | tf_op jit(solution)/shard_map/ppermute | solution.py:215
  674.3 26.1 %collective-permute-start.66 = (bf16[192,2560]{1,0:T(8,128)(2,1)S(1)}, bf16[192,2560]{1,0:T(8,128)(2,1)S(1)}, u32[]{:S(2)}, u32[]{:S(2)}) collective-permute-start(bf16[192,2560]{1,0:T(8,128)(2,1)S(1)} %fusion.10), channel_id=1, source_target_pairs={{1,0},{2,1},{3,2},{5,4},{6,5},{7,6},{9,8},{10,9},{11,10},{13,12},{... | collective-permute-start | bytes 2949128 | tf_op jit(solution)/shard_map/ppermute | solution.py:236
  675.6 24.8 %collective-permute-start.65 = (bf16[192,2560]{1,0:T(8,128)(2,1)S(1)}, bf16[192,2560]{1,0:T(8,128)(2,1)}, u32[]{:S(2)}, u32[]{:S(2)}) collective-permute-start(bf16[192,2560]{1,0:T(8,128)(2,1)S(1)} %fusion.10), channel_id=1, source_target_pairs={{0,1},{1,2},{2,3},{4,5},{5,6},{6,7},{8,9},{9,10},{10,11},{12,13},{... | collective-permute-start | bytes 2949128 | tf_op jit(solution)/shard_map/ppermute | solution.py:235
  700.4 33.8 %collective-permute-start.68 = (bf16[192,2560]{1,0:T(8,128)(2,1)}, bf16[192,2560]{1,0:T(8,128)(2,1)}, u32[]{:S(2)}, u32[]{:S(2)}) collective-permute-start(bf16[192,2560]{1,0:T(8,128)(2,1)} %collective-permute-done.65), channel_id=1, source_target_pairs={{1,2},{2,3},{5,6},{6,7},{9,10},{10,11},{13,14},{14,15},{17,18},{18... | collective-permute-start | bytes 2949128 | tf_op jit(solution)/shard_map/ppermute | solution.py:235
  712.0 22.1 %collective-permute-start.69 = (bf16[192,2560]{1,0:T(8,128)(2,1)S(1)}, bf16[192,2560]{1,0:T(8,128)(2,1)}, u32[]{:S(2)}, u32[]{:S(2)}) collective-permute-start(bf16[192,2560]{1,0:T(8,128)(2,1)S(1)} %copy-done.44), channel_id=1, source_target_pairs={{1,0},{2,1},{5,4},{6,5},{9,8},{10,9},{13,12},{14,13},{17,16},{18,1... | collective-permute-start | bytes 2949128 | tf_op jit(solution)/shard_map/ppermute | solution.py:236
  734.2 21.4 %collective-permute-start.74 = (bf16[192,2560]{1,0:T(8,128)(2,1)}, bf16[192,2560]{1,0:T(8,128)(2,1)}, u32[]{:S(2)}, u32[]{:S(2)}) collective-permute-start(bf16[192,2560]{1,0:T(8,128)(2,1)} %collective-permute-done.69), channel_id=1, source_target_pairs={{1,0},{5,4},{9,8},{13,12},{17,16},{21,20},{25,24},{29,28}} | collective-permute-start | bytes 2949128 | tf_op jit(solution)/shard_map/ppermute | solution.py:236
  (118 other events, 1314.8 us)
Sparse Core Ops, SparseCore 0:
  33.0 31.3 all-gather.3
  66.3 72.1 all-gather.5
  147.8 124.3 all-gather.7
  357.6 128.2 reduce-scatter.4
  489.4 95.3 reduce-scatter.6
  588.2 79.1 reduce-scatter.8
  670.9 65.2 reduce-scatter.10
